TPU v7x, 256 devices: a whole 4x4x8 slice. The times are simulated.
256 devices in a mesh: col: 32 (over z, y), row: 8 (over x, core).
Axes of the slice: x: 4, y: 4, z: 8, core: 2. Of those that a mesh axis runs over, the one named last changes fastest.
Arguments:
- slab: float32 [48, 8, 128, 2, 32, 128], P(None, 'row', None, None, 'col'), may hold values from 0 to 1.4, as said below
Outputs:
- updated: float32 [48, 8, 128, 2, 32, 128], P(None, 'row', None, None, 'col')
Inputs may be any that keep to these rules, and one draw needn't show every extreme that they name: `slab`: entry [g, h] is exp(-sum over the 256 features of a positive rate times the squared difference of the two designs' features), plus a noise variance of 0.1 to 0.4 where g equals h; the leading 8192 x 8192 part is symmetric positive definite.
All inputs are finite; a program needn't handle non-finite values.
Results may differ from a plain program's by a relative error of at most 0.0003.
Values sent between devices are 32-bit elements; how exact they have to be, the bound alone decides.
No kernel may reach another device: no remote copies, remote signals or barrier semaphores. Data moves between devices by JAX's collectives and lax.ppermute only.
A program may use at most 128 MiB of HBM per device.

v0:
```python
import jax
import jax.numpy as jnp
from jax import lax
from jax.sharding import PartitionSpec as P


def from_root(value, axis, source):
    kept = jnp.where(lax.axis_index(axis) == source, value, 0).astype(value.dtype)
    return lax.psum(kept, axis)


def body(slab):
    blocks_rows, width, blocks_cols = (slab.shape[0], slab.shape[2], slab.shape[3])
    row_count = lax.axis_size("row")
    col_count = lax.axis_size("col")
    row_index = lax.axis_index("row")
    col_index = lax.axis_index("col")
    local = slab.reshape(blocks_rows * width, blocks_cols * width)
    offsets = jnp.arange(blocks_rows * width)
    global_rows = (offsets // width * row_count + row_index) * width + offsets % width
    for step in range(2):
        owner_col = step % col_count
        col_block = step // col_count
        raw = local[
            step // row_count * width : (step // row_count + 1) * width,
            col_block * width : (col_block + 1) * width,
        ]
        block = from_root(raw, "row", step % row_count)
        block = jnp.where(col_index == owner_col, block, jnp.eye(width, dtype=jnp.float32))
        factor = jnp.linalg.cholesky(block)
        solved = lax.linalg.triangular_solve(
            factor,
            local[:, col_block * width : (col_block + 1) * width],
            left_side=False,
            lower=True,
            transpose_a=True,
        )
        below = (global_rows >= (step + 1) * width)[:, None]
        lowpart = jnp.where(below, solved, 0.0)
        inside = (global_rows // width == step)[:, None]
        panel = jnp.where(below, solved, jnp.where(inside, jnp.tile(factor, (blocks_rows, 1)), 0.0))
        lowpart, panel = (lowpart, panel)
        lowpart = from_root(lowpart, "col", step % col_count)
        count = blocks_cols * col_count // row_count
        head = lowpart[: count * width].reshape(count, 1, width, width)
        full = lax.all_gather(head, "row", axis=1, tiled=True).reshape(
            count * row_count * width, width
        )
        pieces = [
            lax.dynamic_slice_in_dim(full, (number * col_count + col_index) * width, width, 0)
            for number in range(blocks_cols)
        ]
        place_matrix = local - jnp.dot(
            lowpart,
            jnp.concatenate(pieces, 0).T,
            precision=lax.Precision.HIGHEST,
            preferred_element_type=jnp.float32,
        )
        place_col_block = step // col_count
        current = place_matrix[:, place_col_block * width : (place_col_block + 1) * width]
        chosen = jnp.where(col_index == step % col_count, panel, current)
        local = place_matrix.at[:, place_col_block * width : (place_col_block + 1) * width].set(
            chosen
        )
    return local.reshape(slab.shape)


def solution(mesh):
    placed = (P(None, "row", None, None, "col", None),)
    return jax.shard_map(
        body,
        mesh=mesh,
        in_specs=placed,
        out_specs=P(None, "row", None, None, "col", None),
        check_vma=False,
    )
```

profile of v0, /device:TPU:24, one launch (start us, length us, event | category | flops | bytes accessed | tf_op | source)
XLA Modules:
  0.0 648.2 jit_solution(11449827182267803855)
XLA Ops:
  6.5 5.9 copy.33
  12.4 6.6 %copy.22 = f32[6144,256]{0,1:T(8,128)} copy(f32[6144,256]{1,0:T(8,128)} %bitcast.66) | data formatting | bytes 12582912 | tf_op jit(solution)/shard_map/reshape | solution.py:18
  19.0 1.5 slice_select_fusion.1
  20.6 66.5 %all-reduce.5.cloned.1.call-done = f32[128,128]{0,1:T(8,128)} async-done(((f32[128,128]{0,1:T(8,128)}), f32[128,128]{0,1:T(8,128)}) %all-reduce.5.cloned.1.call-update) | async-done | bytes 65552 | tf_op jit(solution)/shard_map/psum | solution.py:9
  87.3 11.7 %cholesky.44 = f32[128,128]{1,0:T(8,128)S(1)} custom-call(f32[128,128]{1,0:T(8,128)S(1)} %fusion.13), custom_call_target="Cholesky" | custom-call | tf_op jit(solution)/shard_map/jit(cholesky)/cholesky | solution.py:30
  99.0 0.6 compare_reduce_fusion.1
  99.7 0.7 select_bitcast_fusion.1
  100.3 9.8 %custom-call.6 = f32[1,128,128]{1,2,0:T(8,128)S(1)} custom-call(f32[1,128,128]{2,1,0:T(8,128)S(1)} %get-tuple-element.35), custom_call_target="InvertDiagBlocksLowerTriangular" | custom-call | tf_op jit(solution)/shard_map/triangular_solve/custom-call.0 | solution.py:31
  110.1 7.6 %select_select_fusion.3 = (f32[6144,128]{0,1:T(8,128)}, f32[6144,128]{0,1:T(8,128)}) fusion(pred[6144]{0:T(1024)(128)(4,1)S(1)} %broadcast_compare_fusion.1, pred[]{:T(512)S(6)} %eq.40, f32[6144,256]{0,1:T(8,128)} %copy.22, f32[1,128,128]{1,2,0:T(8,128)S(1)} %custom-call.6), kind=kOutput, calls=%fused_computation.14 | convolution fusion | flops 1209532416 | bytes 9508865 | tf_op jit(solution)/shard_map/triangular_solve/dot.3 | solution.py:31
  117.8 155.6 %all-reduce.7.cloned.1.call-done = f32[6144,128]{0,1:T(8,128)} async-done(((f32[6144,128]{0,1:T(8,128)}), f32[6144,128]{0,1:T(8,128)}) %all-reduce.7.cloned.1.call-update) | async-done | bytes 3145744 | tf_op jit(solution)/shard_map/psum | solution.py:9
  273.4 1.1 slice.75
  274.5 1.0 copy.23
  275.7 0.7 compare_reduce_fusion.2
  276.6 32.5 %all-gather.3.cloned.1.call-done = f32[8,8,128,128]{3,2,1,0:T(8,128)} async-done(((f32[8,1,128,128]{3,2,1,0:T(8,128)}), f32[8,8,128,128]{3,2,1,0:T(8,128)}) %all-gather.3.cloned.1.call-update) | async-done | bytes 4194320 | tf_op jit(solution)/shard_map/all_gather | solution.py:46
  309.0 0.9 constant_dynamic-slice_fusion.3
  309.9 10.4 %convolution_subtract_fusion.1 = f32[6144,256]{0,1:T(8,128)} fusion(f32[6144,256]{0,1:T(8,128)} %copy.22, f32[6144,128]{0,1:T(8,128)} %all-reduce.7.cloned.1.call-done, f32[128,128]{1,0:T(8,128)S(1)} %get-tuple-element.40, f32[128,128]{1,0:T(8,128)S(1)} %get-tuple-element.39), kind=kOutput, calls=%fused_computation.1 | convolution fusion | flops 2417524736 | bytes 15859712 | tf_op jit(solution)/shard_map/dot_general | solution.py:53
  320.6 1.7 copy-done
  322.2 6.2 constant_dynamic-update-slice_fusion
  329.2 63.9 %all-reduce.9.cloned.1.call-done = f32[128,128]{0,1:T(8,128)} async-done(((f32[128,128]{0,1:T(8,128)}), f32[128,128]{0,1:T(8,128)}) %all-reduce.9.cloned.1.call-update) | async-done | bytes 65552 | tf_op jit(solution)/shard_map/psum | solution.py:9
  393.2 11.7 %cholesky.55 = f32[128,128]{1,0:T(8,128)S(1)} custom-call(f32[128,128]{1,0:T(8,128)S(1)} %fusion.11), custom_call_target="Cholesky" | custom-call | tf_op jit(solution)/shard_map/jit(cholesky)/cholesky | solution.py:30
  406.2 9.8 %custom-call.7 = f32[1,128,128]{1,2,0:T(8,128)S(1)} custom-call(f32[1,128,128]{2,1,0:T(8,128)S(1)} %get-tuple-element.31), custom_call_target="InvertDiagBlocksLowerTriangular" | custom-call | tf_op jit(solution)/shard_map/triangular_solve/custom-call.0 | solution.py:31
  416.0 4.7 select_select_fusion.2
  421.0 155.3 %all-reduce.11.cloned.1.call-done = f32[6144,128]{0,1:T(8,128)} async-done(((f32[6144,128]{0,1:T(8,128)}), f32[6144,128]{0,1:T(8,128)}) %all-reduce.11.cloned.1.call-update) | async-done | bytes 3145744 | tf_op jit(solution)/shard_map/psum | solution.py:9
  576.3 1.1 slice.78
  577.4 1.0 copy.24
  578.6 33.4 %all-gather.5.cloned.1.call-done = f32[8,8,128,128]{3,2,1,0:T(8,128)} async-done(((f32[8,1,128,128]{3,2,1,0:T(8,128)}), f32[8,8,128,128]{3,2,1,0:T(8,128)}) %all-gather.5.cloned.1.call-update) | async-done | bytes 4194320 | tf_op jit(solution)/shard_map/all_gather | solution.py:46
  612.0 0.9 constant_dynamic-slice_fusion.1
  612.9 9.2 %convolution_subtract_fusion = f32[6144,256]{0,1:T(8,128)S(1)} fusion(f32[6144,256]{0,1:T(8,128)} %get-tuple-element.33, f32[6144,128]{0,1:T(8,128)} %all-reduce.11.cloned.1.call-done, f32[128,128]{1,0:T(8,128)S(1)} %get-tuple-element.38, f32[128,128]{1,0:T(8,128)S(1)} %get-tuple-element.37), kind=kOutput, calls=%fused_computation | convolution fusion | flops 2417524736 | bytes 15859712 | tf_op jit(solution)/shard_map/dot_general | solution.py:53
  622.3 1.7 copy-done.1
  624.0 3.4 fusion
  627.4 3.8 copy.28
  631.2 10.2 %copy.19 = f32[48,1,128,2,1,128]{5,4,3,2,1,0:T(1,128)} copy(f32[48,1,128,2,1,128]{2,0,5,3,4,1:T(8,128)} %bitcast.65) | data formatting | bytes 12582912 | tf_op jit(solution)/shard_map/reshape | solution.py:65
  (33 shorter events, 3.6 us)
Async XLA Ops:
  6.5 80.6 %all-reduce.5.cloned.1.call-start = ((), (), s32[]{:S(2)}) async-start(), calls=%async_computation | async-start | bytes 131072 | tf_op jit(solution)/shard_map/psum | solution.py:9
  20.5 252.8 %all-reduce.7.cloned.1.call-start = ((), (), s32[]{:S(2)}) async-start(), calls=%async_computation.1 | async-start | bytes 6291456 | tf_op jit(solution)/shard_map/psum | solution.py:9
  117.7 191.3 %all-gather.3.cloned.1.call-start = ((), (), s32[]{:S(2)}) async-start(), calls=%async_computation.2 | async-start | bytes 4718592 | tf_op jit(solution)/shard_map/all_gather | solution.py:46
  275.5 117.6 %all-reduce.9.cloned.1.call-start = ((), (), s32[]{:S(2)}) async-start(), calls=%async_computation.3 | async-start | bytes 131072 | tf_op jit(solution)/shard_map/psum | solution.py:9
  320.3 1.9 copy-start
  329.1 247.2 %all-reduce.11.cloned.1.call-start = ((), (), s32[]{:S(2)}) async-start(), calls=%async_computation.4 | async-start | bytes 6291456 | tf_op jit(solution)/shard_map/psum | solution.py:9
  420.8 191.2 %all-gather.5.cloned.1.call-start = ((), (), s32[]{:S(2)}) async-start(), calls=%async_computation.5 | async-start | bytes 4718592 | tf_op jit(solution)/shard_map/all_gather | solution.py:46
  622.1 1.9 copy-start.1
Sparse Core Ops, SparseCore 0:
  20.6 66.4 all-reduce.4
  117.9 155.4 all-reduce.6
  275.6 33.3 all-gather.2
  329.2 63.8 all-reduce.8
  420.9 155.3 all-reduce.10
  578.6 33.3 all-gather.4
where the time goes:
time: 651 us; the launch traced here: 648 us
  waiting for transfers between devices  507 us (78%)
  other arithmetic  58.2 us (9%)
  local copies, waits for them, and re-layouts  36.5 us (6%)
  matrix products  31.9 us (5%)
  between operations  13.7 us (2%)
    psum x4, waiting for transfers between devices, from_root(): return lax.psum(kept, axis)  441 us
    all_gather x2, waiting for transfers between devices, body(): lax.all_gather(head, 'row', axis=1, tiled=True)  65.9 us
    another operation x6, other arithmetic, body(): factor = jnp.linalg.cholesky(block)  24.8 us
    another operation x4, other arithmetic, body(): lax.linalg.triangular_solve(factor, local[:, col_block * width:(col_block...  20.8 us
    dot_general x2, matrix products, body(): jnp.dot(lowpart, jnp.concatenate(pieces, 0).T, precision=lax.Precision.HI...  19.6 us
  transfers between devices with their start and end apart: 6, of which 6 were waited for; matrix products, arithmetic and copies ran while one was open for 0% of the time, Pallas kernels for 0%

commit v1 on v0

v1 whole, which is shorter than its diff:
```python
import functools

import jax
import jax.numpy as jnp
import numpy as np
from jax import lax
from jax.experimental import pallas as pl
from jax.experimental.pallas import tpu as pltpu
from jax.sharding import PartitionSpec as P

F32 = jnp.float32
BF16 = jnp.bfloat16
NZ, NY = 8, 4
ROOTS = (0, 1)
SUBROOTS = ((0, 1), (0, 3), (3, 0), (5, 0))
QUARTERS = [(0, 1), (2, 1), (2, 2), (3, 1), (0, 3), (1, 3), (2, 0), (3, 3), (0, 0), (1, 0), (1, 1), (3, 0), (0, 2), (1, 2), (2, 3), (3, 2)]
DELIVER = [
    [(0, 4, 1, 1), (1, 9, 1, 0), (2, 11, 2, 1), (3, 15, 3, 0), (12, 18, 0, 0), (13, 31, 3, 1), (20, 25, 2, 0), (21, 17, 0, 1)],
    [(0, 18, 0, 1), (1, 13, 3, 0), (2, 10, 1, 1), (3, 26, 2, 0), (12, 5, 2, 0), (13, 6, 2, 1), (20, 28, 3, 0), (21, 8, 2, 1)],
    [(0, 9, 2, 1), (1, 31, 3, 0), (2, 24, 1, 1), (3, 29, 3, 0), (12, 4, 1, 0), (13, 23, 1, 1), (20, 14, 3, 0), (21, 7, 1, 1)],
    [(0, 22, 1, 1), (1, 19, 0, 0), (2, 16, 0, 1), (3, 17, 0, 0), (12, 23, 2, 0), (13, 5, 1, 1), (20, 2, 0, 0), (21, 29, 3, 1)],
    [(0, 12, 3, 1), (1, 27, 1, 0), (2, 25, 2, 1), (3, 7, 1, 0), (12, 22, 1, 0), (13, 20, 2, 1), (20, 6, 1, 0), (21, 3, 0, 1)],
    [(0, 30, 3, 1), (1, 24, 2, 0), (2, 28, 3, 1), (3, 8, 2, 0), (13, 19, 0, 1), (20, 11, 2, 0), (21, 15, 3, 1)],
    [(0, 27, 2, 1), (1, 10, 2, 0), (2, 14, 3, 1), (3, 21, 1, 0), (12, 30, 3, 0), (20, 16, 0, 0), (21, 26, 2, 1)],
]
GATHER = (
    ((1, 0), (0, 0), 0), ((-1, 0), (0, 0), 0), ((0, 1), (0, 0), 0), ((0, -1), (0, 0), 0),
    ((1, 0), (1, 0), 0), ((-1, 0), (-1, 0), 0), ((0, 1), (1, 0), 0), ((0, -1), (1, 0), 0),
    ((0, 1), (-1, 0), 0), ((0, -1), (-1, 0), 0), ((1, 0), (2, 0), 0), ((-1, 0), (-2, 0), 0),
    ((0, 1), (0, 1), 1), ((0, -1), (0, -1), 2), ((1, 0), (1, 1), 0), ((-1, 0), (-1, 1), 0),
)


def at(z, y):
    return (z % NZ) * NY + y % NY


def place(chip):
    return chip // NY, chip % NY


CLASSES = []
for _z in range(NZ):
    for _y in range(NY):
        if not any((_z, _y) in _c for _c in CLASSES):
            CLASSES.append(((_z, _y), ((_z + 4) % NZ, (_y + 2) % NY)))
CLASS_OF = {at(*_m): _i for _i, _c in enumerate(CLASSES) for _m in _c}
PIECES = len(CLASSES)
CHIPS = NZ * NY


def tables():
    order = np.zeros((CHIPS, PIECES), np.int32)
    for chip in range(CHIPS):
        shift = 1 if chip == ROOTS[1] else 0
        order[chip] = [CLASS_OF[at(z, y + shift)] for z, y in QUARTERS]
    origin = np.zeros((2, CHIPS), np.int32)
    index = np.zeros((len(DELIVER), CHIPS), np.int32)
    for step, sends in enumerate(DELIVER):
        for source, target, slot, panel in sends:
            origin[panel, target] = step
            index[step, source] = slot
    held = np.zeros(CHIPS, np.int32)
    for quarter, (z, y) in enumerate(SUBROOTS):
        first = [CLASS_OF[at(*m)] for m in QUARTERS[4 * quarter : 4 * quarter + 4]]
        for panel in (0, 1):
            chip = at(z, y + panel)
            held[chip] = first.index(CLASS_OF[at(z, y)])
            origin[panel, chip] = len(DELIVER)
    for panel in (0, 1):
        origin[panel, ROOTS[panel]] = len(DELIVER) + 1
    mine = [CLASS_OF[at(*m)] for m in QUARTERS].index(CLASS_OF[at(0, 0)])
    return order, origin, index, held, mine


ORDER, ORIGIN, INDEX, HELD, MINE = tables()


def extract_kernel(rows, order_ref, x_ref, o_ref):
    o_ref[0] = x_ref[pl.ds(0, rows, stride=2), :]


def extract(x, order, rows):
    return pl.pallas_call(
        functools.partial(extract_kernel, rows),
        grid_spec=pltpu.PrefetchScalarGridSpec(
            num_scalar_prefetch=1,
            grid=(PIECES,),
            in_specs=[pl.BlockSpec((2 * rows, 128), lambda i, order: (order[i], 0))],
            out_specs=pl.BlockSpec((1, rows, 128), lambda i, order: (i, 0, 0)),
        ),
        out_shape=jax.ShapeDtypeStruct((PIECES, rows, 128), F32),
    )(order, x)


class Sender:
    def __init__(self, depth):
        self.depth = depth
        self.sent = []

    def __call__(self, value, pairs):
        if len(self.sent) >= self.depth:
            oldest = self.sent[-self.depth]
            value, oldest[0] = lax.optimization_barrier((value, oldest[0]))
        result = [lax.ppermute(value, "col", pairs)]
        self.sent.append(result)
        return result


def spread(own, chip):
    send = Sender(5)
    quarters = [
        send(own[4 * k : 4 * k + 4], [(at(0, p), at(z, y + p)) for p in (0, 1)])
        for k, (z, y) in enumerate(SUBROOTS)
    ]
    quarter = sum(q[0] for q in quarters)
    index = jnp.asarray(INDEX)[:, chip]
    arrived = [
        send(
            lax.dynamic_index_in_dim(quarter, index[step], 0, keepdims=False),
            [(source, target) for source, target, _, _ in sends],
        )
        for step, sends in enumerate(DELIVER)
    ]
    held = lax.dynamic_index_in_dim(quarter, jnp.asarray(HELD)[chip], 0, keepdims=False)
    choices = [a[0] for a in arrived] + [held, own[MINE]]

    def pick(panel):
        origin = jnp.asarray(ORIGIN)[panel, chip]
        value = choices[0]
        for k in range(1, len(choices)):
            value = jnp.where(origin == k, choices[k], value)
        return value

    pieces = {(0, 0): [jnp.stack([pick(0), pick(1)])]}
    for (fz, fy), (ez, ey), half in GATHER:
        value = pieces[(ez, ey)][0]
        middle = value.shape[1] // 2
        value = {0: value, 1: value[:, :middle], 2: value[:, middle:]}[half]
        pairs = [(at(z + fz, y + fy), at(z, y)) for z in range(NZ) for y in range(NY)]
        key = (fz + ez, fy + ey) if half == 0 else (0, 2, half)
        pieces[key] = send(value, pairs)
    return {key: value[0] for key, value in pieces.items()}


def corner(head, chip):
    z, y = chip // NY, chip % NY
    move = lambda value, pairs: lax.ppermute(value, "col", pairs)
    up = move(head, [(0, 1), (1, 2)])
    down = move(head, [(0, 3), (1, 0)])
    across = move(head, [(0, 2), (1, 3)])
    first = jnp.where(y == 0, head, jnp.where(y == 1, up, jnp.where(y == 2, across, down)))
    second = jnp.where(y == 1, head, jnp.where(y == 2, up, jnp.where(y == 3, across, down)))
    line = jnp.concatenate([first, second], axis=1)
    far = move(line, [(at(0, j), at(3, j)) for j in range(NY)])
    back = move(line, [(at(0, j), at(5, j)) for j in range(NY)])
    base = jnp.where(z == 0, line, jnp.where(z == 3, far, back))
    above = move(base, [(at(k, j), at(k + 1, j)) for k in (0, 3, 5) for j in range(NY)])
    below = move(base, [(at(k, j), at(k - 1, j)) for k in (0, 3) for j in range(NY)])
    near = (z == 0) | (z == 3) | (z == 5)
    return jnp.where(near, base, jnp.where((z == 1) | (z == 4) | (z == 6), above, below))


def dot(a, b, dims):
    return lax.dot_general(
        a, b, ((dims[:1], dims[1:]), ((), ())), precision=lax.Precision.HIGHEST, preferred_element_type=F32
    )


def eliminate(block):
    n = block.shape[0]
    block = 0.5 * (block + block.T)
    row_id = lax.broadcasted_iota(jnp.int32, (8, n), 0)
    lane_id = lax.broadcasted_iota(jnp.int32, (8, n), 1)
    left = [block[8 * k : 8 * k + 8] for k in range(n // 8)]
    right = [jnp.where(lane_id == row_id + 8 * k, 1.0, 0.0).astype(F32) for k in range(n // 8)]
    for j in range(n):
        k0, r = j // 8, j % 8
        pivot = jnp.broadcast_to(left[k0][r : r + 1, j : j + 1], (8, n))
        scale = lax.rsqrt(pivot)
        scale = scale * (1.5 - 0.5 * pivot * scale * scale)
        lrow = jnp.broadcast_to(left[k0][r : r + 1, :], (8, n)) * scale
        rrow = jnp.broadcast_to(right[k0][r : r + 1, :], (8, n)) * scale
        for k in range(k0, n // 8):
            factor = jnp.broadcast_to(left[k][:, j : j + 1], (8, n)) * scale
            if k == k0:
                below = row_id > r
                left[k] = jnp.where(below, left[k] - factor * lrow, jnp.where(row_id == r, lrow, left[k]))
                right[k] = jnp.where(below, right[k] - factor * rrow, jnp.where(row_id == r, rrow, right[k]))
            else:
                left[k] = left[k] - factor * lrow
                right[k] = right[k] - factor * rrow
    upper = jnp.concatenate(left, axis=0)
    rows = lax.broadcasted_iota(jnp.int32, (n, n), 0)
    lanes = lax.broadcasted_iota(jnp.int32, (n, n), 1)
    return jnp.where(lanes >= rows, upper, 0.0), jnp.concatenate(right, axis=0)


def first_kernel(a_ref, d_ref, w_ref):
    upper, inverse = eliminate(a_ref[...])
    d_ref[...] = upper.T
    w_ref[...] = inverse


def second_kernel(a10_ref, a11_ref, w0_ref, l_ref, d_ref, w_ref):
    low = dot(a10_ref[...], w0_ref[...], (1, 1))
    l_ref[...] = low
    upper, inverse = eliminate(a11_ref[...] - dot(low, low, (1, 1)))
    d_ref[...] = upper.T
    w_ref[...] = inverse


def third_kernel(place_ref, head_ref, d0_ref, w0_ref, l_ref, d1_ref, w1_ref, m_ref, s_ref):
    row, col = place_ref[0], place_ref[1]
    w0, w1, low = w0_ref[...], w1_ref[...], l_ref[...]
    head0, head1 = head_ref[:128], head_ref[128:]
    g0 = dot(w0, head0, (1, 0))
    rest = head1 - dot(low, g0, (1, 0))
    g1 = dot(w1, rest, (1, 0))
    m1 = dot(w1, g1, (0, 0))
    m0 = dot(w0, g0 - dot(low, m1, (0, 0)), (0, 0))
    mixed = dot(w0, dot(low, w1, (0, 1)), (0, 0))
    zero = jnp.zeros((128, 128), F32)
    root0, root1 = col == ROOTS[0], col == ROOTS[1]
    m_ref[:128, 128:] = m0[:, 128:]
    m_ref[128:, 128:] = m1[:, 128:]
    m_ref[:128, :128] = jnp.where(root0, -w0.T, jnp.where(root1, mixed, m0[:, :128]))
    m_ref[128:, :128] = jnp.where(root0, zero, jnp.where(root1, -w1.T, m1[:, :128]))
    top = row == 0
    s_ref[:, 128:] = jnp.where(top, head0[:, 128:], rest[:, 128:])
    normal = jnp.where(top, head0[:, :128], rest[:, :128])
    on0 = jnp.where(top, d0_ref[...], low)
    on1 = jnp.where(top, zero, d1_ref[...])
    s_ref[:, :128] = jnp.where(root0, on0, jnp.where(root1, on1, normal))


def vmem(count):
    return [pl.BlockSpec(memory_space=pltpu.VMEM)] * count


def factor_all(corner_block, head, row, col):
    square = jax.ShapeDtypeStruct((128, 128), F32)
    d0, w0 = pl.pallas_call(
        first_kernel, out_shape=(square, square), in_specs=vmem(1), out_specs=tuple(vmem(2))
    )(corner_block[:128, :128])
    low, d1, w1 = pl.pallas_call(
        second_kernel, out_shape=(square,) * 3, in_specs=vmem(3), out_specs=tuple(vmem(3))
    )(corner_block[128:, :128], corner_block[128:, 128:], w0)
    return pl.pallas_call(
        third_kernel,
        out_shape=(jax.ShapeDtypeStruct((256, 256), F32), jax.ShapeDtypeStruct((128, 256), F32)),
        in_specs=[pl.BlockSpec(memory_space=pltpu.SMEM)] + vmem(6),
        out_specs=tuple(vmem(2)),
    )(jnp.stack([row, col]).astype(jnp.int32), head, d0, w0, low, d1, w1)


def update_kernel(names, rows, chunk_ref, place_ref, x_ref, m_ref, s_ref, *refs):
    pieces, o_ref, wide = refs[: sum(len(n) for n in names)], refs[-2], refs[-1]
    step = pl.program_id(0)
    k = 0
    for i, parts in enumerate(names):
        mine = pieces[k : k + len(parts)]
        k += len(parts)

        @pl.when(step == i)
        def _():
            start = 0
            for ref in mine:
                size = ref.shape[1]
                wide[start : start + size, :128] = ref[0]
                wide[start : start + size, 128:] = ref[1]
                start += size

    value = wide[...]
    high = value.astype(BF16)
    rest = (value - high.astype(F32)).astype(BF16)
    m = m_ref[...]
    m_high = m.astype(BF16)
    m_rest = (m - m_high.astype(F32)).astype(BF16)
    mul = functools.partial(jnp.dot, preferred_element_type=F32)
    product = mul(high, m_high) + (mul(rest, m_high) + mul(high, m_rest))
    root = place_ref[1] < 2
    left = x_ref[pl.ds(0, rows, stride=2), :]
    o_ref[pl.ds(0, rows, stride=2), :] = jnp.where(root, 0.0, left) - product[:, :128]
    o_ref[pl.ds(1, rows, stride=2), :] = x_ref[pl.ds(1, rows, stride=2), :] - product[:, 128:]

    @pl.when((chunk_ref[step] == 0) & (place_ref[0] < 2))
    def _():
        o_ref[pl.ds(0, 128, stride=2), :] = s_ref[:, :128]
        o_ref[pl.ds(1, 128, stride=2), :] = s_ref[:, 128:]


def update(x, m, special, pieces, chunks, row, col, names, rows):
    block = pl.BlockSpec((2 * rows, 128), lambda i, chunk, place: (chunk[i], 0))
    flat = [pieces[key] for parts in names for key in parts]
    return pl.pallas_call(
        functools.partial(update_kernel, names, rows),
        grid_spec=pltpu.PrefetchScalarGridSpec(
            num_scalar_prefetch=2,
            grid=(len(names),),
            in_specs=[block] + vmem(2 + len(flat)),
            out_specs=block,
            scratch_shapes=[pltpu.VMEM((rows, 256), F32)],
        ),
        out_shape=jax.ShapeDtypeStruct(x.shape, F32),
        compiler_params=pltpu.CompilerParams(vmem_limit_bytes=40 * 1024 * 1024),
    )(chunks, jnp.stack([row, col]).astype(jnp.int32), x, m, special, *flat)


def body(slab):
    row, col = lax.axis_index("row"), lax.axis_index("col")
    x = slab.reshape(slab.shape[0] * 128 * 2, 128)
    rows = x.shape[0] // (2 * PIECES)
    own = extract(x, jnp.asarray(ORDER)[col], rows)
    heads = lax.all_gather(x[:256].reshape(128, 256), "row", axis=0)
    head = heads[:2].reshape(256, 256)
    pieces = spread(own, col)
    whole = corner(head[:, :128], col)
    m, special = factor_all(whole, head, row, col)
    names = [((0, 0),)] + [(key,) for key in pieces if key != (0, 0) and len(key) == 2]
    names.append(((0, 2, 1), (0, 2, 2)))
    where = np.zeros((CHIPS, len(names)), np.int32)
    for chip in range(CHIPS):
        z, y = place(chip)
        where[chip] = [CLASS_OF[at(z + n[0][0], y + n[0][1])] for n in names]
    chunks = jnp.asarray(where)[col]
    out = update(x, m, special, pieces, chunks, row, col, names, rows)
    return out.reshape(slab.shape)


def solution(mesh):
    spec = P(None, "row", None, None, "col", None)
    return jax.shard_map(body, mesh=mesh, in_specs=(spec,), out_specs=spec, check_vma=False)
```

time: 651 us -> 218 us (0.33)
  waiting for transfers between devices: 507 us -> 17.9 us
  starting transfers between devices: 0.61 us -> 69 us
  Pallas kernels: 0 us -> 66.6 us
  other arithmetic: 58.2 us -> 8.32 us
  matrix products: 31.9 us -> 0 us
  between operations: 13.7 us -> 38.6 us
  local copies, waits for them, and re-layouts: 36.5 us -> 16.4 us
    psum x4 -> x0, waiting for transfers between devices: 441 us -> none  [from_root(): return lax.psum(kept, axis)]
    ppermute x0 -> x34, starting transfers between devices: none -> 69 us  [the longest x27 54.7 us: __call__(): result = [lax.ppermute(value, 'col', pairs)]]
    pallas_call x0 -> x5, Pallas kernels: none -> 66.6 us  [the longest x1 20.4 us: factor_all(): pl.pallas_call(second_kernel, out_shape=(square,) * 3, in_specs=vmem(3),...]
    all_gather x2 -> x1, waiting for transfers between devices: 65.9 us -> 0.01 us  [body(): heads = lax.all_gather(x[:256].reshape(128, 256), 'row', axis=0)]
    another operation x11 -> x4, other arithmetic: 46.3 us -> 2.66 us  [the longest x3 2.06 us: spread(): pieces = {(0, 0): [jnp.stack([pick(0), pick(1)])]}]
    dot_general x2 -> x0, matrix products: 19.6 us -> none  [body(): jnp.dot(lowpart, jnp.concatenate(pieces, 0).T, precision=lax.Precision.HI...]
    reshape x4 -> x0, local copies, waits for them, and re-layouts: 18.8 us -> none  [the longest x1 10.2 us: body(): return local.reshape(slab.shape)]
    ppermute x0 -> x34, waiting for transfers between devices: none -> 17.9 us  [the longest x27 14.1 us: __call__(): result = [lax.ppermute(value, 'col', pairs)]]
  transfers between devices with their start and end apart: 6 -> 35, of which waited for: 6 -> 8; matrix products, arithmetic and copies ran while one was open for 0% -> 7% of each run, Pallas kernels for 0% -> 20%
where the time goes in v1:
time: 218 us; the launch traced here: 217 us
  starting transfers between devices  69 us (32%)
  Pallas kernels  66.6 us (31%)
  between operations  38.6 us (18%)
  waiting for transfers between devices  17.9 us (8%)
  local copies, waits for them, and re-layouts  16.4 us (8%)
  other arithmetic  8.32 us (4%)
    ppermute x27, starting transfers between devices, __call__(): result = [lax.ppermute(value, 'col', pairs)]  54.7 us
    pallas_call x1, Pallas kernels, factor_all(): pl.pallas_call(second_kernel, out_shape=(square,) * 3, in_specs=vmem(3),...  20.4 us
    pallas_call x1, Pallas kernels, factor_all(): pl.pallas_call(first_kernel, out_shape=(square, square), in_specs=vmem(1)...  19.6 us
    ppermute x7, starting transfers between devices, corner(): move = lambda value, pairs: lax.ppermute(value, 'col', pairs)  14.3 us
    ppermute x27, waiting for transfers between devices, __call__(): result = [lax.ppermute(value, 'col', pairs)]  14.1 us
    pallas_call x1, Pallas kernels, update(): pl.pallas_call(functools.partial(update_kernel, names, rows), grid_spec=p...  11.9 us
    pallas_call x1, Pallas kernels, extract(): pl.pallas_call(functools.partial(extract_kernel, rows), grid_spec=pltpu.P...  10.9 us
    unnamed x20, local copies, waits for them, and re-layouts  5.28 us
  transfers between devices with their start and end apart: 35, of which 8 were waited for; matrix products, arithmetic and copies ran while one was open for 7% of the time, Pallas kernels for 20%

profile of v1, /device:TPU:24, one launch (start us, length us, event | category | flops | bytes accessed | tf_op | source)
XLA Modules:
  0.0 216.8 jit_solution(4784761010586537232)
XLA Ops:
  7.7 10.9 %shard_map.67 = f32[16,384,128]{2,1,0:T(8,128)} custom-call(s32[16]{0:T(128)} %fusion.5.order_ref, f32[12288,128]{1,0:T(8,128)} %bitcast.70), custom_call_target="tpu_custom_call" | custom-call | tf_op jit(solution)/shard_map/pallas_call | solution.py:84
  18.7 2.1 fusion.6
  22.1 1.5 collective-permute-start.10
  23.6 1.5 collective-permute-start.9
  25.2 1.5 collective-permute-start.7
  26.7 1.3 slice_reduce_fusion
  43.3 2.0 add_add_fusion
  45.4 8.1 %collective-permute-start.11 = (f32[384,128]{1,0:T(8,128)S(1)}, f32[384,128]{1,0:T(8,128)S(1)}, u32[]{:S(2)}, u32[]{:S(2)}) collective-permute-start(f32[384,128]{1,0:T(8,128)S(1)} %get-tuple-element.54), channel_id=1, source_target_pairs={{0,144},{8,104},{16,80},{24,208},{96,40},{104,48},{160,224},{168,6... | collective-permute-start | bytes 589832 | tf_op jit(solution)/shard_map/ppermute | solution.py:105
  54.8 1.9 collective-permute-start.15
  59.4 9.3 %collective-permute-start.12 = (f32[384,128]{1,0:T(8,128)S(1)}, f32[384,128]{1,0:T(8,128)S(1)}, u32[]{:S(2)}, u32[]{:S(2)}) collective-permute-start(f32[384,128]{1,0:T(8,128)S(1)} %get-tuple-element.55), channel_id=1, source_target_pairs={{0,216},{8,80},{16,112},{24,168},{96,240},{160,128},{168,208},{1,2... | collective-permute-start | bytes 589832 | tf_op jit(solution)/shard_map/ppermute | solution.py:105
  85.2 10.4 %collective-permute-start.19 = (f32[2,384,128]{2,1,0:T(8,128)S(1)}, f32[2,384,128]{2,1,0:T(8,128)S(1)}, u32[]{:S(2)}, u32[]{:S(2)}) collective-permute-start(f32[2,384,128]{2,1,0:T(8,128)S(1)} %pad_maximum_fusion.refs_0_), channel_id=1, source_target_pairs={{32,0},{40,8},{48,16},{56,24},{64,32},{72,40},{80,48},{88,56},{96,... | collective-permute-start | bytes 1179656 | tf_op jit(solution)/shard_map/ppermute | solution.py:105
  99.8 4.1 %collective-permute-done.19.refs_1_ = f32[2,384,128]{2,1,0:T(8,128)S(1)} collective-permute-done((f32[2,384,128]{2,1,0:T(8,128)S(1)}, f32[2,384,128]{2,1,0:T(8,128)S(1)}, u32[]{:S(2)}, u32[]{:S(2)}) %collective-permute-start.19) | collective-permute-done | bytes 393248 | tf_op jit(solution)/shard_map/ppermute | solution.py:105
  104.0 3.4 %collective-permute-done.18.refs_2_ = f32[2,384,128]{2,1,0:T(8,128)S(1)} collective-permute-done((f32[2,384,128]{2,1,0:T(8,128)S(1)}, f32[2,384,128]{2,1,0:T(8,128)S(1)}, u32[]{:S(2)}, u32[]{:S(2)}) %collective-permute-start.18) | collective-permute-done | bytes 393248 | tf_op jit(solution)/shard_map/ppermute | solution.py:105
  108.1 3.2 %collective-permute-start.22 = (f32[2,384,128]{2,1,0:T(8,128)S(1)}, f32[2,384,128]{2,1,0:T(8,128)S(1)}, u32[]{:S(2)}, u32[]{:S(2)}) collective-permute-start(f32[2,384,128]{2,1,0:T(8,128)S(1)} %collective-permute-done.19.refs_1_), channel_id=1, source_target_pairs={{32,0},{40,8},{48,16},{56,24},{64,32},{72,40},{80,48},{88,56},{96,... | collective-permute-start | bytes 1179656 | tf_op jit(solution)/shard_map/ppermute | solution.py:105
  112.2 2.1 collective-permute-start.4
  114.3 1.6 collective-permute-done.20.refs_3_
  115.9 2.0 collective-permute-start.3
  118.0 2.7 %collective-permute-done.22.refs_5_ = f32[2,384,128]{2,1,0:T(8,128)S(1)} collective-permute-done((f32[2,384,128]{2,1,0:T(8,128)S(1)}, f32[2,384,128]{2,1,0:T(8,128)S(1)}, u32[]{:S(2)}, u32[]{:S(2)}) %collective-permute-start.22) | collective-permute-done | bytes 393248 | tf_op jit(solution)/shard_map/ppermute | solution.py:105
  121.2 1.6 collective-permute-start.26
  122.8 3.1 %collective-permute-done.4 = f32[256,256]{1,0:T(8,128)} collective-permute-done((f32[256,256]{1,0:T(8,128)}, f32[256,256]{1,0:T(8,128)}, u32[]{:S(2)}, u32[]{:S(2)}) %collective-permute-start.4) | collective-permute-done | bytes 262176 | tf_op jit(solution)/shard_map/ppermute | solution.py:148
  126.5 1.3 collective-permute-start.27
  127.8 1.8 select_select_fusion.1
  129.6 1.6 collective-permute-done.24.refs_7_
  131.2 4.9 %collective-permute-start.6 = (f32[256,256]{1,0:T(8,128)}, f32[256,256]{1,0:T(8,128)}, u32[]{:S(2)}, u32[]{:S(2)}) collective-permute-start(f32[256,256]{1,0:T(8,128)} %select_select_fusion.1), channel_id=1, source_target_pairs={{0,224},{8,232},{16,240},{24,248},{96,64},{104,72},{112,80},{120,8... | collective-permute-start | bytes 786440 | tf_op jit(solution)/shard_map/ppermute | solution.py:148
  136.1 2.0 collective-permute-start.5
  140.9 3.2 %collective-permute-start.33 = (f32[2,192,128]{2,1,0:T(8,128)}, f32[2,192,128]{2,1,0:T(8,128)}, u32[]{:S(2)}, u32[]{:S(2)}) collective-permute-start(f32[2,192,128]{2,1,0:T(8,128)} %slice.87), channel_id=1, source_target_pairs={{24,0},{0,8},{8,16},{16,24},{56,32},{32,40},{40,48},{48,56},{88,64... | collective-permute-start | bytes 589832 | tf_op jit(solution)/shard_map/ppermute | solution.py:105
  144.1 3.2 %collective-permute-start.30 = (f32[2,384,128]{2,1,0:T(8,128)S(1)}, f32[2,384,128]{2,1,0:T(8,128)}, u32[]{:S(2)}, u32[]{:S(2)}) collective-permute-start(f32[2,384,128]{2,1,0:T(8,128)S(1)} %collective-permute-done.24.refs_7_), channel_id=1, source_target_pairs={{32,0},{40,8},{48,16},{56,24},{64,32},{72,40},{80,48},{88,56},{96,... | collective-permute-start | bytes 1179656 | tf_op jit(solution)/shard_map/ppermute | solution.py:105
  149.1 19.6 %shard_map.64 = (f32[128,128]{1,0:T(8,128)}, f32[128,128]{1,0:T(8,128)}) custom-call(f32[128,128]{1,0:T(8,128)} %get-tuple-element.104.a_ref), custom_call_target="tpu_custom_call" | custom-call | tf_op jit(solution)/shard_map/pallas_call | solution.py:243
  168.7 20.4 %shard_map.65 = (f32[128,128]{1,0:T(8,128)}, f32[128,128]{1,0:T(8,128)}, f32[128,128]{1,0:T(8,128)}) custom-call(f32[128,128]{1,0:T(8,128)} %get-tuple-element.103.a10_ref, f32[128,128]{1,0:T(8,128)} %get-tuple-element.102.a11_ref, f32[128,128]{1,0:T(8,128)} %get-tuple-element.48.w0_ref), custom_call_target="tpu_custom_call" | custom-call | tf_op jit(solution)/shard_map/pallas_call | solution.py:246
  189.0 3.8 %shard_map.66 = (f32[256,256]{1,0:T(8,128)}, f32[128,256]{1,0:T(8,128)}) custom-call(s32[2]{0:T(128)} %pad_add_fusion.place_ref, f32[256,256]{1,0:T(8,128)} %bitcast.74, f32[128,128]{1,0:T(8,128)} %get-tuple-element.47.d0_ref, f32[128,128]{1,0:T(8,128)} %get-tuple-element.48.w0_ref, f32[128,128]{1,0:T(8,128)} %get-tuple-element.49.l_ref, ...), custom_call_target="tpu_custom_call" | custom-call | tf_op jit(solution)/shard_map/pallas_call | solution.py:249
  192.9 2.8 %copy-done = f32[48,1,128,2,1,128]{5,4,3,2,1,0:T(1,128)S(1)} copy-done((f32[48,1,128,2,1,128]{5,4,3,2,1,0:T(1,128)S(1)}, f32[48,1,128,2,1,128]{5,4,3,2,1,0:T(1,128)}, u32[]{:S(2)}) %copy-start) | copy-done | bytes 6291480
  198.1 11.9 %shard_map.68 = f32[12288,128]{1,0:T(8,128)} custom-call(s32[16]{0:T(128)S(1)} %fusion.4.chunk_ref, s32[2]{0:T(128)S(1)} %copy-done.3, f32[12288,128]{1,0:T(8,128)S(1)} %bitcast.71, f32[256,256]{1,0:T(8,128)S(1)} %copy-done.1, f32[128,256]{1,0:T(8,128)S(1)} %copy-done.2, f32[2,384,128]{2,1,0:T(8,128)S(1)} %pad_maximum_fusion.refs_0_, ...), custom_call_target="tpu_custom_call" | custom-call | tf_op jit(solution)/shard_map/pallas_call | solution.py:296
  (88 shorter events, 27.3 us)
Async XLA Ops:
  6.5 89.0 %all-gather.2.cloned.1.call-start = ((), (), s32[]{:S(2)}) async-start(), calls=%async_computation | async-start | bytes 1179648 | tf_op jit(solution)/shard_map/all_gather | solution.py:315
  20.8 22.5 %collective-permute-start.8 = (f32[4,384,128]{2,1,0:T(8,128)S(1)}, f32[4,384,128]{2,1,0:T(8,128)}, u32[]{:S(2)}, u32[]{:S(2)}) collective-permute-start(f32[4,384,128]{2,1,0:T(8,128)S(1)} %get-tuple-element.89), channel_id=1, source_target_pairs={{0,24},{8,0},{1,25},{9,1},{2,26},{10,2},{3,27},{11,3},{4,28},{12,4... | collective-permute-start | bytes 2359304 | tf_op jit(solution)/shard_map/ppermute | solution.py:105
  22.1 21.2 %collective-permute-start.10 = (f32[4,384,128]{2,1,0:T(8,128)S(1)}, f32[4,384,128]{2,1,0:T(8,128)}, u32[]{:S(2)}, u32[]{:S(2)}) collective-permute-start(f32[4,384,128]{2,1,0:T(8,128)S(1)} %get-tuple-element.90), channel_id=1, source_target_pairs={{0,160},{8,168},{1,161},{9,169},{2,162},{10,170},{3,163},{11,171},... | collective-permute-start | bytes 2359304 | tf_op jit(solution)/shard_map/ppermute | solution.py:105
  23.6 19.7 %collective-permute-start.9 = (f32[4,384,128]{2,1,0:T(8,128)S(1)}, f32[4,384,128]{2,1,0:T(8,128)}, u32[]{:S(2)}, u32[]{:S(2)}) collective-permute-start(f32[4,384,128]{2,1,0:T(8,128)S(1)} %get-tuple-element.91), channel_id=1, source_target_pairs={{0,96},{8,104},{1,97},{9,105},{2,98},{10,106},{3,99},{11,107},{4,1... | collective-permute-start | bytes 2359304 | tf_op jit(solution)/shard_map/ppermute | solution.py:105
  25.2 18.1 %collective-permute-start.7 = (f32[4,384,128]{2,1,0:T(8,128)S(1)}, f32[4,384,128]{2,1,0:T(8,128)}, u32[]{:S(2)}, u32[]{:S(2)}) collective-permute-start(f32[4,384,128]{2,1,0:T(8,128)S(1)} %get-tuple-element.92), channel_id=1, source_target_pairs={{0,8},{8,16},{1,9},{9,17},{2,10},{10,18},{3,11},{11,19},{4,12},{12... | collective-permute-start | bytes 2359304 | tf_op jit(solution)/shard_map/ppermute | solution.py:105
  45.4 14.0 %collective-permute-start.11 = (f32[384,128]{1,0:T(8,128)S(1)}, f32[384,128]{1,0:T(8,128)S(1)}, u32[]{:S(2)}, u32[]{:S(2)}) collective-permute-start(f32[384,128]{1,0:T(8,128)S(1)} %get-tuple-element.54), channel_id=1, source_target_pairs={{0,144},{8,104},{16,80},{24,208},{96,40},{104,48},{160,224},{168,6... | collective-permute-start | bytes 589832 | tf_op jit(solution)/shard_map/ppermute | solution.py:105
  53.5 15.2 %collective-permute-start.13 = (f32[384,128]{1,0:T(8,128)S(1)}, f32[384,128]{1,0:T(8,128)S(1)}, u32[]{:S(2)}, u32[]{:S(2)}) collective-permute-start(f32[384,128]{1,0:T(8,128)S(1)} %get-tuple-element.96), channel_id=1, source_target_pairs={{0,32},{8,72},{16,88},{24,120},{96,144},{104,248},{160,200},{168,1... | collective-permute-start | bytes 589832 | tf_op jit(solution)/shard_map/ppermute | solution.py:105
  54.8 28.3 %collective-permute-start.15 = (f32[384,128]{1,0:T(8,128)S(1)}, f32[384,128]{1,0:T(8,128)S(1)}, u32[]{:S(2)}, u32[]{:S(2)}) collective-permute-start(f32[384,128]{1,0:T(8,128)S(1)} %get-tuple-element.57), channel_id=1, source_target_pairs={{0,96},{8,216},{16,200},{24,56},{96,176},{104,160},{160,48},{168,2... | collective-permute-start | bytes 589832 | tf_op jit(solution)/shard_map/ppermute | solution.py:105
  56.8 26.3 %collective-permute-start.16 = (f32[384,128]{1,0:T(8,128)S(1)}, f32[384,128]{1,0:T(8,128)S(1)}, u32[]{:S(2)}, u32[]{:S(2)}) collective-permute-start(f32[384,128]{1,0:T(8,128)S(1)} %get-tuple-element.58), channel_id=1, source_target_pairs={{0,176},{8,152},{16,128},{24,136},{96,184},{104,40},{160,16},{168,... | collective-permute-start | bytes 589832 | tf_op jit(solution)/shard_map/ppermute | solution.py:105
  58.1 25.0 %collective-permute-start.17 = (f32[384,128]{1,0:T(8,128)S(1)}, f32[384,128]{1,0:T(8,128)S(1)}, u32[]{:S(2)}, u32[]{:S(2)}) collective-permute-start(f32[384,128]{1,0:T(8,128)S(1)} %get-tuple-element.59), channel_id=1, source_target_pairs={{0,72},{8,248},{16,192},{24,232},{96,32},{104,184},{160,112},{168,... | collective-permute-start | bytes 589832 | tf_op jit(solution)/shard_map/ppermute | solution.py:105
  59.4 23.7 %collective-permute-start.12 = (f32[384,128]{1,0:T(8,128)S(1)}, f32[384,128]{1,0:T(8,128)S(1)}, u32[]{:S(2)}, u32[]{:S(2)}) collective-permute-start(f32[384,128]{1,0:T(8,128)S(1)} %get-tuple-element.55), channel_id=1, source_target_pairs={{0,216},{8,80},{16,112},{24,168},{96,240},{160,128},{168,208},{1,2... | collective-permute-start | bytes 589832 | tf_op jit(solution)/shard_map/ppermute | solution.py:105
  68.7 14.4 %collective-permute-start.14 = (f32[384,128]{1,0:T(8,128)S(1)}, f32[384,128]{1,0:T(8,128)S(1)}, u32[]{:S(2)}, u32[]{:S(2)}) collective-permute-start(f32[384,128]{1,0:T(8,128)S(1)} %get-tuple-element.56), channel_id=1, source_target_pairs={{0,240},{8,192},{16,224},{24,64},{104,152},{160,88},{168,120},{1,2... | collective-permute-start | bytes 589832 | tf_op jit(solution)/shard_map/ppermute | solution.py:105
  85.2 18.8 %collective-permute-start.19 = (f32[2,384,128]{2,1,0:T(8,128)S(1)}, f32[2,384,128]{2,1,0:T(8,128)S(1)}, u32[]{:S(2)}, u32[]{:S(2)}) collective-permute-start(f32[2,384,128]{2,1,0:T(8,128)S(1)} %pad_maximum_fusion.refs_0_), channel_id=1, source_target_pairs={{32,0},{40,8},{48,16},{56,24},{64,32},{72,40},{80,48},{88,56},{96,... | collective-permute-start | bytes 1179656 | tf_op jit(solution)/shard_map/ppermute | solution.py:105
  95.6 11.8 %collective-permute-start.18 = (f32[2,384,128]{2,1,0:T(8,128)S(1)}, f32[2,384,128]{2,1,0:T(8,128)S(1)}, u32[]{:S(2)}, u32[]{:S(2)}) collective-permute-start(f32[2,384,128]{2,1,0:T(8,128)S(1)} %pad_maximum_fusion.refs_0_), channel_id=1, source_target_pairs={{224,0},{232,8},{240,16},{248,24},{0,32},{8,40},{16,48},{24,56},{3... | collective-permute-start | bytes 1179656 | tf_op jit(solution)/shard_map/ppermute | solution.py:105
  96.6 11.5 %collective-permute-start.2 = (f32[256,128]{1,0:T(8,128)S(1)}, f32[256,128]{1,0:T(8,128)S(1)}, u32[]{:S(2)}, u32[]{:S(2)}) collective-permute-start(f32[256,128]{1,0:T(8,128)S(1)} %slice.89), channel_id=1, source_target_pairs={{0,24},{8,0},{1,25},{9,1},{2,26},{10,2},{3,27},{11,3},{4,28},{12,4... | collective-permute-start | bytes 393224 | tf_op jit(solution)/shard_map/ppermute | solution.py:148
  99.2 12.2 %collective-permute-start = (f32[256,128]{1,0:T(8,128)S(1)}, f32[256,128]{1,0:T(8,128)S(1)}, u32[]{:S(2)}, u32[]{:S(2)}) collective-permute-start(f32[256,128]{1,0:T(8,128)S(1)} %slice.89), channel_id=1, source_target_pairs={{0,8},{8,16},{1,9},{9,17},{2,10},{10,18},{3,11},{11,19},{4,12},{12... | collective-permute-start | bytes 393224 | tf_op jit(solution)/shard_map/ppermute | solution.py:148
  104.0 11.9 %collective-permute-start.20 = (f32[2,384,128]{2,1,0:T(8,128)S(1)}, f32[2,384,128]{2,1,0:T(8,128)S(1)}, u32[]{:S(2)}, u32[]{:S(2)}) collective-permute-start(f32[2,384,128]{2,1,0:T(8,128)S(1)} %pad_maximum_fusion.refs_0_), channel_id=1, source_target_pairs={{8,0},{16,8},{24,16},{0,24},{40,32},{48,40},{56,48},{32,56},{72,64... | collective-permute-start | bytes 1179656 | tf_op jit(solution)/shard_map/ppermute | solution.py:105
  108.1 13.1 %collective-permute-start.23 = (f32[2,384,128]{2,1,0:T(8,128)S(1)}, f32[2,384,128]{2,1,0:T(8,128)S(1)}, u32[]{:S(2)}, u32[]{:S(2)}) collective-permute-start(f32[2,384,128]{2,1,0:T(8,128)S(1)} %collective-permute-done.18.refs_2_), channel_id=1, source_target_pairs={{224,0},{232,8},{240,16},{248,24},{0,32},{8,40},{16,48},{24,56},{3... | collective-permute-start | bytes 1179656 | tf_op jit(solution)/shard_map/ppermute | solution.py:105
  108.1 12.7 %collective-permute-start.22 = (f32[2,384,128]{2,1,0:T(8,128)S(1)}, f32[2,384,128]{2,1,0:T(8,128)S(1)}, u32[]{:S(2)}, u32[]{:S(2)}) collective-permute-start(f32[2,384,128]{2,1,0:T(8,128)S(1)} %collective-permute-done.19.refs_1_), channel_id=1, source_target_pairs={{32,0},{40,8},{48,16},{56,24},{64,32},{72,40},{80,48},{88,56},{96,... | collective-permute-start | bytes 1179656 | tf_op jit(solution)/shard_map/ppermute | solution.py:105
  112.2 13.7 %collective-permute-start.4 = (f32[256,256]{1,0:T(8,128)}, f32[256,256]{1,0:T(8,128)}, u32[]{:S(2)}, u32[]{:S(2)}) collective-permute-start(f32[256,256]{1,0:T(8,128)} %pad_maximum_fusion.1), channel_id=1, source_target_pairs={{0,160},{8,168},{16,176},{24,184},{1,161},{9,169},{17,177},{25,185... | collective-permute-start | bytes 786440 | tf_op jit(solution)/shard_map/ppermute | solution.py:148
  117.9 13.3 %collective-permute-start.24 = (f32[2,384,128]{2,1,0:T(8,128)S(1)}, f32[2,384,128]{2,1,0:T(8,128)S(1)}, u32[]{:S(2)}, u32[]{:S(2)}) collective-permute-start(f32[2,384,128]{2,1,0:T(8,128)S(1)} %collective-permute-done.19.refs_1_), channel_id=1, source_target_pairs={{8,0},{16,8},{24,16},{0,24},{40,32},{48,40},{56,48},{32,56},{72,64... | collective-permute-start | bytes 1179656 | tf_op jit(solution)/shard_map/ppermute | solution.py:105
  120.8 15.4 %collective-permute-start.25 = (f32[2,384,128]{2,1,0:T(8,128)S(1)}, f32[2,384,128]{2,1,0:T(8,128)S(1)}, u32[]{:S(2)}, u32[]{:S(2)}) collective-permute-start(f32[2,384,128]{2,1,0:T(8,128)S(1)} %collective-permute-done.19.refs_1_), channel_id=1, source_target_pairs={{24,0},{0,8},{8,16},{16,24},{56,32},{32,40},{40,48},{48,56},{88,64... | collective-permute-start | bytes 1179656 | tf_op jit(solution)/shard_map/ppermute | solution.py:105
  121.2 19.6 %collective-permute-start.26 = (f32[2,384,128]{2,1,0:T(8,128)S(1)}, f32[2,384,128]{2,1,0:T(8,128)}, u32[]{:S(2)}, u32[]{:S(2)}) collective-permute-start(f32[2,384,128]{2,1,0:T(8,128)S(1)} %collective-permute-done.18.refs_2_), channel_id=1, source_target_pairs={{8,0},{16,8},{24,16},{0,24},{40,32},{48,40},{56,48},{32,56},{72,64... | collective-permute-start | bytes 1179656 | tf_op jit(solution)/shard_map/ppermute | solution.py:105
  125.9 15.0 %collective-permute-start.28 = (f32[2,384,128]{2,1,0:T(8,128)S(1)}, f32[2,384,128]{2,1,0:T(8,128)}, u32[]{:S(2)}, u32[]{:S(2)}) collective-permute-start(f32[2,384,128]{2,1,0:T(8,128)S(1)} %collective-permute-done.22.refs_5_), channel_id=1, source_target_pairs={{32,0},{40,8},{48,16},{56,24},{64,32},{72,40},{80,48},{88,56},{96,... | collective-permute-start | bytes 1179656 | tf_op jit(solution)/shard_map/ppermute | solution.py:105
  126.5 14.3 %collective-permute-start.27 = (f32[2,384,128]{2,1,0:T(8,128)S(1)}, f32[2,384,128]{2,1,0:T(8,128)}, u32[]{:S(2)}, u32[]{:S(2)}) collective-permute-start(f32[2,384,128]{2,1,0:T(8,128)S(1)} %collective-permute-done.18.refs_2_), channel_id=1, source_target_pairs={{24,0},{0,8},{8,16},{16,24},{56,32},{32,40},{40,48},{48,56},{88,64... | collective-permute-start | bytes 1179656 | tf_op jit(solution)/shard_map/ppermute | solution.py:105
  131.2 13.0 %collective-permute-start.6 = (f32[256,256]{1,0:T(8,128)}, f32[256,256]{1,0:T(8,128)}, u32[]{:S(2)}, u32[]{:S(2)}) collective-permute-start(f32[256,256]{1,0:T(8,128)} %select_select_fusion.1), channel_id=1, source_target_pairs={{0,224},{8,232},{16,240},{24,248},{96,64},{104,72},{112,80},{120,8... | collective-permute-start | bytes 786440 | tf_op jit(solution)/shard_map/ppermute | solution.py:148
  136.1 11.2 %collective-permute-start.5 = (f32[256,256]{1,0:T(8,128)}, f32[256,256]{1,0:T(8,128)}, u32[]{:S(2)}, u32[]{:S(2)}) collective-permute-start(f32[256,256]{1,0:T(8,128)} %select_select_fusion.1), channel_id=1, source_target_pairs={{0,32},{8,40},{16,48},{24,56},{96,128},{104,136},{112,144},{120,15... | collective-permute-start | bytes 786440 | tf_op jit(solution)/shard_map/ppermute | solution.py:148
  140.8 52.0 %collective-permute-start.29 = (f32[2,384,128]{2,1,0:T(8,128)S(1)}, f32[2,384,128]{2,1,0:T(8,128)}, u32[]{:S(2)}, u32[]{:S(2)}) collective-permute-start(f32[2,384,128]{2,1,0:T(8,128)S(1)} %collective-permute-done.23.refs_6_), channel_id=1, source_target_pairs={{224,0},{232,8},{240,16},{248,24},{0,32},{8,40},{16,48},{24,56},{3... | collective-permute-start | bytes 1179656 | tf_op jit(solution)/shard_map/ppermute | solution.py:105
  140.8 52.0 %collective-permute-start.32 = (f32[2,192,128]{2,1,0:T(8,128)}, f32[2,192,128]{2,1,0:T(8,128)}, u32[]{:S(2)}, u32[]{:S(2)}) collective-permute-start(f32[2,192,128]{2,1,0:T(8,128)} %slice.86), channel_id=1, source_target_pairs={{8,0},{16,8},{24,16},{0,24},{40,32},{48,40},{56,48},{32,56},{72,64... | collective-permute-start | bytes 589832 | tf_op jit(solution)/shard_map/ppermute | solution.py:105
  140.9 51.9 %collective-permute-start.33 = (f32[2,192,128]{2,1,0:T(8,128)}, f32[2,192,128]{2,1,0:T(8,128)}, u32[]{:S(2)}, u32[]{:S(2)}) collective-permute-start(f32[2,192,128]{2,1,0:T(8,128)} %slice.87), channel_id=1, source_target_pairs={{24,0},{0,8},{8,16},{16,24},{56,32},{32,40},{40,48},{48,56},{88,64... | collective-permute-start | bytes 589832 | tf_op jit(solution)/shard_map/ppermute | solution.py:105
  144.1 48.7 %collective-permute-start.30 = (f32[2,384,128]{2,1,0:T(8,128)S(1)}, f32[2,384,128]{2,1,0:T(8,128)}, u32[]{:S(2)}, u32[]{:S(2)}) collective-permute-start(f32[2,384,128]{2,1,0:T(8,128)S(1)} %collective-permute-done.24.refs_7_), channel_id=1, source_target_pairs={{32,0},{40,8},{48,16},{56,24},{64,32},{72,40},{80,48},{88,56},{96,... | collective-permute-start | bytes 1179656 | tf_op jit(solution)/shard_map/ppermute | solution.py:105
  147.3 45.6 %collective-permute-start.31 = (f32[2,384,128]{2,1,0:T(8,128)}, f32[2,384,128]{2,1,0:T(8,128)}, u32[]{:S(2)}, u32[]{:S(2)}) collective-permute-start(f32[2,384,128]{2,1,0:T(8,128)} %collective-permute-done.26.refs_9_), channel_id=1, source_target_pairs={{224,0},{232,8},{240,16},{248,24},{0,32},{8,40},{16,48},{24,56},{3... | collective-permute-start | bytes 1179656 | tf_op jit(solution)/shard_map/ppermute | solution.py:105
  (13 other events, 143.7 us)
Sparse Core Ops, SparseCore 0:
  28.9 30.9 all-gather.1

commit v2 on v0

v2 whole, which is shorter than its diff:
```python
import functools

import jax
import jax.numpy as jnp
import numpy as np
from jax import lax
from jax.experimental import pallas as pl
from jax.experimental.pallas import tpu as pltpu
from jax.sharding import PartitionSpec as P

F32 = jnp.float32
BF16 = jnp.bfloat16
NZ, NY = 8, 4
ROWS = 8
ROOTS = (0, 1)
SUBROOTS = ((0, 0), (0, 3), (2, 0), (6, 0))
QUARTERS = ((0, 0), (0, 2), (2, 1), (2, 3), (0, 1), (0, 3), (1, 3), (3, 0), (1, 1), (1, 2), (2, 0), (3, 3), (1, 0), (2, 2), (3, 1), (3, 2))
DELIVER = (
    ((0, 9, 2, 0), (1, 10, 3, 1), (2, 16, 1, 1), (3, 19, 0, 0), (8, 15, 3, 0), (9, 28, 3, 1), (24, 13, 2, 0), (25, 29, 3, 1)),
    ((0, 27, 2, 0), (1, 24, 3, 1), (2, 31, 3, 1), (3, 17, 1, 0), (8, 6, 1, 0), (9, 4, 0, 1), (24, 14, 3, 0), (25, 12, 2, 1)),
    ((0, 25, 3, 0), (1, 26, 2, 1), (2, 0, 0, 1), (3, 1, 0, 0), (8, 23, 0, 0), (9, 22, 0, 1), (24, 10, 1, 0), (25, 11, 1, 1)),
    ((0, 2, 1, 0), (1, 8, 2, 1), (2, 6, 2, 1), (3, 30, 3, 0), (8, 26, 2, 0), (9, 14, 3, 1), (24, 28, 3, 0), (25, 5, 0, 1)),
    ((0, 11, 3, 0), (1, 17, 1, 1), (2, 18, 0, 1), (3, 21, 2, 0), (8, 5, 0, 0), (9, 27, 2, 1), (24, 4, 0, 0), (25, 15, 3, 1)),
    ((0, 16, 1, 0), (1, 3, 1, 1), (2, 20, 2, 1), (3, 12, 3, 0), (8, 29, 3, 0), (9, 7, 1, 1), (24, 31, 2, 0), (25, 23, 0, 1)),
    ((0, 18, 0, 0), (1, 19, 0, 1), (2, 13, 3, 1), (3, 7, 2, 0), (8, 20, 1, 0), (9, 21, 1, 1), (24, 22, 0, 0), (25, 30, 2, 1)),
)


WORKERS = (20, 21)


def at(z, y):
    return (z % NZ) * NY + y % NY


def seen_from(root, z, y):
    return at(z, y) if root == 0 else at(z, ROOTS[1] - y)


def place(chip):
    return chip // NY, chip % NY


PIECES = 16
CHIPS = NZ * NY


def class_of(z, y):
    z, y = z & (NZ - 1), y & (NY - 1)
    return (z & 3) * 4 + ((y + ((z >> 2) << 1)) & 3)


def is_in(chips, chip):
    return ((jnp.uint32(sum(1 << c for c in chips)) >> chip.astype(jnp.uint32)) & 1) == 1


def lookup(slots, chip):
    low = is_in([c for c, slot in slots.items() if slot & 1], chip).astype(jnp.int32)
    high = is_in([c for c, slot in slots.items() if slot & 2], chip).astype(jnp.int32)
    return low + 2 * high


def extract_kernel(rows, where_ref, x_ref, *refs):
    outs, buffer, sem = refs[:-2], refs[-2], refs[-1]
    copies = []
    second = where_ref[1] == ROOTS[1]
    for k, (z, y) in enumerate(QUARTERS):
        piece = jnp.where(second, class_of(z, ROOTS[1] - y), class_of(z, y))
        start = pl.multiple_of(piece * (2 * rows), 2 * rows)
        copies.append(pltpu.make_async_copy(x_ref.at[pl.ds(start, 2 * rows)], buffer.at[k], sem.at[k]))
        copies[-1].start()
    for k, copy in enumerate(copies):
        copy.wait()
        outs[k // 4][k % 4] = buffer[k, pl.ds(0, rows, stride=2), :]


def extract(x, where, rows):
    return pl.pallas_call(
        functools.partial(extract_kernel, rows),
        out_shape=(jax.ShapeDtypeStruct((4, rows, 128), F32),) * 4,
        in_specs=[pl.BlockSpec(memory_space=pltpu.SMEM), pl.BlockSpec(memory_space=pltpu.HBM)],
        out_specs=tuple(vmem(4)),
        cost_estimate=cost(0, PIECES * rows * 3 * 2**9),
        scratch_shapes=[pltpu.VMEM((PIECES, 2 * rows, 128), F32), pltpu.SemaphoreType.DMA((PIECES,))],
        compiler_params=pltpu.CompilerParams(vmem_limit_bytes=60 * 1024 * 1024),
    )(where, x)


class Sender:
    def __init__(self, depth):
        self.depth = depth
        self.sent = []

    def __call__(self, value, pairs, axis="col"):
        if len(self.sent) >= self.depth:
            oldest = self.sent[-self.depth]
            value, oldest[0] = lax.optimization_barrier((value, oldest[0]))
        result = [lax.ppermute(value, axis, pairs)]
        self.sent.append(result)
        return result


def tie(*values):
    return lax.optimization_barrier(values)


def shift(fz, fy):
    return [(at(z + fz, y + fy), at(z, y)) for z in range(NZ) for y in range(NY)]


BOTH = ("col", "row")


def cores(pairs, shift=0):
    return [(a * ROWS + i, b * ROWS + 2 * shift + i) for a, b in pairs for i in (0, 1)]


def to_workers(send, block, row):
    swap = [(root * ROWS + i, root * ROWS + 1 - i) for root in ROOTS for i in (0, 1)]
    other = send(block, swap, BOTH)[0]
    pair = jnp.where(row == 0, jnp.concatenate([block, other]), jnp.concatenate([other, block]))
    return send(pair, cores(zip(ROOTS, WORKERS)), BOTH)


def scatter(send, own, got, row, chip):
    quarters = [
        send(own[k], [(root, seen_from(p, *SUBROOTS[k])) for p, root in enumerate(ROOTS)]) for k in (1, 2, 3)
    ]
    got = got[0]
    other = send(got, cores([WORKERS, WORKERS[::-1]]), BOTH)[0]
    quarter = jnp.where(chip < 2, own[0], sum(q[0] for q in quarters))
    arrived = []

    def deal(count):
        for _ in range(count):
            sends = DELIVER[len(arrived)]
            slot = lookup({source: slot for source, _, slot, _ in sends}, chip)
            value = lax.dynamic_index_in_dim(quarter, slot, 0, keepdims=False)
            arrived.append(send(value, [(source, target) for source, target, _, _ in sends]))

    deal(4)
    first, second = jnp.where(chip == WORKERS[0], got, other), jnp.where(chip == WORKERS[0], other, got)
    whole = jnp.concatenate([first, second[128:]])
    factor = lax.cond(is_in(WORKERS, chip) & (row < 2), factor_corner, jnp.zeros_like, whole)
    factor, quarter = tie(factor, quarter)
    deal(1)
    factor = factor + sum(send(factor, cores([(w, w) for w in WORKERS], k), BOTH)[0] for k in (1, 3, 2))
    deal(len(DELIVER) - len(arrived))
    places = {}
    for panel in (0, 1):
        for k, (pz, py) in enumerate(SUBROOTS):
            kinds = [class_of(*m) for m in QUARTERS[4 * k : 4 * k + 4]]
            places[seen_from(panel, pz, py)] = kinds.index(class_of(pz, py))
    held = lax.dynamic_index_in_dim(quarter, lookup(places, chip), 0, keepdims=False)
    mine = []
    for panel in (0, 1):
        value = held
        for k, sends in enumerate(DELIVER):
            got = is_in([target for _, target, _, p in sends if p == panel], chip)
            value = jnp.where(got, arrived[k][0], value)
        mine.append(value)
    return jnp.stack(mine), factor


def share_far(send, factor):
    z, y = place(WORKERS[0])
    line = send(factor, [(at(z, y), at(z, y - 1)), (at(z, y + 1), at(z, y + 2))])[0]
    line = factor + line
    far = send(line, [(at(z, j), at(z + 3, j)) for j in range(NY)])
    back = send(line, [(at(z, j), at(z - 3, j)) for j in range(NY)])
    return line + far[0] + back[0]


def share_near(send, base, chip):
    z = place(WORKERS[0])[0]
    above = send(base, [(at(z + k, j), at(z + k + 1, j)) for k in (0, 3, -3) for j in range(NY)])
    below = send(base, [(at(z + k, j), at(z + k - 1, j)) for k in (0, 3) for j in range(NY)])
    return base + above[0] + below[0]


def dot(a, b, dims):
    return lax.dot_general(
        a, b, ((dims[:1], dims[1:]), ((), ())), precision=lax.Precision.HIGHEST, preferred_element_type=F32
    )


def eliminate(block):
    n = block.shape[0]
    block = 0.5 * (block + block.T)
    row_id = lax.broadcasted_iota(jnp.int32, (8, n), 0)
    lane_id = lax.broadcasted_iota(jnp.int32, (8, n), 1)
    left = [block[8 * k : 8 * k + 8] for k in range(n // 8)]
    right = [jnp.where(lane_id == row_id + 8 * k, 1.0, 0.0).astype(F32) for k in range(n // 8)]
    spread_rows = lambda v, r: jnp.broadcast_to(v[r : r + 1, :], (8, n))
    spread_lanes = lambda v, j: jnp.broadcast_to(v[:, j : j + 1], (8, n))
    for j in range(0, n, 2):
        k0, r = j // 8, j % 8
        lanes0 = [spread_lanes(left[k], j) for k in range(k0, n // 8)]
        lanes1 = [spread_lanes(left[k], j + 1) for k in range(k0, n // 8)]
        a, b, c = spread_rows(lanes0[0], r), spread_rows(lanes0[0], r + 1), spread_rows(lanes1[0], r + 1)
        over = 1.0 / (a * c - b * b)
        done = []
        for part in (left, right):
            row0, row1 = spread_rows(part[k0], r), spread_rows(part[k0], r + 1)
            u0, u1 = (c * row0 - b * row1) * over, (a * row1 - b * row0) * over
            done.append((row0, row1))
            for k in range(k0, n // 8):
                new = part[k] - (lanes0[k - k0] * u0 + lanes1[k - k0] * u1)
                part[k] = jnp.where(row_id > r + 1, new, part[k]) if k == k0 else new
        first = 1.0 / jnp.sqrt(a)
        ratio = b / a
        second = 1.0 / jnp.sqrt(c - b * ratio)
        row0, row1 = done[1]
        right[k0] = jnp.where(
            row_id == r, row0 * first, jnp.where(row_id == r + 1, (row1 - ratio * row0) * second, right[k0])
        )
    return jnp.concatenate(right, axis=0)


def factor_kernel(a_ref, o_ref):
    inverse = eliminate(a_ref[:128])
    o_ref[:128] = inverse
    low = dot(a_ref[128:256], inverse, (1, 1))
    o_ref[128:256] = low
    o_ref[256:] = eliminate(a_ref[256:] - dot(low, low, (1, 1)))


def combine_kernel(place_ref, head_ref, f_ref, m_ref, s_ref):
    row, col = place_ref[0], place_ref[1]
    w0, low, w1 = f_ref[:128], f_ref[128:256], f_ref[256:]
    head0, head1 = head_ref[0], head_ref[1]
    g0 = dot(w0, head0, (1, 0))
    rest = head1 - dot(low, g0, (1, 0))
    g1 = dot(w1, rest, (1, 0))
    m1 = dot(w1, g1, (0, 0))
    m0 = dot(w0, g0 - dot(low, m1, (0, 0)), (0, 0))
    mixed = dot(w0, dot(low, w1, (0, 1)), (0, 0))
    zero = jnp.zeros((128, 128), F32)
    root0, root1 = col == ROOTS[0], col == ROOTS[1]
    m_ref[:128, 128:] = m0[:, 128:]
    m_ref[128:, 128:] = m1[:, 128:]
    m_ref[:128, :128] = jnp.where(root0, -w0.T, jnp.where(root1, mixed, m0[:, :128]))
    m_ref[128:, :128] = jnp.where(root0, zero, jnp.where(root1, -w1.T, m1[:, :128]))
    top = row == 0
    s_ref[:, 128:] = jnp.where(top, head0[:, 128:], rest[:, 128:])
    normal = jnp.where(top, head0[:, :128], rest[:, :128])
    lower = lax.broadcasted_iota(jnp.int32, (128, 128), 0) >= lax.broadcasted_iota(jnp.int32, (128, 128), 1)
    diagonal = jnp.where(top, dot(head0[:, :128], w0, (1, 1)), dot(rest[:, :128], w1, (1, 1)))
    diagonal = jnp.where(lower, diagonal, 0.0)
    on0 = jnp.where(top, diagonal, low)
    on1 = jnp.where(top, zero, diagonal)
    s_ref[:, :128] = jnp.where(root0, on0, jnp.where(root1, on1, normal))


def cost(flops, size):
    return pl.CostEstimate(flops=flops, bytes_accessed=size, transcendentals=0)


def vmem(count):
    return [pl.BlockSpec(memory_space=pltpu.VMEM)] * count


def factor_corner(whole):
    return pl.pallas_call(
        factor_kernel,
        out_shape=jax.ShapeDtypeStruct((384, 128), F32),
        in_specs=vmem(1),
        out_specs=vmem(1)[0],
        cost_estimate=cost(24 * 10**9, 6 * 2**16),
    )(whole)


def combine(heads, factor, where):
    return pl.pallas_call(
        combine_kernel,
        out_shape=(jax.ShapeDtypeStruct((256, 256), F32), jax.ShapeDtypeStruct((128, 256), F32)),
        grid=(1,),
        in_specs=[pl.BlockSpec(memory_space=pltpu.SMEM), pl.BlockSpec((2, 128, 256), lambda i: (0, 0, 0))] + vmem(1),
        out_specs=tuple(vmem(2)),
        cost_estimate=cost(4 * 10**9, 2**20),
    )(where, heads, factor)


def update_kernel(parts, keys, rows, aliased, place_ref, x_ref, m_ref, s_ref, *refs):
    count = len(parts)
    o_ref, xs, wide, chunk_ref, x_sem, p_sem, o_sem = refs[-7:]
    pieces = refs[: len(refs) - 7 - (1 if aliased else 0)]
    col_z, col_y = place_ref[1] >> 2, place_ref[1] & 3
    for k, (z, y) in enumerate(keys):
        chunk_ref[k] = class_of(col_z + z, col_y + y)

    def rows_of(ref, k):
        return ref.at[pl.ds(pl.multiple_of(chunk_ref[k] * (2 * rows), 2 * rows), 2 * rows)]

    def x_copy(k):
        return pltpu.make_async_copy(rows_of(x_ref, k), xs.at[k], x_sem.at[k])

    def o_copy(k):
        return pltpu.make_async_copy(xs.at[k], rows_of(o_ref, k), o_sem.at[k])

    for k, sources in enumerate(parts):
        x_copy(k).start()
        start = 0
        for which, offset, size in sources:
            for panel in (0, 1):
                pltpu.make_async_copy(
                    pieces[which].at[panel, pl.ds(offset, size)],
                    wide.at[k, pl.ds(start, size), pl.ds(128 * panel, 128)],
                    p_sem.at[k],
                ).start()
            start += size
    m = m_ref[...]
    m_high = m.astype(BF16)
    m_rest = (m - m_high.astype(F32)).astype(BF16)
    m_wide = jnp.concatenate([m_high, m_high, m_rest], axis=0)
    root = place_ref[1] < 2

    def step(k, carry):
        pltpu.make_async_copy(wide.at[k], wide.at[k], p_sem.at[k]).wait()
        value = wide[k]
        high = value.astype(BF16)
        rest = (value - high.astype(F32)).astype(BF16)
        product = jnp.dot(
            jnp.concatenate([high, rest, high], axis=1), m_wide, preferred_element_type=F32
        )
        x_copy(k).wait()
        left = xs[k, pl.ds(0, rows, stride=2), :]
        xs[k, pl.ds(0, rows, stride=2), :] = jnp.where(root, 0.0, left) - product[:, :128]
        xs[k, pl.ds(1, rows, stride=2), :] = xs[k, pl.ds(1, rows, stride=2), :] - product[:, 128:]

        @pl.when((chunk_ref[k] == 0) & (place_ref[0] < 2))
        def _():
            xs[k, pl.ds(0, 128, stride=2), :] = s_ref[:, :128]
            xs[k, pl.ds(1, 128, stride=2), :] = s_ref[:, 128:]

        o_copy(k).start()
        return carry

    lax.fori_loop(0, count, step, 0)

    def finish(k, carry):
        o_copy(k).wait()
        return carry

    lax.fori_loop(0, count, finish, 0)


def update(x, m, special, parts, keys, where, rows, out=None):
    arrays = []
    for sources in parts:
        for array, _, _ in sources:
            if not any(array is other for other in arrays):
                arrays.append(array)
    place_of = lambda array: [other is array for other in arrays].index(True)
    parts = [tuple((place_of(array), offset, size) for array, offset, size in sources) for sources in parts]
    count = len(parts)
    in_hbm = [pl.BlockSpec(memory_space=pltpu.HBM)]
    operands = [where, x, m, special, *arrays] + ([] if out is None else [out])
    return pl.pallas_call(
        functools.partial(update_kernel, parts, keys, rows, out is not None),
        out_shape=jax.ShapeDtypeStruct(x.shape, F32),
        in_specs=[pl.BlockSpec(memory_space=pltpu.SMEM)]
        + in_hbm
        + vmem(2)
        + [pl.BlockSpec(memory_space=pl.ANY)] * (len(operands) - 4),
        out_specs=in_hbm[0],
        scratch_shapes=[
            pltpu.VMEM((count, 2 * rows, 128), F32),
            pltpu.VMEM((count, rows, 256), F32),
            pltpu.SMEM((count,), jnp.int32),
            pltpu.SemaphoreType.DMA((count,)),
            pltpu.SemaphoreType.DMA((count,)),
            pltpu.SemaphoreType.DMA((count,)),
        ],
        cost_estimate=cost(count * rows * 2**18, count * rows * 3 * 2**10),
        input_output_aliases={} if out is None else {len(operands) - 1: 0},
        compiler_params=pltpu.CompilerParams(vmem_limit_bytes=60 * 1024 * 1024),
    )(*operands)


def body(slab):
    row, col = lax.axis_index("row"), lax.axis_index("col")
    x = slab.reshape(slab.shape[0] * 128 * 2, 128)
    rows = x.shape[0] // (2 * PIECES)
    half = rows // 2
    where = jnp.stack([row, col]).astype(jnp.int32)
    top, x = tie(x[:256].reshape(128, 256), x)
    send = Sender(5)
    got = to_workers(send, top[:, :128], row)
    own = extract(x, where, rows)
    heads = lax.all_gather(top, "row", axis=0)
    mine, factor = scatter(send, own, got, row, col)

    north, south = send(mine, shift(1, 0)), send(mine, shift(-1, 0))
    east, west = send(mine, shift(0, 1)), send(mine, shift(0, -1))
    factor = share_far(send, factor)
    north, south, east, west = north[0], south[0], east[0], west[0]
    north2, south2 = send(north, shift(1, 0)), send(south, shift(-1, 0))
    east2 = send(jnp.concatenate([north, south, east[:, :half]], axis=1), shift(0, 1))
    west2 = send(jnp.concatenate([north, south, west[:, half:]], axis=1), shift(0, -1))
    factor = share_near(send, factor, col)
    north2, south2 = north2[0], south2[0]
    north3, south3 = send(north2, shift(1, 0)), send(south2, shift(-1, 0))
    m, special = combine(heads, factor, where)
    east2 = east2[0]
    corner0, corner1 = send(east2[:, :rows], shift(1, 0)), send(east2[:, rows : 2 * rows], shift(-1, 0))

    def whole_piece(array):
        return ((array, 0, rows),)

    keys = [(0, 0), (1, 0), (-1, 0), (0, 1), (0, -1), (2, 0), (-2, 0)]
    parts = [whole_piece(v) for v in (mine, north, south, east, west, north2, south2)]
    out = update(x, m, special, parts, keys, where, rows)
    west2, north3, south3 = west2[0], north3[0], south3[0]
    keys = [(1, 1), (-1, 1), (1, -1), (-1, -1), (0, 2), (3, 0), (-3, 0)]
    parts = [((v, k * rows, rows),) for v in (east2, west2) for k in (0, 1)]
    parts += [((east2, 2 * rows, half), (west2, 2 * rows, half)), whole_piece(north3), whole_piece(south3)]
    out = update(x, m, special, parts, keys, where, rows, out)
    parts = [whole_piece(corner0[0]), whole_piece(corner1[0])]
    out = update(x, m, special, parts, [(2, 1), (-2, 1)], where, rows, out)
    return out.reshape(slab.shape)


def solution(mesh):
    spec = P(None, "row", None, None, "col", None)
    return jax.shard_map(body, mesh=mesh, in_specs=(spec,), out_specs=spec, check_vma=False)
```

time: 651 us -> 154 us (0.24)
  waiting for transfers between devices: 507 us -> 56.1 us
  other arithmetic: 58.2 us -> 3.79 us
  starting transfers between devices: 0.61 us -> 52.1 us
  local copies, waits for them, and re-layouts: 36.5 us -> 3.36 us
  matrix products: 31.9 us -> 0 us
  Pallas kernels: 0 us -> 24.4 us
    psum x4 -> x0, waiting for transfers between devices: 441 us -> none  [from_root(): return lax.psum(kept, axis)]
    all_gather x2 -> x1, waiting for transfers between devices: 65.9 us -> 0.01 us  [body(): heads = lax.all_gather(top, 'row', axis=0)]
    ppermute x0 -> x33, waiting for transfers between devices: none -> 56.1 us  [__call__(): result = [lax.ppermute(value, axis, pairs)]]
    ppermute x0 -> x33, starting transfers between devices: none -> 52.1 us  [__call__(): result = [lax.ppermute(value, axis, pairs)]]
    another operation x11 -> x4, other arithmetic: 46.3 us -> 0.85 us  [the longest x1 0.67 us: body(): where = jnp.stack([row, col]).astype(jnp.int32)]
    pallas_call x0 -> x5, Pallas kernels: none -> 24.4 us  [the longest x3 15.2 us: update(): pl.pallas_call(functools.partial(update_kernel, parts, keys, rows, out is...]
    dot_general x2 -> x0, matrix products: 19.6 us -> none  [body(): jnp.dot(lowpart, jnp.concatenate(pieces, 0).T, precision=lax.Precision.HI...]
    reshape x4 -> x0, local copies, waits for them, and re-layouts: 18.8 us -> none  [the longest x1 10.2 us: body(): return local.reshape(slab.shape)]
  transfers between devices with their start and end apart: 6 -> 34, of which waited for: 6 -> 8; matrix products, arithmetic and copies ran while one was open for 0% -> 2% of each run, Pallas kernels for 0% -> 14%
where the time goes in v2:
time: 154 us
  waiting for transfers between devices  56.1 us (36%)
  starting transfers between devices  52.1 us (34%)
  Pallas kernels  24.4 us (16%)
  between operations  14.1 us (9%)
  other arithmetic  3.79 us (2%)
  local copies, waits for them, and re-layouts  3.36 us (2%)
    ppermute x33, waiting for transfers between devices, __call__(): result = [lax.ppermute(value, axis, pairs)]  56.1 us
    ppermute x33, starting transfers between devices, __call__(): result = [lax.ppermute(value, axis, pairs)]  52.1 us
    pallas_call x3, Pallas kernels, update(): pl.pallas_call(functools.partial(update_kernel, parts, keys, rows, out is...  15.2 us
    pallas_call x1, Pallas kernels, extract(): pl.pallas_call(functools.partial(extract_kernel, rows), out_shape=(jax.Sh...  5.25 us
    pallas_call x1, Pallas kernels, combine(): pl.pallas_call(combine_kernel, out_shape=(jax.ShapeDtypeStruct((256, 256)...  3.95 us
  transfers between devices with their start and end apart: 34, of which 8 were waited for; matrix products, arithmetic and copies ran while one was open for 2% of the time, Pallas kernels for 14%

profile of v2, /device:TPU:24, one launch (start us, length us, event | category | flops | bytes accessed | tf_op | source)
XLA Modules:
  0.0 153.8 jit_solution(17571307765229231437)
XLA Ops:
  6.5 1.3 slice_reduce_fusion
  9.9 5.2 %shard_map.17 = (f32[4,384,128]{2,1,0:T(8,128)}, f32[4,384,128]{2,1,0:T(8,128)}, f32[4,384,128]{2,1,0:T(8,128)}, f32[4,384,128]{2,1,0:T(8,128)}) custom-call(s32[2]{0:T(128)} %pad_add_fusion.where_ref.place_ref, f32[12288,128]{1,0:T(8,128)} %bitcast.60), custom_call_target="tpu_custom_call" | custom-call | bytes 9437184 | tf_op jit(solution)/shard_map/pallas_call | solution.py:78
  15.2 1.3 collective-permute-start.3
  19.5 22.7 %collective-permute-done.3 = f32[4,384,128]{2,1,0:T(8,128)S(1)} collective-permute-done((f32[4,384,128]{2,1,0:T(8,128)}, f32[4,384,128]{2,1,0:T(8,128)S(1)}, u32[]{:S(2)}, u32[]{:S(2)}) %collective-permute-start.3) | collective-permute-done | bytes 786464 | tf_op jit(solution)/shard_map/ppermute | solution.py:98
  43.1 1.3 add_select_fusion
  44.4 13.0 %collective-permute-start.12 = (f32[384,128]{1,0:T(8,128)S(1)}, f32[384,128]{1,0:T(8,128)S(1)}, u32[]{:S(2)}, u32[]{:S(2)}) collective-permute-start(f32[384,128]{1,0:T(8,128)S(1)} %get-tuple-element.72), channel_id=1, source_target_pairs={{0,88},{8,136},{16,144},{24,168},{64,40},{72,216},{192,32},{200,12... | collective-permute-start | bytes 589832 | tf_op jit(solution)/shard_map/ppermute | solution.py:98
  57.5 1.3 collective-permute-start.15
  58.8 1.3 collective-permute-start.6
  60.1 1.3 collective-permute-start.8
  61.4 1.3 collective-permute-start.10
  62.7 1.3 collective-permute-start.13
  64.0 1.9 %collective-permute-start.16 = (f32[384,128]{1,0:T(8,128)S(1)}, f32[384,128]{1,0:T(8,128)S(1)}, u32[]{:S(2)}, u32[]{:S(2)}) collective-permute-start(f32[384,128]{1,0:T(8,128)S(1)} %get-tuple-element.76), channel_id=1, source_target_pairs={{0,128},{8,24},{16,160},{24,96},{64,232},{72,56},{192,248},{200,18... | collective-permute-start | bytes 589832 | tf_op jit(solution)/shard_map/ppermute | solution.py:98
  66.7 2.9 %collective-permute-done.8 = f32[384,128]{1,0:T(8,128)S(1)} collective-permute-done((f32[384,128]{1,0:T(8,128)S(1)}, f32[384,128]{1,0:T(8,128)S(1)}, u32[]{:S(2)}, u32[]{:S(2)}) %collective-permute-start.8) | collective-permute-done | bytes 196640 | tf_op jit(solution)/shard_map/ppermute | solution.py:98
  71.0 1.9 %collective-permute-done.13 = f32[384,128]{1,0:T(8,128)S(1)} collective-permute-done((f32[384,128]{1,0:T(8,128)S(1)}, f32[384,128]{1,0:T(8,128)S(1)}, u32[]{:S(2)}, u32[]{:S(2)}) %collective-permute-start.13) | collective-permute-done | bytes 196640 | tf_op jit(solution)/shard_map/ppermute | solution.py:98
  72.9 2.8 %collective-permute-done.16 = f32[384,128]{1,0:T(8,128)S(1)} collective-permute-done((f32[384,128]{1,0:T(8,128)S(1)}, f32[384,128]{1,0:T(8,128)S(1)}, u32[]{:S(2)}, u32[]{:S(2)}) %collective-permute-start.16) | collective-permute-done | bytes 196640 | tf_op jit(solution)/shard_map/ppermute | solution.py:98
  76.0 3.8 %collective-permute-start.19 = (f32[2,384,128]{2,1,0:T(8,128)S(1)}, f32[2,384,128]{2,1,0:T(8,128)S(1)}, u32[]{:S(2)}, u32[]{:S(2)}) collective-permute-start(f32[2,384,128]{2,1,0:T(8,128)S(1)} %pad_maximum_fusion.3.refs_0_), channel_id=1, source_target_pairs={{224,0},{232,8},{240,16},{248,24},{0,32},{8,40},{16,48},{24,56},{3... | collective-permute-start | bytes 1179656 | tf_op jit(solution)/shard_map/ppermute | solution.py:98
  79.8 3.2 %collective-permute-start.25 = (f32[2,384,128]{2,1,0:T(8,128)S(1)}, f32[2,384,128]{2,1,0:T(8,128)S(1)}, u32[]{:S(2)}, u32[]{:S(2)}) collective-permute-start(f32[2,384,128]{2,1,0:T(8,128)S(1)} %pad_maximum_fusion.3.refs_0_), channel_id=1, source_target_pairs={{24,0},{0,8},{8,16},{16,24},{56,32},{32,40},{40,48},{48,56},{88,64... | collective-permute-start | bytes 1179656 | tf_op jit(solution)/shard_map/ppermute | solution.py:98
  83.8 1.5 collective-permute-done.17.refs_1_
  85.3 6.1 %collective-permute-done.22.refs_3_ = f32[2,384,128]{2,1,0:T(8,128)S(1)} collective-permute-done((f32[2,384,128]{2,1,0:T(8,128)S(1)}, f32[2,384,128]{2,1,0:T(8,128)S(1)}, u32[]{:S(2)}, u32[]{:S(2)}) %collective-permute-start.22) | collective-permute-done | bytes 393248 | tf_op jit(solution)/shard_map/ppermute | solution.py:98
  91.8 1.3 collective-permute-start.18
  93.8 11.0 %collective-permute-done.18 = f32[384,128]{1,0:T(8,128)S(1)} collective-permute-done((f32[384,128]{1,0:T(8,128)S(1)}, f32[384,128]{1,0:T(8,128)S(1)}, u32[]{:S(2)}, u32[]{:S(2)}) %collective-permute-start.18) | collective-permute-done | bytes 196640 | tf_op jit(solution)/shard_map/ppermute | solution.py:98
  104.8 2.9 %collective-permute-start.28 = (f32[2,960,128]{2,1,0:T(8,128)S(1)}, f32[2,960,128]{2,1,0:T(8,128)S(1)}, u32[]{:S(2)}, u32[]{:S(2)}) collective-permute-start(f32[2,960,128]{2,1,0:T(8,128)S(1)} %get-tuple-element.98), channel_id=1, source_target_pairs={{24,0},{0,8},{8,16},{16,24},{56,32},{32,40},{40,48},{48,56},{88,64... | collective-permute-start | bytes 2949128 | tf_op jit(solution)/shard_map/ppermute | solution.py:98
  107.8 1.3 collective-permute-start.21
  109.1 4.5 %collective-permute-start.24 = (f32[384,128]{1,0:T(8,128)S(1)}, f32[384,128]{1,0:T(8,128)S(1)}, u32[]{:S(2)}, u32[]{:S(2)}) collective-permute-start(f32[384,128]{1,0:T(8,128)S(1)} %add_add_fusion.1), channel_id=1, source_target_pairs={{160,128},{168,136},{176,144},{184,152},{0,224},{8,232},{16,240},{... | collective-permute-start | bytes 589832 | tf_op jit(solution)/shard_map/ppermute | solution.py:98
  113.6 7.1 %collective-permute-done.26.refs_6_ = f32[2,384,128]{2,1,0:T(8,128)} collective-permute-done((f32[2,384,128]{2,1,0:T(8,128)S(1)}, f32[2,384,128]{2,1,0:T(8,128)}, u32[]{:S(2)}, u32[]{:S(2)}) %collective-permute-start.26) | collective-permute-done | bytes 393248 | tf_op jit(solution)/shard_map/ppermute | solution.py:98
  121.4 2.0 %collective-permute-start.32 = (f32[2,384,128]{2,1,0:T(8,128)}, f32[2,384,128]{2,1,0:T(8,128)}, u32[]{:S(2)}, u32[]{:S(2)}) collective-permute-start(f32[2,384,128]{2,1,0:T(8,128)} %collective-permute-done.26.refs_6_), channel_id=1, source_target_pairs={{224,0},{232,8},{240,16},{248,24},{0,32},{8,40},{16,48},{24,56},{3... | collective-permute-start | bytes 1179656 | tf_op jit(solution)/shard_map/ppermute | solution.py:98
  123.5 0.9 fusion.14
  124.5 3.2 %collective-permute-start.29 = (f32[2,384,128]{2,1,0:T(8,128)}, f32[2,384,128]{2,1,0:T(8,128)}, u32[]{:S(2)}, u32[]{:S(2)}) collective-permute-start(f32[2,384,128]{2,1,0:T(8,128)} %get-tuple-element.99), channel_id=1, source_target_pairs={{32,0},{40,8},{48,16},{56,24},{64,32},{72,40},{80,48},{88,56},{96,... | collective-permute-start | bytes 1179656 | tf_op jit(solution)/shard_map/ppermute | solution.py:98
  127.7 3.9 %shard_map.18 = (f32[256,256]{1,0:T(8,128)}, f32[128,256]{1,0:T(8,128)}) custom-call(s32[2]{0:T(128)} %pad_add_fusion.where_ref.place_ref, f32[8,128,256]{2,1,0:T(8,128)} %bitcast.67, f32[384,128]{1,0:T(8,128)} %add_add_fusion.f_ref), custom_call_target="tpu_custom_call" | custom-call | flops 4000000000 | bytes 1048576 | tf_op jit(solution)/shard_map/pallas_call | solution.py:274
  131.6 5.8 %shard_map.19.refs_4_ = f32[12288,128]{1,0:T(8,128)} custom-call(s32[2]{0:T(128)} %pad_add_fusion.where_ref.place_ref, f32[12288,128]{1,0:T(8,128)} %bitcast.61, f32[256,256]{1,0:T(8,128)} %get-tuple-element.91.m_ref, f32[128,256]{1,0:T(8,128)} %get-tuple-element.92.s_ref, f32[2,384,128]{2,1,0:T(8,128)} %copy-done.3, f32[2,384,128]{2,1,0:T(8,128)} %copy-done.1, ...), custom_call_target="tpu_custom_call" | custom-call | flops 704643072 | bytes 8257536 | tf_op jit(solution)/shard_map/pallas_call | solution.py:359
  137.4 5.8 %shard_map.20.refs_2_ = f32[12288,128]{1,0:T(8,128)} custom-call(s32[2]{0:T(128)} %pad_add_fusion.where_ref.place_ref, f32[12288,128]{1,0:T(8,128)} %bitcast.62, f32[256,256]{1,0:T(8,128)} %get-tuple-element.91.m_ref, f32[128,256]{1,0:T(8,128)} %get-tuple-element.92.s_ref, f32[2,960,128]{2,1,0:T(8,128)} %copy-done, ...), custom_call_target="tpu_custom_call", output_to_operand_aliasing={{}: (8, {})} | custom-call | flops 704643072 | bytes 8257536 | tf_op jit(solution)/shard_map/pallas_call | solution.py:359
  143.3 3.6 %shard_map.21 = f32[12288,128]{1,0:T(8,128)} custom-call(s32[2]{0:T(128)} %pad_add_fusion.where_ref.place_ref, f32[12288,128]{1,0:T(8,128)} %bitcast.63, f32[256,256]{1,0:T(8,128)} %get-tuple-element.91.m_ref, f32[128,256]{1,0:T(8,128)} %get-tuple-element.92.s_ref, f32[2,384,128]{2,1,0:T(8,128)} %collective-permute-done.29.refs_0_, ...), custom_call_target="tpu_custom_call", output_to_operand_aliasing={{}: (6, {})} | custom-call | flops 201326592 | bytes 2359296 | tf_op jit(solution)/shard_map/pallas_call | solution.py:359
  (86 shorter events, 10.8 us)
Async XLA Ops:
  6.5 121.1 %all-gather.3.cloned.1.call-start = ((), (), s32[]{:S(2)}) async-start(), calls=%async_computation | async-start | bytes 1179648 | tf_op jit(solution)/shard_map/all_gather | solution.py:391
  8.6 9.3 %collective-permute-start.1 = (f32[256,128]{1,0:T(8,128)S(1)}, f32[256,128]{1,0:T(8,128)S(1)}, u32[]{:S(2)}, u32[]{:S(2)}) collective-permute-start(f32[256,128]{1,0:T(8,128)S(1)} %maximum_select_fusion), channel_id=1, source_target_pairs={{0,160},{1,161},{8,168},{9,169}} | collective-permute-start | bytes 393224 | tf_op jit(solution)/shard_map/ppermute | solution.py:98
  15.2 27.0 %collective-permute-start.3 = (f32[4,384,128]{2,1,0:T(8,128)}, f32[4,384,128]{2,1,0:T(8,128)S(1)}, u32[]{:S(2)}, u32[]{:S(2)}) collective-permute-start(f32[4,384,128]{2,1,0:T(8,128)} %get-tuple-element.61), channel_id=1, source_target_pairs={{0,24},{8,16},{1,25},{9,17},{2,26},{10,18},{3,27},{11,19},{4,28},{... | collective-permute-start | bytes 2359304 | tf_op jit(solution)/shard_map/ppermute | solution.py:98
  16.5 25.7 %collective-permute-start.4 = (f32[4,384,128]{2,1,0:T(8,128)}, f32[4,384,128]{2,1,0:T(8,128)S(1)}, u32[]{:S(2)}, u32[]{:S(2)}) collective-permute-start(f32[4,384,128]{2,1,0:T(8,128)} %get-tuple-element.62), channel_id=1, source_target_pairs={{0,64},{8,72},{1,65},{9,73},{2,66},{10,74},{3,67},{11,75},{4,68},{... | collective-permute-start | bytes 2359304 | tf_op jit(solution)/shard_map/ppermute | solution.py:98
  17.2 24.9 %collective-permute-start.5 = (f32[4,384,128]{2,1,0:T(8,128)}, f32[4,384,128]{2,1,0:T(8,128)S(1)}, u32[]{:S(2)}, u32[]{:S(2)}) collective-permute-start(f32[4,384,128]{2,1,0:T(8,128)} %get-tuple-element.63), channel_id=1, source_target_pairs={{0,192},{8,200},{1,193},{9,201},{2,194},{10,202},{3,195},{11,203},... | collective-permute-start | bytes 2359304 | tf_op jit(solution)/shard_map/ppermute | solution.py:98
  17.9 0.7 collective-permute-start.2
  44.4 18.3 %collective-permute-start.12 = (f32[384,128]{1,0:T(8,128)S(1)}, f32[384,128]{1,0:T(8,128)S(1)}, u32[]{:S(2)}, u32[]{:S(2)}) collective-permute-start(f32[384,128]{1,0:T(8,128)S(1)} %get-tuple-element.72), channel_id=1, source_target_pairs={{0,88},{8,136},{16,144},{24,168},{64,40},{72,216},{192,32},{200,12... | collective-permute-start | bytes 589832 | tf_op jit(solution)/shard_map/ppermute | solution.py:98
  57.5 6.6 %collective-permute-start.15 = (f32[384,128]{1,0:T(8,128)S(1)}, f32[384,128]{1,0:T(8,128)S(1)}, u32[]{:S(2)}, u32[]{:S(2)}) collective-permute-start(f32[384,128]{1,0:T(8,128)S(1)} %get-tuple-element.75), channel_id=1, source_target_pairs={{0,16},{8,64},{16,48},{24,240},{64,208},{72,112},{192,224},{200,40... | collective-permute-start | bytes 589832 | tf_op jit(solution)/shard_map/ppermute | solution.py:98
  58.8 7.2 %collective-permute-start.6 = (f32[384,128]{1,0:T(8,128)S(1)}, f32[384,128]{1,0:T(8,128)S(1)}, u32[]{:S(2)}, u32[]{:S(2)}) collective-permute-start(f32[384,128]{1,0:T(8,128)S(1)} %get-tuple-element.65), channel_id=1, source_target_pairs={{0,72},{8,80},{16,128},{24,152},{64,120},{72,224},{192,104},{200,2... | collective-permute-start | bytes 589832 | tf_op jit(solution)/shard_map/ppermute | solution.py:98
  60.1 9.5 %collective-permute-start.8 = (f32[384,128]{1,0:T(8,128)S(1)}, f32[384,128]{1,0:T(8,128)S(1)}, u32[]{:S(2)}, u32[]{:S(2)}) collective-permute-start(f32[384,128]{1,0:T(8,128)S(1)} %get-tuple-element.67), channel_id=1, source_target_pairs={{0,216},{8,192},{16,248},{24,136},{64,48},{72,32},{192,112},{200,9... | collective-permute-start | bytes 589832 | tf_op jit(solution)/shard_map/ppermute | solution.py:98
  61.4 8.9 %collective-permute-start.10 = (f32[384,128]{1,0:T(8,128)S(1)}, f32[384,128]{1,0:T(8,128)S(1)}, u32[]{:S(2)}, u32[]{:S(2)}) collective-permute-start(f32[384,128]{1,0:T(8,128)S(1)} %get-tuple-element.69), channel_id=1, source_target_pairs={{0,200},{8,208},{16,0},{24,8},{64,184},{72,176},{192,80},{200,88},... | collective-permute-start | bytes 589832 | tf_op jit(solution)/shard_map/ppermute | solution.py:98
  62.7 10.1 %collective-permute-start.13 = (f32[384,128]{1,0:T(8,128)S(1)}, f32[384,128]{1,0:T(8,128)S(1)}, u32[]{:S(2)}, u32[]{:S(2)}) collective-permute-start(f32[384,128]{1,0:T(8,128)S(1)} %get-tuple-element.73), channel_id=1, source_target_pairs={{0,144},{8,152},{16,104},{24,56},{64,160},{72,168},{192,176},{200,... | collective-permute-start | bytes 589832 | tf_op jit(solution)/shard_map/ppermute | solution.py:98
  64.0 11.7 %collective-permute-start.16 = (f32[384,128]{1,0:T(8,128)S(1)}, f32[384,128]{1,0:T(8,128)S(1)}, u32[]{:S(2)}, u32[]{:S(2)}) collective-permute-start(f32[384,128]{1,0:T(8,128)S(1)} %get-tuple-element.76), channel_id=1, source_target_pairs={{0,128},{8,24},{16,160},{24,96},{64,232},{72,56},{192,248},{200,18... | collective-permute-start | bytes 589832 | tf_op jit(solution)/shard_map/ppermute | solution.py:98
  66.0 9.9 %collective-permute-start.7 = (f32[384,128]{1,0:T(8,128)S(1)}, f32[384,128]{1,0:T(8,128)S(1)}, u32[]{:S(2)}, u32[]{:S(2)}) collective-permute-start(f32[384,128]{1,0:T(8,128)S(1)} %get-tuple-element.116), channel_id=1, source_target_pairs={{160,162},{161,163},{168,170},{169,171}} | collective-permute-start | bytes 589832 | tf_op jit(solution)/shard_map/ppermute | solution.py:98
  69.6 6.3 %collective-permute-start.9 = (f32[384,128]{1,0:T(8,128)S(1)}, f32[384,128]{1,0:T(8,128)S(1)}, u32[]{:S(2)}, u32[]{:S(2)}) collective-permute-start(f32[384,128]{1,0:T(8,128)S(1)} %get-tuple-element.116), channel_id=1, source_target_pairs={{160,166},{161,167},{168,174},{169,175}} | collective-permute-start | bytes 589832 | tf_op jit(solution)/shard_map/ppermute | solution.py:98
  70.3 5.6 %collective-permute-start.11 = (f32[384,128]{1,0:T(8,128)S(1)}, f32[384,128]{1,0:T(8,128)S(1)}, u32[]{:S(2)}, u32[]{:S(2)}) collective-permute-start(f32[384,128]{1,0:T(8,128)S(1)} %get-tuple-element.116), channel_id=1, source_target_pairs={{160,164},{161,165},{168,172},{169,173}} | collective-permute-start | bytes 589832 | tf_op jit(solution)/shard_map/ppermute | solution.py:98
  75.9 9.4 %collective-permute-start.17 = (f32[2,384,128]{2,1,0:T(8,128)S(1)}, f32[2,384,128]{2,1,0:T(8,128)S(1)}, u32[]{:S(2)}, u32[]{:S(2)}) collective-permute-start(f32[2,384,128]{2,1,0:T(8,128)S(1)} %pad_maximum_fusion.3.refs_0_), channel_id=1, source_target_pairs={{32,0},{40,8},{48,16},{56,24},{64,32},{72,40},{80,48},{88,56},{96,... | collective-permute-start | bytes 1179656 | tf_op jit(solution)/shard_map/ppermute | solution.py:98
  76.0 9.3 %collective-permute-start.19 = (f32[2,384,128]{2,1,0:T(8,128)S(1)}, f32[2,384,128]{2,1,0:T(8,128)S(1)}, u32[]{:S(2)}, u32[]{:S(2)}) collective-permute-start(f32[2,384,128]{2,1,0:T(8,128)S(1)} %pad_maximum_fusion.3.refs_0_), channel_id=1, source_target_pairs={{224,0},{232,8},{240,16},{248,24},{0,32},{8,40},{16,48},{24,56},{3... | collective-permute-start | bytes 1179656 | tf_op jit(solution)/shard_map/ppermute | solution.py:98
  79.8 11.6 %collective-permute-start.22 = (f32[2,384,128]{2,1,0:T(8,128)S(1)}, f32[2,384,128]{2,1,0:T(8,128)S(1)}, u32[]{:S(2)}, u32[]{:S(2)}) collective-permute-start(f32[2,384,128]{2,1,0:T(8,128)S(1)} %pad_maximum_fusion.3.refs_0_), channel_id=1, source_target_pairs={{8,0},{16,8},{24,16},{0,24},{40,32},{48,40},{56,48},{32,56},{72,64... | collective-permute-start | bytes 1179656 | tf_op jit(solution)/shard_map/ppermute | solution.py:98
  79.8 11.7 %collective-permute-start.25 = (f32[2,384,128]{2,1,0:T(8,128)S(1)}, f32[2,384,128]{2,1,0:T(8,128)S(1)}, u32[]{:S(2)}, u32[]{:S(2)}) collective-permute-start(f32[2,384,128]{2,1,0:T(8,128)S(1)} %pad_maximum_fusion.3.refs_0_), channel_id=1, source_target_pairs={{24,0},{0,8},{8,16},{16,24},{56,32},{32,40},{40,48},{48,56},{88,64... | collective-permute-start | bytes 1179656 | tf_op jit(solution)/shard_map/ppermute | solution.py:98
  91.7 29.8 %collective-permute-start.27 = (f32[2,960,128]{2,1,0:T(8,128)S(1)}, f32[2,960,128]{2,1,0:T(8,128)S(1)}, u32[]{:S(2)}, u32[]{:S(2)}) collective-permute-start(f32[2,960,128]{2,1,0:T(8,128)S(1)} %get-tuple-element.96), channel_id=1, source_target_pairs={{8,0},{16,8},{24,16},{0,24},{40,32},{48,40},{56,48},{32,56},{72,64... | collective-permute-start | bytes 2949128 | tf_op jit(solution)/shard_map/ppermute | solution.py:98
  91.8 13.1 %collective-permute-start.18 = (f32[384,128]{1,0:T(8,128)S(1)}, f32[384,128]{1,0:T(8,128)S(1)}, u32[]{:S(2)}, u32[]{:S(2)}) collective-permute-start(f32[384,128]{1,0:T(8,128)S(1)} %add.94), channel_id=1, source_target_pairs={{160,0},{168,8},{176,16},{184,24},{161,1},{169,9},{177,17},{185,25... | collective-permute-start | bytes 589832 | tf_op jit(solution)/shard_map/ppermute | solution.py:98
  93.1 14.7 %collective-permute-start.20 = (f32[384,128]{1,0:T(8,128)S(1)}, f32[384,128]{1,0:T(8,128)S(1)}, u32[]{:S(2)}, u32[]{:S(2)}) collective-permute-start(f32[384,128]{1,0:T(8,128)S(1)} %add.94), channel_id=1, source_target_pairs={{160,64},{168,72},{176,80},{184,88},{161,65},{169,73},{177,81},{18... | collective-permute-start | bytes 589832 | tf_op jit(solution)/shard_map/ppermute | solution.py:98
  93.7 15.3 %collective-permute-start.23 = (f32[2,384,128]{2,1,0:T(8,128)S(1)}, f32[2,384,128]{2,1,0:T(8,128)}, u32[]{:S(2)}, u32[]{:S(2)}) collective-permute-start(f32[2,384,128]{2,1,0:T(8,128)S(1)} %collective-permute-done.17.refs_1_), channel_id=1, source_target_pairs={{32,0},{40,8},{48,16},{56,24},{64,32},{72,40},{80,48},{88,56},{96,... | collective-permute-start | bytes 1179656 | tf_op jit(solution)/shard_map/ppermute | solution.py:98
  104.8 19.7 %collective-permute-start.28 = (f32[2,960,128]{2,1,0:T(8,128)S(1)}, f32[2,960,128]{2,1,0:T(8,128)S(1)}, u32[]{:S(2)}, u32[]{:S(2)}) collective-permute-start(f32[2,960,128]{2,1,0:T(8,128)S(1)} %get-tuple-element.98), channel_id=1, source_target_pairs={{24,0},{0,8},{8,16},{16,24},{56,32},{32,40},{40,48},{48,56},{88,64... | collective-permute-start | bytes 2949128 | tf_op jit(solution)/shard_map/ppermute | solution.py:98
  107.7 13.0 %collective-permute-start.26 = (f32[2,384,128]{2,1,0:T(8,128)S(1)}, f32[2,384,128]{2,1,0:T(8,128)}, u32[]{:S(2)}, u32[]{:S(2)}) collective-permute-start(f32[2,384,128]{2,1,0:T(8,128)S(1)} %collective-permute-done.19.refs_2_), channel_id=1, source_target_pairs={{224,0},{232,8},{240,16},{248,24},{0,32},{8,40},{16,48},{24,56},{3... | collective-permute-start | bytes 1179656 | tf_op jit(solution)/shard_map/ppermute | solution.py:98
  107.8 13.0 %collective-permute-start.21 = (f32[384,128]{1,0:T(8,128)S(1)}, f32[384,128]{1,0:T(8,128)S(1)}, u32[]{:S(2)}, u32[]{:S(2)}) collective-permute-start(f32[384,128]{1,0:T(8,128)S(1)} %add_add_fusion.1), channel_id=1, source_target_pairs={{160,192},{168,200},{176,208},{184,216},{0,32},{8,40},{16,48},{24,... | collective-permute-start | bytes 589832 | tf_op jit(solution)/shard_map/ppermute | solution.py:98
  109.1 11.6 %collective-permute-start.24 = (f32[384,128]{1,0:T(8,128)S(1)}, f32[384,128]{1,0:T(8,128)S(1)}, u32[]{:S(2)}, u32[]{:S(2)}) collective-permute-start(f32[384,128]{1,0:T(8,128)S(1)} %add_add_fusion.1), channel_id=1, source_target_pairs={{160,128},{168,136},{176,144},{184,152},{0,224},{8,232},{16,240},{... | collective-permute-start | bytes 589832 | tf_op jit(solution)/shard_map/ppermute | solution.py:98
  120.7 16.7 %collective-permute-start.31 = (f32[2,384,128]{2,1,0:T(8,128)}, f32[2,384,128]{2,1,0:T(8,128)}, u32[]{:S(2)}, u32[]{:S(2)}) collective-permute-start(f32[2,384,128]{2,1,0:T(8,128)} %collective-permute-done.23.refs_5_), channel_id=1, source_target_pairs={{32,0},{40,8},{48,16},{56,24},{64,32},{72,40},{80,48},{88,56},{96,... | collective-permute-start | bytes 1179656 | tf_op jit(solution)/shard_map/ppermute | solution.py:98
  121.4 16.0 %collective-permute-start.32 = (f32[2,384,128]{2,1,0:T(8,128)}, f32[2,384,128]{2,1,0:T(8,128)}, u32[]{:S(2)}, u32[]{:S(2)}) collective-permute-start(f32[2,384,128]{2,1,0:T(8,128)} %collective-permute-done.26.refs_6_), channel_id=1, source_target_pairs={{224,0},{232,8},{240,16},{248,24},{0,32},{8,40},{16,48},{24,56},{3... | collective-permute-start | bytes 1179656 | tf_op jit(solution)/shard_map/ppermute | solution.py:98
  124.4 18.9 %collective-permute-start.30 = (f32[2,384,128]{2,1,0:T(8,128)}, f32[2,384,128]{2,1,0:T(8,128)}, u32[]{:S(2)}, u32[]{:S(2)}) collective-permute-start(f32[2,384,128]{2,1,0:T(8,128)} %get-tuple-element.100), channel_id=1, source_target_pairs={{224,0},{232,8},{240,16},{248,24},{0,32},{8,40},{16,48},{24,56},{3... | collective-permute-start | bytes 1179656 | tf_op jit(solution)/shard_map/ppermute | solution.py:98
  124.5 18.8 %collective-permute-start.29 = (f32[2,384,128]{2,1,0:T(8,128)}, f32[2,384,128]{2,1,0:T(8,128)}, u32[]{:S(2)}, u32[]{:S(2)}) collective-permute-start(f32[2,384,128]{2,1,0:T(8,128)} %get-tuple-element.99), channel_id=1, source_target_pairs={{32,0},{40,8},{48,16},{56,24},{64,32},{72,40},{80,48},{88,56},{96,... | collective-permute-start | bytes 1179656 | tf_op jit(solution)/shard_map/ppermute | solution.py:98
  (12 other events, 256.5 us)
Sparse Core Ops, SparseCore 0:
  66.1 24.9 all-gather.2

commit v3 on v2

--- a/solution.py
+++ b/solution.py
@@ -393,13 +393,13 @@
 
     north, south = send(mine, shift(1, 0)), send(mine, shift(-1, 0))
     east, west = send(mine, shift(0, 1)), send(mine, shift(0, -1))
-    factor = share_far(send, factor)
     north, south, east, west = north[0], south[0], east[0], west[0]
     north2, south2 = send(north, shift(1, 0)), send(south, shift(-1, 0))
+    factor = share_far(send, factor)
     east2 = send(jnp.concatenate([north, south, east[:, :half]], axis=1), shift(0, 1))
     west2 = send(jnp.concatenate([north, south, west[:, half:]], axis=1), shift(0, -1))
+    factor, north2, south2 = tie(factor, north2[0], south2[0])
     factor = share_near(send, factor, col)
-    north2, south2 = north2[0], south2[0]
     north3, south3 = send(north2, shift(1, 0)), send(south2, shift(-1, 0))
     m, special = combine(heads, factor, where)
     east2 = east2[0]
@@ -408,14 +408,13 @@
     def whole_piece(array):
         return ((array, 0, rows),)
 
-    keys = [(0, 0), (1, 0), (-1, 0), (0, 1), (0, -1), (2, 0), (-2, 0)]
-    parts = [whole_piece(v) for v in (mine, north, south, east, west, north2, south2)]
+    west2, north3, south3 = west2[0], north3[0], south3[0]
+    keys = [(0, 0), (1, 0), (-1, 0), (0, 1), (0, -1), (2, 0), (-2, 0), (3, 0), (-3, 0)]
+    keys += [(1, 1), (-1, 1), (1, -1), (-1, -1), (0, 2)]
+    parts = [whole_piece(v) for v in (mine, north, south, east, west, north2, south2, north3, south3)]
+    parts += [((v, k * rows, rows),) for v in (east2, west2) for k in (0, 1)]
+    parts += [((east2, 2 * rows, half), (west2, 2 * rows, half))]
     out = update(x, m, special, parts, keys, where, rows)
-    west2, north3, south3 = west2[0], north3[0], south3[0]
-    keys = [(1, 1), (-1, 1), (1, -1), (-1, -1), (0, 2), (3, 0), (-3, 0)]
-    parts = [((v, k * rows, rows),) for v in (east2, west2) for k in (0, 1)]
-    parts += [((east2, 2 * rows, half), (west2, 2 * rows, half)), whole_piece(north3), whole_piece(south3)]
-    out = update(x, m, special, parts, keys, where, rows, out)
     parts = [whole_piece(corner0[0]), whole_piece(corner1[0])]
     out = update(x, m, special, parts, [(2, 1), (-2, 1)], where, rows, out)
     return out.reshape(slab.shape)

time: 154 us -> 150 us (0.974)
  the two profiles are of different devices: /device:TPU:24 before, /device:TPU:96 now
where the time goes in v3:
time: 150 us; the launch traced here: 149 us
  waiting for transfers between devices  63 us (42%)
  starting transfers between devices  41.1 us (27%)
  Pallas kernels  21.9 us (15%)
  between operations  14 us (9%)
  other arithmetic  4.85 us (3%)
  local copies, waits for them, and re-layouts  4.51 us (3%)
    ppermute x33, waiting for transfers between devices, __call__(): result = [lax.ppermute(value, axis, pairs)]  63 us
    ppermute x33, starting transfers between devices, __call__(): result = [lax.ppermute(value, axis, pairs)]  41.1 us
    pallas_call x2, Pallas kernels, update(): pl.pallas_call(functools.partial(update_kernel, parts, keys, rows, out is...  12.7 us
    pallas_call x1, Pallas kernels, extract(): pl.pallas_call(functools.partial(extract_kernel, rows), out_shape=(jax.Sh...  5.25 us
    pallas_call x1, Pallas kernels, combine(): pl.pallas_call(combine_kernel, out_shape=(jax.ShapeDtypeStruct((256, 256)...  3.94 us
  transfers between devices with their start and end apart: 34, of which 7 were waited for; matrix products, arithmetic and copies ran while one was open for 3% of the time, Pallas kernels for 12%

profile of v3, /device:TPU:96, one launch (start us, length us, event | category | flops | bytes accessed | tf_op | source)
XLA Modules:
  0.0 149.3 jit_solution(1872994447164740478)
XLA Ops:
  6.5 1.3 slice_reduce_fusion
  9.9 5.2 %shard_map.17 = (f32[4,384,128]{2,1,0:T(8,128)}, f32[4,384,128]{2,1,0:T(8,128)}, f32[4,384,128]{2,1,0:T(8,128)}, f32[4,384,128]{2,1,0:T(8,128)}) custom-call(s32[2]{0:T(128)} %pad_add_fusion.where_ref.place_ref, f32[12288,128]{1,0:T(8,128)} %bitcast.60), custom_call_target="tpu_custom_call" | custom-call | bytes 9437184 | tf_op jit(solution)/shard_map/pallas_call | solution.py:78
  15.2 0.7 collective-permute-start.3
  15.9 0.7 collective-permute-start.4
  16.6 0.7 collective-permute-start.5
  18.1 0.7 pad_maximum_fusion.4
  18.9 0.9 copy-done.9
  20.3 1.3 add_select_fusion
  21.6 0.7 collective-permute-start.12
  22.4 0.7 collective-permute-start.14
  23.7 1.3 collective-permute-start.8
  26.4 1.3 collective-permute-start.15
  28.4 33.0 %collective-permute-done.8 = f32[384,128]{1,0:T(8,128)S(1)} collective-permute-done((f32[384,128]{1,0:T(8,128)S(1)}, f32[384,128]{1,0:T(8,128)S(1)}, u32[]{:S(2)}, u32[]{:S(2)}) %collective-permute-start.8) | collective-permute-done | bytes 196640 | tf_op jit(solution)/shard_map/ppermute | solution.py:98
  61.4 15.8 %collective-permute-done.15 = f32[384,128]{1,0:T(8,128)S(1)} collective-permute-done((f32[384,128]{1,0:T(8,128)S(1)}, f32[384,128]{1,0:T(8,128)S(1)}, u32[]{:S(2)}, u32[]{:S(2)}) %collective-permute-start.15) | collective-permute-done | bytes 196640 | tf_op jit(solution)/shard_map/ppermute | solution.py:98
  79.5 2.9 %collective-permute-start.16 = (f32[2,384,128]{2,1,0:T(8,128)S(1)}, f32[2,384,128]{2,1,0:T(8,128)S(1)}, u32[]{:S(2)}, u32[]{:S(2)}) collective-permute-start(f32[2,384,128]{2,1,0:T(8,128)S(1)} %pad_maximum_fusion.3.refs_0_), channel_id=1, source_target_pairs={{224,0},{232,8},{240,16},{248,24},{0,32},{8,40},{16,48},{24,56},{3... | collective-permute-start | bytes 1179656 | tf_op jit(solution)/shard_map/ppermute | solution.py:98
  82.3 2.0 %collective-permute-start.20 = (f32[2,384,128]{2,1,0:T(8,128)S(1)}, f32[2,384,128]{2,1,0:T(8,128)S(1)}, u32[]{:S(2)}, u32[]{:S(2)}) collective-permute-start(f32[2,384,128]{2,1,0:T(8,128)S(1)} %pad_maximum_fusion.3.refs_0_), channel_id=1, source_target_pairs={{24,0},{0,8},{8,16},{16,24},{56,32},{32,40},{40,48},{48,56},{88,64... | collective-permute-start | bytes 1179656 | tf_op jit(solution)/shard_map/ppermute | solution.py:98
  84.4 2.7 %collective-permute-done.22.refs_1_ = f32[2,384,128]{2,1,0:T(8,128)S(1)} collective-permute-done((f32[2,384,128]{2,1,0:T(8,128)S(1)}, f32[2,384,128]{2,1,0:T(8,128)S(1)}, u32[]{:S(2)}, u32[]{:S(2)}) %collective-permute-start.22) | collective-permute-done | bytes 393248 | tf_op jit(solution)/shard_map/ppermute | solution.py:98
  87.1 1.1 add_add_fusion.2
  89.0 3.1 %collective-permute-start.24 = (f32[2,384,128]{2,1,0:T(8,128)S(1)}, f32[2,384,128]{2,1,0:T(8,128)}, u32[]{:S(2)}, u32[]{:S(2)}) collective-permute-start(f32[2,384,128]{2,1,0:T(8,128)S(1)} %collective-permute-done.16.refs_2_), channel_id=1, source_target_pairs={{224,0},{232,8},{240,16},{248,24},{0,32},{8,40},{16,48},{24,56},{3... | collective-permute-start | bytes 1179656 | tf_op jit(solution)/shard_map/ppermute | solution.py:98
  92.3 3.9 %collective-permute-done.23.refs_5_ = f32[2,384,128]{2,1,0:T(8,128)} collective-permute-done((f32[2,384,128]{2,1,0:T(8,128)S(1)}, f32[2,384,128]{2,1,0:T(8,128)}, u32[]{:S(2)}, u32[]{:S(2)}) %collective-permute-start.23) | collective-permute-done | bytes 393248 | tf_op jit(solution)/shard_map/ppermute | solution.py:98
  96.2 1.2 collective-permute-start.27
  98.8 0.9 collective-permute-start.28
  99.7 1.3 collective-permute-start.25
  101.7 12.8 %collective-permute-start.31 = (f32[2,384,128]{2,1,0:T(8,128)}, f32[2,384,128]{2,1,0:T(8,128)}, u32[]{:S(2)}, u32[]{:S(2)}) collective-permute-start(f32[2,384,128]{2,1,0:T(8,128)} %collective-permute-done.23.refs_5_), channel_id=1, source_target_pairs={{32,0},{40,8},{48,16},{56,24},{64,32},{72,40},{80,48},{88,56},{96,... | collective-permute-start | bytes 1179656 | tf_op jit(solution)/shard_map/ppermute | solution.py:98
  114.6 4.9 %collective-permute-done.25 = f32[384,128]{1,0:T(8,128)S(1)} collective-permute-done((f32[384,128]{1,0:T(8,128)S(1)}, f32[384,128]{1,0:T(8,128)S(1)}, u32[]{:S(2)}, u32[]{:S(2)}) %collective-permute-start.25) | collective-permute-done | bytes 196640 | tf_op jit(solution)/shard_map/ppermute | solution.py:98
  119.4 0.7 add_add_fusion.f_ref
  120.1 1.0 fusion.14
  121.2 2.0 %collective-permute-start.29 = (f32[2,384,128]{2,1,0:T(8,128)}, f32[2,384,128]{2,1,0:T(8,128)}, u32[]{:S(2)}, u32[]{:S(2)}) collective-permute-start(f32[2,384,128]{2,1,0:T(8,128)} %get-tuple-element.103), channel_id=1, source_target_pairs={{32,0},{40,8},{48,16},{56,24},{64,32},{72,40},{80,48},{88,56},{96,... | collective-permute-start | bytes 1179656 | tf_op jit(solution)/shard_map/ppermute | solution.py:98
  123.2 3.9 %shard_map.18 = (f32[256,256]{1,0:T(8,128)}, f32[128,256]{1,0:T(8,128)}) custom-call(s32[2]{0:T(128)} %pad_add_fusion.where_ref.place_ref, f32[8,128,256]{2,1,0:T(8,128)} %bitcast.66, f32[384,128]{1,0:T(8,128)} %add_add_fusion.f_ref), custom_call_target="tpu_custom_call" | custom-call | flops 4000000000 | bytes 1048576 | tf_op jit(solution)/shard_map/pallas_call | solution.py:274
  127.2 2.6 %collective-permute-done.32.refs_8_ = f32[2,384,128]{2,1,0:T(8,128)} collective-permute-done((f32[2,384,128]{2,1,0:T(8,128)}, f32[2,384,128]{2,1,0:T(8,128)}, u32[]{:S(2)}, u32[]{:S(2)}) %collective-permute-start.32) | collective-permute-done | bytes 393248 | tf_op jit(solution)/shard_map/ppermute | solution.py:98
  129.8 9.1 %shard_map.19.refs_2_ = f32[12288,128]{1,0:T(8,128)} custom-call(s32[2]{0:T(128)} %pad_add_fusion.where_ref.place_ref, f32[12288,128]{1,0:T(8,128)} %bitcast.61, f32[256,256]{1,0:T(8,128)} %get-tuple-element.97.m_ref, f32[128,256]{1,0:T(8,128)} %get-tuple-element.98.s_ref, f32[2,384,128]{2,1,0:T(8,128)} %copy-done.3, f32[2,384,128]{2,1,0:T(8,128)} %copy-done.1, ...), custom_call_target="tpu_custom_call" | custom-call | flops 1409286144 | bytes 16515072 | tf_op jit(solution)/shard_map/pallas_call | solution.py:359
  138.8 3.6 %shard_map.20 = f32[12288,128]{1,0:T(8,128)} custom-call(s32[2]{0:T(128)} %pad_add_fusion.where_ref.place_ref, f32[12288,128]{1,0:T(8,128)} %bitcast.62, f32[256,256]{1,0:T(8,128)} %get-tuple-element.97.m_ref, f32[128,256]{1,0:T(8,128)} %get-tuple-element.98.s_ref, f32[2,384,128]{2,1,0:T(8,128)} %collective-permute-done.29.refs_0_, ...), custom_call_target="tpu_custom_call", output_to_operand_aliasing={{}: (6, {})} | custom-call | flops 201326592 | bytes 2359296 | tf_op jit(solution)/shard_map/pallas_call | solution.py:359
  (87 shorter events, 11.4 us)
Async XLA Ops:
  6.5 116.7 %all-gather.3.cloned.1.call-start = ((), (), s32[]{:S(2)}) async-start(), calls=%async_computation | async-start | bytes 1179648 | tf_op jit(solution)/shard_map/all_gather | solution.py:391
  8.6 8.7 %collective-permute-start.1 = (f32[256,128]{1,0:T(8,128)S(1)}, f32[256,128]{1,0:T(8,128)S(1)}, u32[]{:S(2)}, u32[]{:S(2)}) collective-permute-start(f32[256,128]{1,0:T(8,128)S(1)} %maximum_select_fusion), channel_id=1, source_target_pairs={{0,160},{1,161},{8,168},{9,169}} | collective-permute-start | bytes 393224 | tf_op jit(solution)/shard_map/ppermute | solution.py:98
  15.2 3.7 %collective-permute-start.3 = (f32[4,384,128]{2,1,0:T(8,128)}, f32[4,384,128]{2,1,0:T(8,128)S(1)}, u32[]{:S(2)}, u32[]{:S(2)}) collective-permute-start(f32[4,384,128]{2,1,0:T(8,128)} %get-tuple-element.63), channel_id=1, source_target_pairs={{0,24},{8,16},{1,25},{9,17},{2,26},{10,18},{3,27},{11,19},{4,28},{... | collective-permute-start | bytes 2359304 | tf_op jit(solution)/shard_map/ppermute | solution.py:98
  15.9 3.0 %collective-permute-start.4 = (f32[4,384,128]{2,1,0:T(8,128)}, f32[4,384,128]{2,1,0:T(8,128)S(1)}, u32[]{:S(2)}, u32[]{:S(2)}) collective-permute-start(f32[4,384,128]{2,1,0:T(8,128)} %get-tuple-element.64), channel_id=1, source_target_pairs={{0,64},{8,72},{1,65},{9,73},{2,66},{10,74},{3,67},{11,75},{4,68},{... | collective-permute-start | bytes 2359304 | tf_op jit(solution)/shard_map/ppermute | solution.py:98
  16.6 2.3 %collective-permute-start.5 = (f32[4,384,128]{2,1,0:T(8,128)}, f32[4,384,128]{2,1,0:T(8,128)S(1)}, u32[]{:S(2)}, u32[]{:S(2)}) collective-permute-start(f32[4,384,128]{2,1,0:T(8,128)} %get-tuple-element.65), channel_id=1, source_target_pairs={{0,192},{8,200},{1,193},{9,201},{2,194},{10,202},{3,195},{11,203},... | collective-permute-start | bytes 2359304 | tf_op jit(solution)/shard_map/ppermute | solution.py:98
  21.6 4.1 %collective-permute-start.12 = (f32[384,128]{1,0:T(8,128)S(1)}, f32[384,128]{1,0:T(8,128)S(1)}, u32[]{:S(2)}, u32[]{:S(2)}) collective-permute-start(f32[384,128]{1,0:T(8,128)S(1)} %get-tuple-element.74), channel_id=1, source_target_pairs={{0,88},{8,136},{16,144},{24,168},{64,40},{72,216},{192,32},{200,12... | collective-permute-start | bytes 589832 | tf_op jit(solution)/shard_map/ppermute | solution.py:98
  22.4 4.0 %collective-permute-start.14 = (f32[384,128]{1,0:T(8,128)S(1)}, f32[384,128]{1,0:T(8,128)S(1)}, u32[]{:S(2)}, u32[]{:S(2)}) collective-permute-start(f32[384,128]{1,0:T(8,128)S(1)} %get-tuple-element.76), channel_id=1, source_target_pairs={{0,16},{8,64},{16,48},{24,240},{64,208},{72,112},{192,224},{200,40... | collective-permute-start | bytes 589832 | tf_op jit(solution)/shard_map/ppermute | solution.py:98
  23.0 4.7 %collective-permute-start.6 = (f32[384,128]{1,0:T(8,128)S(1)}, f32[384,128]{1,0:T(8,128)S(1)}, u32[]{:S(2)}, u32[]{:S(2)}) collective-permute-start(f32[384,128]{1,0:T(8,128)S(1)} %get-tuple-element.67), channel_id=1, source_target_pairs={{0,72},{8,80},{16,128},{24,152},{64,120},{72,224},{192,104},{200,2... | collective-permute-start | bytes 589832 | tf_op jit(solution)/shard_map/ppermute | solution.py:98
  23.7 37.7 %collective-permute-start.8 = (f32[384,128]{1,0:T(8,128)S(1)}, f32[384,128]{1,0:T(8,128)S(1)}, u32[]{:S(2)}, u32[]{:S(2)}) collective-permute-start(f32[384,128]{1,0:T(8,128)S(1)} %get-tuple-element.69), channel_id=1, source_target_pairs={{0,216},{8,192},{16,248},{24,136},{64,48},{72,32},{192,112},{200,9... | collective-permute-start | bytes 589832 | tf_op jit(solution)/shard_map/ppermute | solution.py:98
  25.0 36.4 %collective-permute-start.10 = (f32[384,128]{1,0:T(8,128)S(1)}, f32[384,128]{1,0:T(8,128)S(1)}, u32[]{:S(2)}, u32[]{:S(2)}) collective-permute-start(f32[384,128]{1,0:T(8,128)S(1)} %get-tuple-element.71), channel_id=1, source_target_pairs={{0,200},{8,208},{16,0},{24,8},{64,184},{72,176},{192,80},{200,88},... | collective-permute-start | bytes 589832 | tf_op jit(solution)/shard_map/ppermute | solution.py:98
  25.7 35.7 %collective-permute-start.13 = (f32[384,128]{1,0:T(8,128)S(1)}, f32[384,128]{1,0:T(8,128)S(1)}, u32[]{:S(2)}, u32[]{:S(2)}) collective-permute-start(f32[384,128]{1,0:T(8,128)S(1)} %get-tuple-element.75), channel_id=1, source_target_pairs={{0,144},{8,152},{16,104},{24,56},{64,160},{72,168},{192,176},{200,... | collective-permute-start | bytes 589832 | tf_op jit(solution)/shard_map/ppermute | solution.py:98
  26.4 50.7 %collective-permute-start.15 = (f32[384,128]{1,0:T(8,128)S(1)}, f32[384,128]{1,0:T(8,128)S(1)}, u32[]{:S(2)}, u32[]{:S(2)}) collective-permute-start(f32[384,128]{1,0:T(8,128)S(1)} %get-tuple-element.77), channel_id=1, source_target_pairs={{0,128},{8,24},{16,160},{24,96},{64,232},{72,56},{192,248},{200,18... | collective-permute-start | bytes 589832 | tf_op jit(solution)/shard_map/ppermute | solution.py:98
  27.7 49.6 %collective-permute-start.7 = (f32[384,128]{1,0:T(8,128)S(1)}, f32[384,128]{1,0:T(8,128)S(1)}, u32[]{:S(2)}, u32[]{:S(2)}) collective-permute-start(f32[384,128]{1,0:T(8,128)S(1)} %get-tuple-element.120), channel_id=1, source_target_pairs={{160,162},{161,163},{168,170},{169,171}} | collective-permute-start | bytes 589832 | tf_op jit(solution)/shard_map/ppermute | solution.py:98
  77.4 9.7 %collective-permute-start.22 = (f32[2,384,128]{2,1,0:T(8,128)S(1)}, f32[2,384,128]{2,1,0:T(8,128)S(1)}, u32[]{:S(2)}, u32[]{:S(2)}) collective-permute-start(f32[2,384,128]{2,1,0:T(8,128)S(1)} %pad_maximum_fusion.3.refs_0_), channel_id=1, source_target_pairs={{32,0},{40,8},{48,16},{56,24},{64,32},{72,40},{80,48},{88,56},{96,... | collective-permute-start | bytes 1179656 | tf_op jit(solution)/shard_map/ppermute | solution.py:98
  78.1 1.4 collective-permute-start.9
  78.8 3.6 %collective-permute-start.11 = (f32[384,128]{1,0:T(8,128)S(1)}, f32[384,128]{1,0:T(8,128)S(1)}, u32[]{:S(2)}, u32[]{:S(2)}) collective-permute-start(f32[384,128]{1,0:T(8,128)S(1)} %get-tuple-element.120), channel_id=1, source_target_pairs={{160,164},{161,165},{168,172},{169,173}} | collective-permute-start | bytes 589832 | tf_op jit(solution)/shard_map/ppermute | solution.py:98
  79.5 8.9 %collective-permute-start.16 = (f32[2,384,128]{2,1,0:T(8,128)S(1)}, f32[2,384,128]{2,1,0:T(8,128)S(1)}, u32[]{:S(2)}, u32[]{:S(2)}) collective-permute-start(f32[2,384,128]{2,1,0:T(8,128)S(1)} %pad_maximum_fusion.3.refs_0_), channel_id=1, source_target_pairs={{224,0},{232,8},{240,16},{248,24},{0,32},{8,40},{16,48},{24,56},{3... | collective-permute-start | bytes 1179656 | tf_op jit(solution)/shard_map/ppermute | solution.py:98
  82.3 9.7 %collective-permute-start.18 = (f32[2,384,128]{2,1,0:T(8,128)S(1)}, f32[2,384,128]{2,1,0:T(8,128)S(1)}, u32[]{:S(2)}, u32[]{:S(2)}) collective-permute-start(f32[2,384,128]{2,1,0:T(8,128)S(1)} %pad_maximum_fusion.3.refs_0_), channel_id=1, source_target_pairs={{8,0},{16,8},{24,16},{0,24},{40,32},{48,40},{56,48},{32,56},{72,64... | collective-permute-start | bytes 1179656 | tf_op jit(solution)/shard_map/ppermute | solution.py:98
  82.3 9.8 %collective-permute-start.20 = (f32[2,384,128]{2,1,0:T(8,128)S(1)}, f32[2,384,128]{2,1,0:T(8,128)S(1)}, u32[]{:S(2)}, u32[]{:S(2)}) collective-permute-start(f32[2,384,128]{2,1,0:T(8,128)S(1)} %pad_maximum_fusion.3.refs_0_), channel_id=1, source_target_pairs={{24,0},{0,8},{8,16},{16,24},{56,32},{32,40},{40,48},{48,56},{88,64... | collective-permute-start | bytes 1179656 | tf_op jit(solution)/shard_map/ppermute | solution.py:98
  87.1 9.1 %collective-permute-start.23 = (f32[2,384,128]{2,1,0:T(8,128)S(1)}, f32[2,384,128]{2,1,0:T(8,128)}, u32[]{:S(2)}, u32[]{:S(2)}) collective-permute-start(f32[2,384,128]{2,1,0:T(8,128)S(1)} %collective-permute-done.22.refs_1_), channel_id=1, source_target_pairs={{32,0},{40,8},{48,16},{56,24},{64,32},{72,40},{80,48},{88,56},{96,... | collective-permute-start | bytes 1179656 | tf_op jit(solution)/shard_map/ppermute | solution.py:98
  88.3 9.0 %collective-permute-start.17 = (f32[384,128]{1,0:T(8,128)S(1)}, f32[384,128]{1,0:T(8,128)S(1)}, u32[]{:S(2)}, u32[]{:S(2)}) collective-permute-start(f32[384,128]{1,0:T(8,128)S(1)} %add_add_fusion.2), channel_id=1, source_target_pairs={{160,184},{168,176},{161,185},{169,177},{162,186},{170,178},{163,1... | collective-permute-start | bytes 589832 | tf_op jit(solution)/shard_map/ppermute | solution.py:98
  89.0 9.8 %collective-permute-start.24 = (f32[2,384,128]{2,1,0:T(8,128)S(1)}, f32[2,384,128]{2,1,0:T(8,128)}, u32[]{:S(2)}, u32[]{:S(2)}) collective-permute-start(f32[2,384,128]{2,1,0:T(8,128)S(1)} %collective-permute-done.16.refs_2_), channel_id=1, source_target_pairs={{224,0},{232,8},{240,16},{248,24},{0,32},{8,40},{16,48},{24,56},{3... | collective-permute-start | bytes 1179656 | tf_op jit(solution)/shard_map/ppermute | solution.py:98
  96.2 24.0 %collective-permute-start.27 = (f32[2,960,128]{2,1,0:T(8,128)S(1)}, f32[2,960,128]{2,1,0:T(8,128)S(1)}, u32[]{:S(2)}, u32[]{:S(2)}) collective-permute-start(f32[2,960,128]{2,1,0:T(8,128)S(1)} %get-tuple-element.100), channel_id=1, source_target_pairs={{8,0},{16,8},{24,16},{0,24},{40,32},{48,40},{56,48},{32,56},{72,64... | collective-permute-start | bytes 2949128 | tf_op jit(solution)/shard_map/ppermute | solution.py:98
  97.4 2.3 %collective-permute-start.19 = (f32[384,128]{1,0:T(8,128)S(1)}, f32[384,128]{1,0:T(8,128)S(1)}, u32[]{:S(2)}, u32[]{:S(2)}) collective-permute-start(f32[384,128]{1,0:T(8,128)S(1)} %add.100), channel_id=1, source_target_pairs={{160,0},{168,8},{176,16},{184,24},{161,1},{169,9},{177,17},{185,25... | collective-permute-start | bytes 589832 | tf_op jit(solution)/shard_map/ppermute | solution.py:98
  98.1 1.6 %collective-permute-start.21 = (f32[384,128]{1,0:T(8,128)S(1)}, f32[384,128]{1,0:T(8,128)S(1)}, u32[]{:S(2)}, u32[]{:S(2)}) collective-permute-start(f32[384,128]{1,0:T(8,128)S(1)} %add.100), channel_id=1, source_target_pairs={{160,64},{168,72},{176,80},{184,88},{161,65},{169,73},{177,81},{18... | collective-permute-start | bytes 589832 | tf_op jit(solution)/shard_map/ppermute | solution.py:98
  98.8 22.4 %collective-permute-start.28 = (f32[2,960,128]{2,1,0:T(8,128)S(1)}, f32[2,960,128]{2,1,0:T(8,128)S(1)}, u32[]{:S(2)}, u32[]{:S(2)}) collective-permute-start(f32[2,960,128]{2,1,0:T(8,128)S(1)} %get-tuple-element.102), channel_id=1, source_target_pairs={{24,0},{0,8},{8,16},{16,24},{56,32},{32,40},{40,48},{48,56},{88,64... | collective-permute-start | bytes 2949128 | tf_op jit(solution)/shard_map/ppermute | solution.py:98
  99.7 19.7 %collective-permute-start.25 = (f32[384,128]{1,0:T(8,128)S(1)}, f32[384,128]{1,0:T(8,128)S(1)}, u32[]{:S(2)}, u32[]{:S(2)}) collective-permute-start(f32[384,128]{1,0:T(8,128)S(1)} %add_add_fusion.1), channel_id=1, source_target_pairs={{160,192},{168,200},{176,208},{184,216},{0,32},{8,40},{16,48},{24,... | collective-permute-start | bytes 589832 | tf_op jit(solution)/shard_map/ppermute | solution.py:98
  101.0 18.4 %collective-permute-start.26 = (f32[384,128]{1,0:T(8,128)S(1)}, f32[384,128]{1,0:T(8,128)S(1)}, u32[]{:S(2)}, u32[]{:S(2)}) collective-permute-start(f32[384,128]{1,0:T(8,128)S(1)} %add_add_fusion.1), channel_id=1, source_target_pairs={{160,128},{168,136},{176,144},{184,152},{0,224},{8,232},{16,240},{... | collective-permute-start | bytes 589832 | tf_op jit(solution)/shard_map/ppermute | solution.py:98
  101.7 25.5 %collective-permute-start.31 = (f32[2,384,128]{2,1,0:T(8,128)}, f32[2,384,128]{2,1,0:T(8,128)}, u32[]{:S(2)}, u32[]{:S(2)}) collective-permute-start(f32[2,384,128]{2,1,0:T(8,128)} %collective-permute-done.23.refs_5_), channel_id=1, source_target_pairs={{32,0},{40,8},{48,16},{56,24},{64,32},{72,40},{80,48},{88,56},{96,... | collective-permute-start | bytes 1179656 | tf_op jit(solution)/shard_map/ppermute | solution.py:98
  120.1 9.6 %collective-permute-start.32 = (f32[2,384,128]{2,1,0:T(8,128)}, f32[2,384,128]{2,1,0:T(8,128)}, u32[]{:S(2)}, u32[]{:S(2)}) collective-permute-start(f32[2,384,128]{2,1,0:T(8,128)} %collective-permute-done.24.refs_6_), channel_id=1, source_target_pairs={{224,0},{232,8},{240,16},{248,24},{0,32},{8,40},{16,48},{24,56},{3... | collective-permute-start | bytes 1179656 | tf_op jit(solution)/shard_map/ppermute | solution.py:98
  121.2 17.7 %collective-permute-start.30 = (f32[2,384,128]{2,1,0:T(8,128)}, f32[2,384,128]{2,1,0:T(8,128)}, u32[]{:S(2)}, u32[]{:S(2)}) collective-permute-start(f32[2,384,128]{2,1,0:T(8,128)} %get-tuple-element.104), channel_id=1, source_target_pairs={{224,0},{232,8},{240,16},{248,24},{0,32},{8,40},{16,48},{24,56},{3... | collective-permute-start | bytes 1179656 | tf_op jit(solution)/shard_map/ppermute | solution.py:98
  121.2 17.7 %collective-permute-start.29 = (f32[2,384,128]{2,1,0:T(8,128)}, f32[2,384,128]{2,1,0:T(8,128)}, u32[]{:S(2)}, u32[]{:S(2)}) collective-permute-start(f32[2,384,128]{2,1,0:T(8,128)} %get-tuple-element.103), channel_id=1, source_target_pairs={{32,0},{40,8},{48,16},{56,24},{64,32},{72,40},{80,48},{88,56},{96,... | collective-permute-start | bytes 1179656 | tf_op jit(solution)/shard_map/ppermute | solution.py:98
  (13 other events, 198.9 us)
Sparse Core Ops, SparseCore 0:
  79.6 22.1 all-gather.2

commit v4 on v3

--- a/solution.py
+++ b/solution.py
@@ -391,6 +391,7 @@
     heads = lax.all_gather(top, "row", axis=0)
     mine, factor = scatter(send, own, got, row, col)
 
+    send = Sender(99)
     north, south = send(mine, shift(1, 0)), send(mine, shift(-1, 0))
     east, west = send(mine, shift(0, 1)), send(mine, shift(0, -1))
     north, south, east, west = north[0], south[0], east[0], west[0]
@@ -408,15 +409,16 @@
     def whole_piece(array):
         return ((array, 0, rows),)
 
-    west2, north3, south3 = west2[0], north3[0], south3[0]
-    keys = [(0, 0), (1, 0), (-1, 0), (0, 1), (0, -1), (2, 0), (-2, 0), (3, 0), (-3, 0)]
-    keys += [(1, 1), (-1, 1), (1, -1), (-1, -1), (0, 2)]
-    parts = [whole_piece(v) for v in (mine, north, south, east, west, north2, south2, north3, south3)]
-    parts += [((v, k * rows, rows),) for v in (east2, west2) for k in (0, 1)]
+    keys = [(0, 0), (1, 0), (-1, 0), (0, 1), (0, -1), (2, 0), (-2, 0), (1, 1), (-1, 1)]
+    parts = [whole_piece(v) for v in (mine, north, south, east, west, north2, south2)]
+    parts += [((east2, k * rows, rows),) for k in (0, 1)]
+    out = update(x, m, special, parts, keys, where, rows)
+    west2 = west2[0]
+    keys = [(1, -1), (-1, -1), (0, 2), (3, 0), (-3, 0), (2, 1), (-2, 1)]
+    parts = [((west2, k * rows, rows),) for k in (0, 1)]
     parts += [((east2, 2 * rows, half), (west2, 2 * rows, half))]
-    out = update(x, m, special, parts, keys, where, rows)
-    parts = [whole_piece(corner0[0]), whole_piece(corner1[0])]
-    out = update(x, m, special, parts, [(2, 1), (-2, 1)], where, rows, out)
+    parts += [whole_piece(v[0]) for v in (north3, south3, corner0, corner1)]
+    out = update(x, m, special, parts, keys, where, rows, out)
     return out.reshape(slab.shape)
 
 

time: 150 us -> 146 us (0.973)
  the two profiles are of different devices: /device:TPU:96 before, /device:TPU:24 now
where the time goes in v4:
time: 146 us; the launch traced here: 143 us
  starting transfers between devices  54.8 us (38%)
  waiting for transfers between devices  45.4 us (31%)
  Pallas kernels  21.6 us (15%)
  between operations  14 us (10%)
  other arithmetic  3.71 us (3%)
  local copies, waits for them, and re-layouts  3.51 us (2%)
    ppermute x33, starting transfers between devices, __call__(): result = [lax.ppermute(value, axis, pairs)]  54.8 us
    ppermute x33, waiting for transfers between devices, __call__(): result = [lax.ppermute(value, axis, pairs)]  45.4 us
    pallas_call x2, Pallas kernels, update(): pl.pallas_call(functools.partial(update_kernel, parts, keys, rows, out is...  12.4 us
    pallas_call x1, Pallas kernels, extract(): pl.pallas_call(functools.partial(extract_kernel, rows), out_shape=(jax.Sh...  5.24 us
    pallas_call x1, Pallas kernels, combine(): pl.pallas_call(combine_kernel, out_shape=(jax.ShapeDtypeStruct((256, 256)...  3.94 us
  transfers between devices with their start and end apart: 34, of which 8 were waited for; matrix products, arithmetic and copies ran while one was open for 3% of the time, Pallas kernels for 11%

profile of v4, /device:TPU:24, one launch (start us, length us, event | category | flops | bytes accessed | tf_op | source)
XLA Modules:
  0.0 143.0 jit_solution(12725555845203009352)
XLA Ops:
  6.5 1.3 slice_reduce_fusion
  9.9 5.2 %shard_map.17 = (f32[4,384,128]{2,1,0:T(8,128)}, f32[4,384,128]{2,1,0:T(8,128)}, f32[4,384,128]{2,1,0:T(8,128)}, f32[4,384,128]{2,1,0:T(8,128)}) custom-call(s32[2]{0:T(128)} %pad_add_fusion.where_ref.place_ref, f32[12288,128]{1,0:T(8,128)} %bitcast.60), custom_call_target="tpu_custom_call" | custom-call | bytes 9437184 | tf_op jit(solution)/shard_map/pallas_call | solution.py:78
  15.1 1.3 collective-permute-start.3
  19.4 22.7 %collective-permute-done.3 = f32[4,384,128]{2,1,0:T(8,128)S(1)} collective-permute-done((f32[4,384,128]{2,1,0:T(8,128)}, f32[4,384,128]{2,1,0:T(8,128)S(1)}, u32[]{:S(2)}, u32[]{:S(2)}) %collective-permute-start.3) | collective-permute-done | bytes 786464 | tf_op jit(solution)/shard_map/ppermute | solution.py:98
  43.0 1.3 add_select_fusion
  44.3 13.1 %collective-permute-start.15 = (f32[384,128]{1,0:T(8,128)S(1)}, f32[384,128]{1,0:T(8,128)S(1)}, u32[]{:S(2)}, u32[]{:S(2)}) collective-permute-start(f32[384,128]{1,0:T(8,128)S(1)} %get-tuple-element.53), channel_id=1, source_target_pairs={{0,88},{8,136},{16,144},{24,168},{64,40},{72,216},{192,32},{200,12... | collective-permute-start | bytes 589832 | tf_op jit(solution)/shard_map/ppermute | solution.py:98
  57.5 1.3 collective-permute-start.17
  58.8 1.3 collective-permute-start.6
  60.1 1.3 collective-permute-start.8
  61.4 1.3 collective-permute-start.10
  62.7 1.3 collective-permute-start.16
  64.0 1.9 %collective-permute-start.18 = (f32[384,128]{1,0:T(8,128)S(1)}, f32[384,128]{1,0:T(8,128)S(1)}, u32[]{:S(2)}, u32[]{:S(2)}) collective-permute-start(f32[384,128]{1,0:T(8,128)S(1)} %get-tuple-element.56), channel_id=1, source_target_pairs={{0,128},{8,24},{16,160},{24,96},{64,232},{72,56},{192,248},{200,18... | collective-permute-start | bytes 589832 | tf_op jit(solution)/shard_map/ppermute | solution.py:98
  66.7 2.9 %collective-permute-done.8 = f32[384,128]{1,0:T(8,128)S(1)} collective-permute-done((f32[384,128]{1,0:T(8,128)S(1)}, f32[384,128]{1,0:T(8,128)S(1)}, u32[]{:S(2)}, u32[]{:S(2)}) %collective-permute-start.8) | collective-permute-done | bytes 196640 | tf_op jit(solution)/shard_map/ppermute | solution.py:98
  71.0 1.8 %collective-permute-done.16 = f32[384,128]{1,0:T(8,128)S(1)} collective-permute-done((f32[384,128]{1,0:T(8,128)S(1)}, f32[384,128]{1,0:T(8,128)S(1)}, u32[]{:S(2)}, u32[]{:S(2)}) %collective-permute-start.16) | collective-permute-done | bytes 196640 | tf_op jit(solution)/shard_map/ppermute | solution.py:98
  72.8 2.1 %collective-permute-done.18 = f32[384,128]{1,0:T(8,128)S(1)} collective-permute-done((f32[384,128]{1,0:T(8,128)S(1)}, f32[384,128]{1,0:T(8,128)S(1)}, u32[]{:S(2)}, u32[]{:S(2)}) %collective-permute-start.18) | collective-permute-done | bytes 196640 | tf_op jit(solution)/shard_map/ppermute | solution.py:98
  75.2 3.2 %collective-permute-start.25 = (f32[2,384,128]{2,1,0:T(8,128)S(1)}, f32[2,384,128]{2,1,0:T(8,128)S(1)}, u32[]{:S(2)}, u32[]{:S(2)}) collective-permute-start(f32[2,384,128]{2,1,0:T(8,128)S(1)} %pad_maximum_fusion.3.refs_0_), channel_id=1, source_target_pairs={{24,0},{0,8},{8,16},{16,24},{56,32},{32,40},{40,48},{48,56},{88,64... | collective-permute-start | bytes 1179656 | tf_op jit(solution)/shard_map/ppermute | solution.py:98
  78.4 3.6 %collective-permute-start.21 = (f32[2,384,128]{2,1,0:T(8,128)S(1)}, f32[2,384,128]{2,1,0:T(8,128)S(1)}, u32[]{:S(2)}, u32[]{:S(2)}) collective-permute-start(f32[2,384,128]{2,1,0:T(8,128)S(1)} %pad_maximum_fusion.3.refs_0_), channel_id=1, source_target_pairs={{224,0},{232,8},{240,16},{248,24},{0,32},{8,40},{16,48},{24,56},{3... | collective-permute-start | bytes 1179656 | tf_op jit(solution)/shard_map/ppermute | solution.py:98
  82.8 1.5 %collective-permute-done.27.refs_3_ = f32[2,384,128]{2,1,0:T(8,128)S(1)} collective-permute-done((f32[2,384,128]{2,1,0:T(8,128)S(1)}, f32[2,384,128]{2,1,0:T(8,128)S(1)}, u32[]{:S(2)}, u32[]{:S(2)}) %collective-permute-start.27) | collective-permute-done | bytes 393248 | tf_op jit(solution)/shard_map/ppermute | solution.py:98
  84.4 3.6 %collective-permute-done.21.refs_2_ = f32[2,384,128]{2,1,0:T(8,128)S(1)} collective-permute-done((f32[2,384,128]{2,1,0:T(8,128)S(1)}, f32[2,384,128]{2,1,0:T(8,128)S(1)}, u32[]{:S(2)}, u32[]{:S(2)}) %collective-permute-start.21) | collective-permute-done | bytes 393248 | tf_op jit(solution)/shard_map/ppermute | solution.py:98
  88.0 1.8 %collective-permute-done.19.refs_1_ = f32[2,384,128]{2,1,0:T(8,128)S(1)} collective-permute-done((f32[2,384,128]{2,1,0:T(8,128)S(1)}, f32[2,384,128]{2,1,0:T(8,128)S(1)}, u32[]{:S(2)}, u32[]{:S(2)}) %collective-permute-start.19) | collective-permute-done | bytes 393248 | tf_op jit(solution)/shard_map/ppermute | solution.py:98
  90.8 1.3 collective-permute-start.13
  92.2 3.2 %collective-permute-start.20 = (f32[2,384,128]{2,1,0:T(8,128)S(1)}, f32[2,384,128]{2,1,0:T(8,128)}, u32[]{:S(2)}, u32[]{:S(2)}) collective-permute-start(f32[2,384,128]{2,1,0:T(8,128)S(1)} %collective-permute-done.19.refs_1_), channel_id=1, source_target_pairs={{32,0},{40,8},{48,16},{56,24},{64,32},{72,40},{80,48},{88,56},{96,... | collective-permute-start | bytes 1179656 | tf_op jit(solution)/shard_map/ppermute | solution.py:98
  95.4 8.8 %collective-permute-done.13 = f32[384,128]{1,0:T(8,128)S(1)} collective-permute-done((f32[384,128]{1,0:T(8,128)S(1)}, f32[384,128]{1,0:T(8,128)S(1)}, u32[]{:S(2)}, u32[]{:S(2)}) %collective-permute-start.13) | collective-permute-done | bytes 196640 | tf_op jit(solution)/shard_map/ppermute | solution.py:98
  104.3 3.2 %collective-permute-start.24 = (f32[384,128]{1,0:T(8,128)S(1)}, f32[384,128]{1,0:T(8,128)S(1)}, u32[]{:S(2)}, u32[]{:S(2)}) collective-permute-start(f32[384,128]{1,0:T(8,128)S(1)} %add_add_fusion.1), channel_id=1, source_target_pairs={{160,128},{168,136},{176,144},{184,152},{0,224},{8,232},{16,240},{... | collective-permute-start | bytes 589832 | tf_op jit(solution)/shard_map/ppermute | solution.py:98
  107.5 1.3 collective-permute-start.23
  108.8 3.8 %collective-permute-start.26 = (f32[2,960,128]{2,1,0:T(8,128)S(1)}, f32[2,960,128]{2,1,0:T(8,128)}, u32[]{:S(2)}, u32[]{:S(2)}) collective-permute-start(f32[2,960,128]{2,1,0:T(8,128)S(1)} %get-tuple-element.70), channel_id=1, source_target_pairs={{24,0},{0,8},{8,16},{16,24},{56,32},{32,40},{40,48},{48,56},{88,64... | collective-permute-start | bytes 2949128 | tf_op jit(solution)/shard_map/ppermute | solution.py:98
  112.6 2.0 %collective-permute-start.30 = (f32[2,384,128]{2,1,0:T(8,128)}, f32[2,384,128]{2,1,0:T(8,128)}, u32[]{:S(2)}, u32[]{:S(2)}) collective-permute-start(f32[2,384,128]{2,1,0:T(8,128)} %collective-permute-done.22.refs_6_), channel_id=1, source_target_pairs={{224,0},{232,8},{240,16},{248,24},{0,32},{8,40},{16,48},{24,56},{3... | collective-permute-start | bytes 1179656 | tf_op jit(solution)/shard_map/ppermute | solution.py:98
  115.4 1.1 fusion.14
  117.0 2.7 %collective-permute-start.31 = (f32[2,384,128]{2,1,0:T(8,128)}, f32[2,384,128]{2,1,0:T(8,128)}, u32[]{:S(2)}, u32[]{:S(2)}) collective-permute-start(f32[2,384,128]{2,1,0:T(8,128)} %get-tuple-element.68), channel_id=1, source_target_pairs={{32,0},{40,8},{48,16},{56,24},{64,32},{72,40},{80,48},{88,56},{96,... | collective-permute-start | bytes 1179656 | tf_op jit(solution)/shard_map/ppermute | solution.py:98
  119.7 3.9 %shard_map.18 = (f32[256,256]{1,0:T(8,128)}, f32[128,256]{1,0:T(8,128)}) custom-call(s32[2]{0:T(128)} %pad_add_fusion.where_ref.place_ref, f32[8,128,256]{2,1,0:T(8,128)} %bitcast.66, f32[384,128]{1,0:T(8,128)} %add_add_fusion.f_ref), custom_call_target="tpu_custom_call" | custom-call | flops 4000000000 | bytes 1048576 | tf_op jit(solution)/shard_map/pallas_call | solution.py:274
  123.7 6.7 %shard_map.19.refs_6_ = f32[12288,128]{1,0:T(8,128)} custom-call(s32[2]{0:T(128)} %pad_add_fusion.where_ref.place_ref, f32[12288,128]{1,0:T(8,128)} %bitcast.61, f32[256,256]{1,0:T(8,128)} %get-tuple-element.63.m_ref, f32[128,256]{1,0:T(8,128)} %get-tuple-element.64.s_ref, f32[2,384,128]{2,1,0:T(8,128)} %copy-done.3, f32[2,384,128]{2,1,0:T(8,128)} %copy-done.2, ...), custom_call_target="tpu_custom_call" | custom-call | flops 905969664 | bytes 10616832 | tf_op jit(solution)/shard_map/pallas_call | solution.py:359
  130.4 5.8 %shard_map.20 = f32[12288,128]{1,0:T(8,128)} custom-call(s32[2]{0:T(128)} %pad_add_fusion.where_ref.place_ref, f32[12288,128]{1,0:T(8,128)} %bitcast.62, f32[256,256]{1,0:T(8,128)} %get-tuple-element.63.m_ref, f32[128,256]{1,0:T(8,128)} %get-tuple-element.64.s_ref, f32[2,960,128]{2,1,0:T(8,128)} %collective-permute-done.26.refs_0_, ...), custom_call_target="tpu_custom_call", output_to_operand_aliasing={{}: (10, {})} | custom-call | flops 704643072 | bytes 8257536 | tf_op jit(solution)/shard_map/pallas_call | solution.py:359
  (83 shorter events, 11.3 us)
Async XLA Ops:
  6.5 113.2 %all-gather.3.cloned.1.call-start = ((), (), s32[]{:S(2)}) async-start(), calls=%async_computation | async-start | bytes 1179648 | tf_op jit(solution)/shard_map/all_gather | solution.py:391
  8.6 9.3 %collective-permute-start.1 = (f32[256,128]{1,0:T(8,128)S(1)}, f32[256,128]{1,0:T(8,128)S(1)}, u32[]{:S(2)}, u32[]{:S(2)}) collective-permute-start(f32[256,128]{1,0:T(8,128)S(1)} %maximum_select_fusion), channel_id=1, source_target_pairs={{0,160},{1,161},{8,168},{9,169}} | collective-permute-start | bytes 393224 | tf_op jit(solution)/shard_map/ppermute | solution.py:98
  15.1 27.0 %collective-permute-start.3 = (f32[4,384,128]{2,1,0:T(8,128)}, f32[4,384,128]{2,1,0:T(8,128)S(1)}, u32[]{:S(2)}, u32[]{:S(2)}) collective-permute-start(f32[4,384,128]{2,1,0:T(8,128)} %get-tuple-element.42), channel_id=1, source_target_pairs={{0,24},{8,16},{1,25},{9,17},{2,26},{10,18},{3,27},{11,19},{4,28},{... | collective-permute-start | bytes 2359304 | tf_op jit(solution)/shard_map/ppermute | solution.py:98
  16.4 25.7 %collective-permute-start.4 = (f32[4,384,128]{2,1,0:T(8,128)}, f32[4,384,128]{2,1,0:T(8,128)S(1)}, u32[]{:S(2)}, u32[]{:S(2)}) collective-permute-start(f32[4,384,128]{2,1,0:T(8,128)} %get-tuple-element.43), channel_id=1, source_target_pairs={{0,64},{8,72},{1,65},{9,73},{2,66},{10,74},{3,67},{11,75},{4,68},{... | collective-permute-start | bytes 2359304 | tf_op jit(solution)/shard_map/ppermute | solution.py:98
  17.1 24.9 %collective-permute-start.5 = (f32[4,384,128]{2,1,0:T(8,128)}, f32[4,384,128]{2,1,0:T(8,128)S(1)}, u32[]{:S(2)}, u32[]{:S(2)}) collective-permute-start(f32[4,384,128]{2,1,0:T(8,128)} %get-tuple-element.44), channel_id=1, source_target_pairs={{0,192},{8,200},{1,193},{9,201},{2,194},{10,202},{3,195},{11,203},... | collective-permute-start | bytes 2359304 | tf_op jit(solution)/shard_map/ppermute | solution.py:98
  44.3 18.4 %collective-permute-start.15 = (f32[384,128]{1,0:T(8,128)S(1)}, f32[384,128]{1,0:T(8,128)S(1)}, u32[]{:S(2)}, u32[]{:S(2)}) collective-permute-start(f32[384,128]{1,0:T(8,128)S(1)} %get-tuple-element.53), channel_id=1, source_target_pairs={{0,88},{8,136},{16,144},{24,168},{64,40},{72,216},{192,32},{200,12... | collective-permute-start | bytes 589832 | tf_op jit(solution)/shard_map/ppermute | solution.py:98
  57.5 6.6 %collective-permute-start.17 = (f32[384,128]{1,0:T(8,128)S(1)}, f32[384,128]{1,0:T(8,128)S(1)}, u32[]{:S(2)}, u32[]{:S(2)}) collective-permute-start(f32[384,128]{1,0:T(8,128)S(1)} %get-tuple-element.55), channel_id=1, source_target_pairs={{0,16},{8,64},{16,48},{24,240},{64,208},{72,112},{192,224},{200,40... | collective-permute-start | bytes 589832 | tf_op jit(solution)/shard_map/ppermute | solution.py:98
  58.8 7.2 %collective-permute-start.6 = (f32[384,128]{1,0:T(8,128)S(1)}, f32[384,128]{1,0:T(8,128)S(1)}, u32[]{:S(2)}, u32[]{:S(2)}) collective-permute-start(f32[384,128]{1,0:T(8,128)S(1)} %get-tuple-element.46), channel_id=1, source_target_pairs={{0,72},{8,80},{16,128},{24,152},{64,120},{72,224},{192,104},{200,2... | collective-permute-start | bytes 589832 | tf_op jit(solution)/shard_map/ppermute | solution.py:98
  60.1 9.5 %collective-permute-start.8 = (f32[384,128]{1,0:T(8,128)S(1)}, f32[384,128]{1,0:T(8,128)S(1)}, u32[]{:S(2)}, u32[]{:S(2)}) collective-permute-start(f32[384,128]{1,0:T(8,128)S(1)} %get-tuple-element.48), channel_id=1, source_target_pairs={{0,216},{8,192},{16,248},{24,136},{64,48},{72,32},{192,112},{200,9... | collective-permute-start | bytes 589832 | tf_op jit(solution)/shard_map/ppermute | solution.py:98
  61.4 8.9 %collective-permute-start.10 = (f32[384,128]{1,0:T(8,128)S(1)}, f32[384,128]{1,0:T(8,128)S(1)}, u32[]{:S(2)}, u32[]{:S(2)}) collective-permute-start(f32[384,128]{1,0:T(8,128)S(1)} %get-tuple-element.50), channel_id=1, source_target_pairs={{0,200},{8,208},{16,0},{24,8},{64,184},{72,176},{192,80},{200,88},... | collective-permute-start | bytes 589832 | tf_op jit(solution)/shard_map/ppermute | solution.py:98
  62.7 10.1 %collective-permute-start.16 = (f32[384,128]{1,0:T(8,128)S(1)}, f32[384,128]{1,0:T(8,128)S(1)}, u32[]{:S(2)}, u32[]{:S(2)}) collective-permute-start(f32[384,128]{1,0:T(8,128)S(1)} %get-tuple-element.54), channel_id=1, source_target_pairs={{0,144},{8,152},{16,104},{24,56},{64,160},{72,168},{192,176},{200,... | collective-permute-start | bytes 589832 | tf_op jit(solution)/shard_map/ppermute | solution.py:98
  64.0 10.9 %collective-permute-start.18 = (f32[384,128]{1,0:T(8,128)S(1)}, f32[384,128]{1,0:T(8,128)S(1)}, u32[]{:S(2)}, u32[]{:S(2)}) collective-permute-start(f32[384,128]{1,0:T(8,128)S(1)} %get-tuple-element.56), channel_id=1, source_target_pairs={{0,128},{8,24},{16,160},{24,96},{64,232},{72,56},{192,248},{200,18... | collective-permute-start | bytes 589832 | tf_op jit(solution)/shard_map/ppermute | solution.py:98
  66.0 12.4 %collective-permute-start.7 = (f32[384,128]{1,0:T(8,128)S(1)}, f32[384,128]{1,0:T(8,128)S(1)}, u32[]{:S(2)}, u32[]{:S(2)}) collective-permute-start(f32[384,128]{1,0:T(8,128)S(1)} %get-tuple-element.78), channel_id=1, source_target_pairs={{160,162},{161,163},{168,170},{169,171}} | collective-permute-start | bytes 589832 | tf_op jit(solution)/shard_map/ppermute | solution.py:98
  69.6 12.4 %collective-permute-start.9 = (f32[384,128]{1,0:T(8,128)S(1)}, f32[384,128]{1,0:T(8,128)S(1)}, u32[]{:S(2)}, u32[]{:S(2)}) collective-permute-start(f32[384,128]{1,0:T(8,128)S(1)} %get-tuple-element.78), channel_id=1, source_target_pairs={{160,166},{161,167},{168,174},{169,175}} | collective-permute-start | bytes 589832 | tf_op jit(solution)/shard_map/ppermute | solution.py:98
  70.3 11.8 %collective-permute-start.11 = (f32[384,128]{1,0:T(8,128)S(1)}, f32[384,128]{1,0:T(8,128)S(1)}, u32[]{:S(2)}, u32[]{:S(2)}) collective-permute-start(f32[384,128]{1,0:T(8,128)S(1)} %get-tuple-element.78), channel_id=1, source_target_pairs={{160,164},{161,165},{168,172},{169,173}} | collective-permute-start | bytes 589832 | tf_op jit(solution)/shard_map/ppermute | solution.py:98
  75.1 9.3 %collective-permute-start.27 = (f32[2,384,128]{2,1,0:T(8,128)S(1)}, f32[2,384,128]{2,1,0:T(8,128)S(1)}, u32[]{:S(2)}, u32[]{:S(2)}) collective-permute-start(f32[2,384,128]{2,1,0:T(8,128)S(1)} %pad_maximum_fusion.3.refs_0_), channel_id=1, source_target_pairs={{8,0},{16,8},{24,16},{0,24},{40,32},{48,40},{56,48},{32,56},{72,64... | collective-permute-start | bytes 1179656 | tf_op jit(solution)/shard_map/ppermute | solution.py:98
  75.2 9.2 %collective-permute-start.25 = (f32[2,384,128]{2,1,0:T(8,128)S(1)}, f32[2,384,128]{2,1,0:T(8,128)S(1)}, u32[]{:S(2)}, u32[]{:S(2)}) collective-permute-start(f32[2,384,128]{2,1,0:T(8,128)S(1)} %pad_maximum_fusion.3.refs_0_), channel_id=1, source_target_pairs={{24,0},{0,8},{8,16},{16,24},{56,32},{32,40},{40,48},{48,56},{88,64... | collective-permute-start | bytes 1179656 | tf_op jit(solution)/shard_map/ppermute | solution.py:98
  78.4 9.6 %collective-permute-start.21 = (f32[2,384,128]{2,1,0:T(8,128)S(1)}, f32[2,384,128]{2,1,0:T(8,128)S(1)}, u32[]{:S(2)}, u32[]{:S(2)}) collective-permute-start(f32[2,384,128]{2,1,0:T(8,128)S(1)} %pad_maximum_fusion.3.refs_0_), channel_id=1, source_target_pairs={{224,0},{232,8},{240,16},{248,24},{0,32},{8,40},{16,48},{24,56},{3... | collective-permute-start | bytes 1179656 | tf_op jit(solution)/shard_map/ppermute | solution.py:98
  82.1 7.8 %collective-permute-start.19 = (f32[2,384,128]{2,1,0:T(8,128)S(1)}, f32[2,384,128]{2,1,0:T(8,128)S(1)}, u32[]{:S(2)}, u32[]{:S(2)}) collective-permute-start(f32[2,384,128]{2,1,0:T(8,128)S(1)} %pad_maximum_fusion.3.refs_0_), channel_id=1, source_target_pairs={{32,0},{40,8},{48,16},{56,24},{64,32},{72,40},{80,48},{88,56},{96,... | collective-permute-start | bytes 1179656 | tf_op jit(solution)/shard_map/ppermute | solution.py:98
  82.1 7.9 %collective-permute-start.12 = (f32[384,128]{1,0:T(8,128)S(1)}, f32[384,128]{1,0:T(8,128)S(1)}, u32[]{:S(2)}, u32[]{:S(2)}) collective-permute-start(f32[384,128]{1,0:T(8,128)S(1)} %add_add_fusion.2), channel_id=1, source_target_pairs={{160,184},{168,176},{161,185},{169,177},{162,186},{170,178},{163,1... | collective-permute-start | bytes 589832 | tf_op jit(solution)/shard_map/ppermute | solution.py:98
  90.0 25.4 %collective-permute-start.28 = (f32[2,960,128]{2,1,0:T(8,128)S(1)}, f32[2,960,128]{2,1,0:T(8,128)S(1)}, u32[]{:S(2)}, u32[]{:S(2)}) collective-permute-start(f32[2,960,128]{2,1,0:T(8,128)S(1)} %get-tuple-element.69), channel_id=1, source_target_pairs={{8,0},{16,8},{24,16},{0,24},{40,32},{48,40},{56,48},{32,56},{72,64... | collective-permute-start | bytes 2949128 | tf_op jit(solution)/shard_map/ppermute | solution.py:98
  90.1 5.3 %collective-permute-start.14 = (f32[384,128]{1,0:T(8,128)S(1)}, f32[384,128]{1,0:T(8,128)S(1)}, u32[]{:S(2)}, u32[]{:S(2)}) collective-permute-start(f32[384,128]{1,0:T(8,128)S(1)} %add.90), channel_id=1, source_target_pairs={{160,64},{168,72},{176,80},{184,88},{161,65},{169,73},{177,81},{18... | collective-permute-start | bytes 589832 | tf_op jit(solution)/shard_map/ppermute | solution.py:98
  90.8 13.4 %collective-permute-start.13 = (f32[384,128]{1,0:T(8,128)S(1)}, f32[384,128]{1,0:T(8,128)S(1)}, u32[]{:S(2)}, u32[]{:S(2)}) collective-permute-start(f32[384,128]{1,0:T(8,128)S(1)} %add.90), channel_id=1, source_target_pairs={{160,0},{168,8},{176,16},{184,24},{161,1},{169,9},{177,17},{185,25... | collective-permute-start | bytes 589832 | tf_op jit(solution)/shard_map/ppermute | solution.py:98
  92.1 12.2 %collective-permute-start.22 = (f32[2,384,128]{2,1,0:T(8,128)S(1)}, f32[2,384,128]{2,1,0:T(8,128)}, u32[]{:S(2)}, u32[]{:S(2)}) collective-permute-start(f32[2,384,128]{2,1,0:T(8,128)S(1)} %collective-permute-done.21.refs_2_), channel_id=1, source_target_pairs={{224,0},{232,8},{240,16},{248,24},{0,32},{8,40},{16,48},{24,56},{3... | collective-permute-start | bytes 1179656 | tf_op jit(solution)/shard_map/ppermute | solution.py:98
  92.2 12.1 %collective-permute-start.20 = (f32[2,384,128]{2,1,0:T(8,128)S(1)}, f32[2,384,128]{2,1,0:T(8,128)}, u32[]{:S(2)}, u32[]{:S(2)}) collective-permute-start(f32[2,384,128]{2,1,0:T(8,128)S(1)} %collective-permute-done.19.refs_1_), channel_id=1, source_target_pairs={{32,0},{40,8},{48,16},{56,24},{64,32},{72,40},{80,48},{88,56},{96,... | collective-permute-start | bytes 1179656 | tf_op jit(solution)/shard_map/ppermute | solution.py:98
  104.3 8.3 %collective-permute-start.24 = (f32[384,128]{1,0:T(8,128)S(1)}, f32[384,128]{1,0:T(8,128)S(1)}, u32[]{:S(2)}, u32[]{:S(2)}) collective-permute-start(f32[384,128]{1,0:T(8,128)S(1)} %add_add_fusion.1), channel_id=1, source_target_pairs={{160,128},{168,136},{176,144},{184,152},{0,224},{8,232},{16,240},{... | collective-permute-start | bytes 589832 | tf_op jit(solution)/shard_map/ppermute | solution.py:98
  107.5 7.2 %collective-permute-start.23 = (f32[384,128]{1,0:T(8,128)S(1)}, f32[384,128]{1,0:T(8,128)S(1)}, u32[]{:S(2)}, u32[]{:S(2)}) collective-permute-start(f32[384,128]{1,0:T(8,128)S(1)} %add_add_fusion.1), channel_id=1, source_target_pairs={{160,192},{168,200},{176,208},{184,216},{0,32},{8,40},{16,48},{24,... | collective-permute-start | bytes 589832 | tf_op jit(solution)/shard_map/ppermute | solution.py:98
  108.8 21.6 %collective-permute-start.26 = (f32[2,960,128]{2,1,0:T(8,128)S(1)}, f32[2,960,128]{2,1,0:T(8,128)}, u32[]{:S(2)}, u32[]{:S(2)}) collective-permute-start(f32[2,960,128]{2,1,0:T(8,128)S(1)} %get-tuple-element.70), channel_id=1, source_target_pairs={{24,0},{0,8},{8,16},{16,24},{56,32},{32,40},{40,48},{48,56},{88,64... | collective-permute-start | bytes 2949128 | tf_op jit(solution)/shard_map/ppermute | solution.py:98
  112.6 17.8 %collective-permute-start.29 = (f32[2,384,128]{2,1,0:T(8,128)}, f32[2,384,128]{2,1,0:T(8,128)}, u32[]{:S(2)}, u32[]{:S(2)}) collective-permute-start(f32[2,384,128]{2,1,0:T(8,128)} %collective-permute-done.20.refs_5_), channel_id=1, source_target_pairs={{32,0},{40,8},{48,16},{56,24},{64,32},{72,40},{80,48},{88,56},{96,... | collective-permute-start | bytes 1179656 | tf_op jit(solution)/shard_map/ppermute | solution.py:98
  112.6 17.8 %collective-permute-start.30 = (f32[2,384,128]{2,1,0:T(8,128)}, f32[2,384,128]{2,1,0:T(8,128)}, u32[]{:S(2)}, u32[]{:S(2)}) collective-permute-start(f32[2,384,128]{2,1,0:T(8,128)} %collective-permute-done.22.refs_6_), channel_id=1, source_target_pairs={{224,0},{232,8},{240,16},{248,24},{0,32},{8,40},{16,48},{24,56},{3... | collective-permute-start | bytes 1179656 | tf_op jit(solution)/shard_map/ppermute | solution.py:98
  116.5 13.9 %collective-permute-start.32 = (f32[2,384,128]{2,1,0:T(8,128)}, f32[2,384,128]{2,1,0:T(8,128)}, u32[]{:S(2)}, u32[]{:S(2)}) collective-permute-start(f32[2,384,128]{2,1,0:T(8,128)} %get-tuple-element.67), channel_id=1, source_target_pairs={{224,0},{232,8},{240,16},{248,24},{0,32},{8,40},{16,48},{24,56},{3... | collective-permute-start | bytes 1179656 | tf_op jit(solution)/shard_map/ppermute | solution.py:98
  117.0 13.4 %collective-permute-start.31 = (f32[2,384,128]{2,1,0:T(8,128)}, f32[2,384,128]{2,1,0:T(8,128)}, u32[]{:S(2)}, u32[]{:S(2)}) collective-permute-start(f32[2,384,128]{2,1,0:T(8,128)} %get-tuple-element.68), channel_id=1, source_target_pairs={{32,0},{40,8},{48,16},{56,24},{64,32},{72,40},{80,48},{88,56},{96,... | collective-permute-start | bytes 1179656 | tf_op jit(solution)/shard_map/ppermute | solution.py:98
  (11 other events, 206.6 us)
Sparse Core Ops, SparseCore 0:
  66.1 24.9 all-gather.2

commit v5 on v4

--- a/solution.py
+++ b/solution.py
@@ -298,10 +298,10 @@
     def o_copy(k):
         return pltpu.make_async_copy(xs.at[k], rows_of(o_ref, k), o_sem.at[k])
 
-    for k, sources in enumerate(parts):
+    def fetch(k):
         x_copy(k).start()
         start = 0
-        for which, offset, size in sources:
+        for which, offset, size in parts[k]:
             for panel in (0, 1):
                 pltpu.make_async_copy(
                     pieces[which].at[panel, pl.ds(offset, size)],
@@ -309,6 +309,9 @@
                     p_sem.at[k],
                 ).start()
             start += size
+
+    for k in range(min(4, count)):
+        fetch(k)
     m = m_ref[...]
     m_high = m.astype(BF16)
     m_rest = (m - m_high.astype(F32)).astype(BF16)
@@ -336,7 +339,10 @@
         o_copy(k).start()
         return carry
 
-    lax.fori_loop(0, count, step, 0)
+    for k in range(count):
+        if k + 4 < count:
+            fetch(k + 4)
+        step(k, 0)
 
     def finish(k, carry):
         o_copy(k).wait()

time: 146 us -> 148 us (1.014)
  Pallas kernels: 21.6 us -> 23.3 us
    pallas_call x2, Pallas kernels: 12.4 us -> 14.1 us  [update(): pl.pallas_call(functools.partial(update_kernel, parts, keys, rows, out is...]
  transfers between devices with their start and end apart: 34 -> 34, of which waited for: 8 -> 8; matrix products, arithmetic and copies ran while one was open for 3% -> 3% of each run, Pallas kernels for 11% -> 12%
where the time goes in v5:
time: 148 us; the launch traced here: 145 us
  starting transfers between devices  54.8 us (37%)
  waiting for transfers between devices  45.4 us (31%)
  Pallas kernels  23.3 us (16%)
  between operations  14 us (9%)
  other arithmetic  3.71 us (3%)
  local copies, waits for them, and re-layouts  3.51 us (2%)
    ppermute x33, starting transfers between devices, __call__(): result = [lax.ppermute(value, axis, pairs)]  54.8 us
    ppermute x33, waiting for transfers between devices, __call__(): result = [lax.ppermute(value, axis, pairs)]  45.4 us
    pallas_call x2, Pallas kernels, update(): pl.pallas_call(functools.partial(update_kernel, parts, keys, rows, out is...  14.1 us
    pallas_call x1, Pallas kernels, extract(): pl.pallas_call(functools.partial(extract_kernel, rows), out_shape=(jax.Sh...  5.24 us
    pallas_call x1, Pallas kernels, combine(): pl.pallas_call(combine_kernel, out_shape=(jax.ShapeDtypeStruct((256, 256)...  3.94 us
  transfers between devices with their start and end apart: 34, of which 8 were waited for; matrix products, arithmetic and copies ran while one was open for 3% of the time, Pallas kernels for 12%

profile of v5, /device:TPU:24, one launch (start us, length us, event | category | flops | bytes accessed | tf_op | source)
XLA Modules:
  0.0 144.7 jit_solution(2116357736590360572)
XLA Ops:
  6.5 1.3 slice_reduce_fusion
  9.9 5.2 %shard_map.17 = (f32[4,384,128]{2,1,0:T(8,128)}, f32[4,384,128]{2,1,0:T(8,128)}, f32[4,384,128]{2,1,0:T(8,128)}, f32[4,384,128]{2,1,0:T(8,128)}) custom-call(s32[2]{0:T(128)} %pad_add_fusion.where_ref.place_ref, f32[12288,128]{1,0:T(8,128)} %bitcast.60), custom_call_target="tpu_custom_call" | custom-call | bytes 9437184 | tf_op jit(solution)/shard_map/pallas_call | solution.py:78
  15.1 1.3 collective-permute-start.3
  19.4 22.7 %collective-permute-done.3 = f32[4,384,128]{2,1,0:T(8,128)S(1)} collective-permute-done((f32[4,384,128]{2,1,0:T(8,128)}, f32[4,384,128]{2,1,0:T(8,128)S(1)}, u32[]{:S(2)}, u32[]{:S(2)}) %collective-permute-start.3) | collective-permute-done | bytes 786464 | tf_op jit(solution)/shard_map/ppermute | solution.py:98
  43.0 1.3 add_select_fusion
  44.3 13.1 %collective-permute-start.15 = (f32[384,128]{1,0:T(8,128)S(1)}, f32[384,128]{1,0:T(8,128)S(1)}, u32[]{:S(2)}, u32[]{:S(2)}) collective-permute-start(f32[384,128]{1,0:T(8,128)S(1)} %get-tuple-element.53), channel_id=1, source_target_pairs={{0,88},{8,136},{16,144},{24,168},{64,40},{72,216},{192,32},{200,12... | collective-permute-start | bytes 589832 | tf_op jit(solution)/shard_map/ppermute | solution.py:98
  57.5 1.3 collective-permute-start.17
  58.8 1.3 collective-permute-start.6
  60.1 1.3 collective-permute-start.8
  61.4 1.3 collective-permute-start.10
  62.7 1.3 collective-permute-start.16
  64.0 1.9 %collective-permute-start.18 = (f32[384,128]{1,0:T(8,128)S(1)}, f32[384,128]{1,0:T(8,128)S(1)}, u32[]{:S(2)}, u32[]{:S(2)}) collective-permute-start(f32[384,128]{1,0:T(8,128)S(1)} %get-tuple-element.56), channel_id=1, source_target_pairs={{0,128},{8,24},{16,160},{24,96},{64,232},{72,56},{192,248},{200,18... | collective-permute-start | bytes 589832 | tf_op jit(solution)/shard_map/ppermute | solution.py:98
  66.7 2.9 %collective-permute-done.8 = f32[384,128]{1,0:T(8,128)S(1)} collective-permute-done((f32[384,128]{1,0:T(8,128)S(1)}, f32[384,128]{1,0:T(8,128)S(1)}, u32[]{:S(2)}, u32[]{:S(2)}) %collective-permute-start.8) | collective-permute-done | bytes 196640 | tf_op jit(solution)/shard_map/ppermute | solution.py:98
  71.0 1.8 %collective-permute-done.16 = f32[384,128]{1,0:T(8,128)S(1)} collective-permute-done((f32[384,128]{1,0:T(8,128)S(1)}, f32[384,128]{1,0:T(8,128)S(1)}, u32[]{:S(2)}, u32[]{:S(2)}) %collective-permute-start.16) | collective-permute-done | bytes 196640 | tf_op jit(solution)/shard_map/ppermute | solution.py:98
  72.8 2.1 %collective-permute-done.18 = f32[384,128]{1,0:T(8,128)S(1)} collective-permute-done((f32[384,128]{1,0:T(8,128)S(1)}, f32[384,128]{1,0:T(8,128)S(1)}, u32[]{:S(2)}, u32[]{:S(2)}) %collective-permute-start.18) | collective-permute-done | bytes 196640 | tf_op jit(solution)/shard_map/ppermute | solution.py:98
  75.2 3.2 %collective-permute-start.25 = (f32[2,384,128]{2,1,0:T(8,128)S(1)}, f32[2,384,128]{2,1,0:T(8,128)S(1)}, u32[]{:S(2)}, u32[]{:S(2)}) collective-permute-start(f32[2,384,128]{2,1,0:T(8,128)S(1)} %pad_maximum_fusion.3.refs_0_), channel_id=1, source_target_pairs={{24,0},{0,8},{8,16},{16,24},{56,32},{32,40},{40,48},{48,56},{88,64... | collective-permute-start | bytes 1179656 | tf_op jit(solution)/shard_map/ppermute | solution.py:98
  78.4 3.6 %collective-permute-start.21 = (f32[2,384,128]{2,1,0:T(8,128)S(1)}, f32[2,384,128]{2,1,0:T(8,128)S(1)}, u32[]{:S(2)}, u32[]{:S(2)}) collective-permute-start(f32[2,384,128]{2,1,0:T(8,128)S(1)} %pad_maximum_fusion.3.refs_0_), channel_id=1, source_target_pairs={{224,0},{232,8},{240,16},{248,24},{0,32},{8,40},{16,48},{24,56},{3... | collective-permute-start | bytes 1179656 | tf_op jit(solution)/shard_map/ppermute | solution.py:98
  82.8 1.5 %collective-permute-done.27.refs_3_ = f32[2,384,128]{2,1,0:T(8,128)S(1)} collective-permute-done((f32[2,384,128]{2,1,0:T(8,128)S(1)}, f32[2,384,128]{2,1,0:T(8,128)S(1)}, u32[]{:S(2)}, u32[]{:S(2)}) %collective-permute-start.27) | collective-permute-done | bytes 393248 | tf_op jit(solution)/shard_map/ppermute | solution.py:98
  84.4 3.6 %collective-permute-done.21.refs_2_ = f32[2,384,128]{2,1,0:T(8,128)S(1)} collective-permute-done((f32[2,384,128]{2,1,0:T(8,128)S(1)}, f32[2,384,128]{2,1,0:T(8,128)S(1)}, u32[]{:S(2)}, u32[]{:S(2)}) %collective-permute-start.21) | collective-permute-done | bytes 393248 | tf_op jit(solution)/shard_map/ppermute | solution.py:98
  88.0 1.8 %collective-permute-done.19.refs_1_ = f32[2,384,128]{2,1,0:T(8,128)S(1)} collective-permute-done((f32[2,384,128]{2,1,0:T(8,128)S(1)}, f32[2,384,128]{2,1,0:T(8,128)S(1)}, u32[]{:S(2)}, u32[]{:S(2)}) %collective-permute-start.19) | collective-permute-done | bytes 393248 | tf_op jit(solution)/shard_map/ppermute | solution.py:98
  90.8 1.3 collective-permute-start.13
  92.2 3.2 %collective-permute-start.20 = (f32[2,384,128]{2,1,0:T(8,128)S(1)}, f32[2,384,128]{2,1,0:T(8,128)}, u32[]{:S(2)}, u32[]{:S(2)}) collective-permute-start(f32[2,384,128]{2,1,0:T(8,128)S(1)} %collective-permute-done.19.refs_1_), channel_id=1, source_target_pairs={{32,0},{40,8},{48,16},{56,24},{64,32},{72,40},{80,48},{88,56},{96,... | collective-permute-start | bytes 1179656 | tf_op jit(solution)/shard_map/ppermute | solution.py:98
  95.4 8.8 %collective-permute-done.13 = f32[384,128]{1,0:T(8,128)S(1)} collective-permute-done((f32[384,128]{1,0:T(8,128)S(1)}, f32[384,128]{1,0:T(8,128)S(1)}, u32[]{:S(2)}, u32[]{:S(2)}) %collective-permute-start.13) | collective-permute-done | bytes 196640 | tf_op jit(solution)/shard_map/ppermute | solution.py:98
  104.3 3.2 %collective-permute-start.24 = (f32[384,128]{1,0:T(8,128)S(1)}, f32[384,128]{1,0:T(8,128)S(1)}, u32[]{:S(2)}, u32[]{:S(2)}) collective-permute-start(f32[384,128]{1,0:T(8,128)S(1)} %add_add_fusion.1), channel_id=1, source_target_pairs={{160,128},{168,136},{176,144},{184,152},{0,224},{8,232},{16,240},{... | collective-permute-start | bytes 589832 | tf_op jit(solution)/shard_map/ppermute | solution.py:98
  107.5 1.3 collective-permute-start.23
  108.8 3.8 %collective-permute-start.26 = (f32[2,960,128]{2,1,0:T(8,128)S(1)}, f32[2,960,128]{2,1,0:T(8,128)}, u32[]{:S(2)}, u32[]{:S(2)}) collective-permute-start(f32[2,960,128]{2,1,0:T(8,128)S(1)} %get-tuple-element.70), channel_id=1, source_target_pairs={{24,0},{0,8},{8,16},{16,24},{56,32},{32,40},{40,48},{48,56},{88,64... | collective-permute-start | bytes 2949128 | tf_op jit(solution)/shard_map/ppermute | solution.py:98
  112.6 2.0 %collective-permute-start.30 = (f32[2,384,128]{2,1,0:T(8,128)}, f32[2,384,128]{2,1,0:T(8,128)}, u32[]{:S(2)}, u32[]{:S(2)}) collective-permute-start(f32[2,384,128]{2,1,0:T(8,128)} %collective-permute-done.22.refs_6_), channel_id=1, source_target_pairs={{224,0},{232,8},{240,16},{248,24},{0,32},{8,40},{16,48},{24,56},{3... | collective-permute-start | bytes 1179656 | tf_op jit(solution)/shard_map/ppermute | solution.py:98
  115.4 1.1 fusion.14
  117.0 2.7 %collective-permute-start.31 = (f32[2,384,128]{2,1,0:T(8,128)}, f32[2,384,128]{2,1,0:T(8,128)}, u32[]{:S(2)}, u32[]{:S(2)}) collective-permute-start(f32[2,384,128]{2,1,0:T(8,128)} %get-tuple-element.68), channel_id=1, source_target_pairs={{32,0},{40,8},{48,16},{56,24},{64,32},{72,40},{80,48},{88,56},{96,... | collective-permute-start | bytes 1179656 | tf_op jit(solution)/shard_map/ppermute | solution.py:98
  119.7 3.9 %shard_map.18 = (f32[256,256]{1,0:T(8,128)}, f32[128,256]{1,0:T(8,128)}) custom-call(s32[2]{0:T(128)} %pad_add_fusion.where_ref.place_ref, f32[8,128,256]{2,1,0:T(8,128)} %bitcast.66, f32[384,128]{1,0:T(8,128)} %add_add_fusion.f_ref), custom_call_target="tpu_custom_call" | custom-call | flops 4000000000 | bytes 1048576 | tf_op jit(solution)/shard_map/pallas_call | solution.py:274
  123.7 7.7 %shard_map.19.refs_6_ = f32[12288,128]{1,0:T(8,128)} custom-call(s32[2]{0:T(128)} %pad_add_fusion.where_ref.place_ref, f32[12288,128]{1,0:T(8,128)} %bitcast.61, f32[256,256]{1,0:T(8,128)} %get-tuple-element.63.m_ref, f32[128,256]{1,0:T(8,128)} %get-tuple-element.64.s_ref, f32[2,384,128]{2,1,0:T(8,128)} %copy-done.3, f32[2,384,128]{2,1,0:T(8,128)} %copy-done.2, ...), custom_call_target="tpu_custom_call" | custom-call | flops 905969664 | bytes 10616832 | tf_op jit(solution)/shard_map/pallas_call | solution.py:365
  131.4 6.4 %shard_map.20 = f32[12288,128]{1,0:T(8,128)} custom-call(s32[2]{0:T(128)} %pad_add_fusion.where_ref.place_ref, f32[12288,128]{1,0:T(8,128)} %bitcast.62, f32[256,256]{1,0:T(8,128)} %get-tuple-element.63.m_ref, f32[128,256]{1,0:T(8,128)} %get-tuple-element.64.s_ref, f32[2,960,128]{2,1,0:T(8,128)} %collective-permute-done.26.refs_0_, ...), custom_call_target="tpu_custom_call", output_to_operand_aliasing={{}: (10, {})} | custom-call | flops 704643072 | bytes 8257536 | tf_op jit(solution)/shard_map/pallas_call | solution.py:365
  (83 shorter events, 11.3 us)
Async XLA Ops:
  6.5 113.2 %all-gather.3.cloned.1.call-start = ((), (), s32[]{:S(2)}) async-start(), calls=%async_computation | async-start | bytes 1179648 | tf_op jit(solution)/shard_map/all_gather | solution.py:397
  8.6 9.3 %collective-permute-start.1 = (f32[256,128]{1,0:T(8,128)S(1)}, f32[256,128]{1,0:T(8,128)S(1)}, u32[]{:S(2)}, u32[]{:S(2)}) collective-permute-start(f32[256,128]{1,0:T(8,128)S(1)} %maximum_select_fusion), channel_id=1, source_target_pairs={{0,160},{1,161},{8,168},{9,169}} | collective-permute-start | bytes 393224 | tf_op jit(solution)/shard_map/ppermute | solution.py:98
  15.1 27.0 %collective-permute-start.3 = (f32[4,384,128]{2,1,0:T(8,128)}, f32[4,384,128]{2,1,0:T(8,128)S(1)}, u32[]{:S(2)}, u32[]{:S(2)}) collective-permute-start(f32[4,384,128]{2,1,0:T(8,128)} %get-tuple-element.42), channel_id=1, source_target_pairs={{0,24},{8,16},{1,25},{9,17},{2,26},{10,18},{3,27},{11,19},{4,28},{... | collective-permute-start | bytes 2359304 | tf_op jit(solution)/shard_map/ppermute | solution.py:98
  16.4 25.7 %collective-permute-start.4 = (f32[4,384,128]{2,1,0:T(8,128)}, f32[4,384,128]{2,1,0:T(8,128)S(1)}, u32[]{:S(2)}, u32[]{:S(2)}) collective-permute-start(f32[4,384,128]{2,1,0:T(8,128)} %get-tuple-element.43), channel_id=1, source_target_pairs={{0,64},{8,72},{1,65},{9,73},{2,66},{10,74},{3,67},{11,75},{4,68},{... | collective-permute-start | bytes 2359304 | tf_op jit(solution)/shard_map/ppermute | solution.py:98
  17.1 24.9 %collective-permute-start.5 = (f32[4,384,128]{2,1,0:T(8,128)}, f32[4,384,128]{2,1,0:T(8,128)S(1)}, u32[]{:S(2)}, u32[]{:S(2)}) collective-permute-start(f32[4,384,128]{2,1,0:T(8,128)} %get-tuple-element.44), channel_id=1, source_target_pairs={{0,192},{8,200},{1,193},{9,201},{2,194},{10,202},{3,195},{11,203},... | collective-permute-start | bytes 2359304 | tf_op jit(solution)/shard_map/ppermute | solution.py:98
  44.3 18.4 %collective-permute-start.15 = (f32[384,128]{1,0:T(8,128)S(1)}, f32[384,128]{1,0:T(8,128)S(1)}, u32[]{:S(2)}, u32[]{:S(2)}) collective-permute-start(f32[384,128]{1,0:T(8,128)S(1)} %get-tuple-element.53), channel_id=1, source_target_pairs={{0,88},{8,136},{16,144},{24,168},{64,40},{72,216},{192,32},{200,12... | collective-permute-start | bytes 589832 | tf_op jit(solution)/shard_map/ppermute | solution.py:98
  57.5 6.6 %collective-permute-start.17 = (f32[384,128]{1,0:T(8,128)S(1)}, f32[384,128]{1,0:T(8,128)S(1)}, u32[]{:S(2)}, u32[]{:S(2)}) collective-permute-start(f32[384,128]{1,0:T(8,128)S(1)} %get-tuple-element.55), channel_id=1, source_target_pairs={{0,16},{8,64},{16,48},{24,240},{64,208},{72,112},{192,224},{200,40... | collective-permute-start | bytes 589832 | tf_op jit(solution)/shard_map/ppermute | solution.py:98
  58.8 7.2 %collective-permute-start.6 = (f32[384,128]{1,0:T(8,128)S(1)}, f32[384,128]{1,0:T(8,128)S(1)}, u32[]{:S(2)}, u32[]{:S(2)}) collective-permute-start(f32[384,128]{1,0:T(8,128)S(1)} %get-tuple-element.46), channel_id=1, source_target_pairs={{0,72},{8,80},{16,128},{24,152},{64,120},{72,224},{192,104},{200,2... | collective-permute-start | bytes 589832 | tf_op jit(solution)/shard_map/ppermute | solution.py:98
  60.1 9.5 %collective-permute-start.8 = (f32[384,128]{1,0:T(8,128)S(1)}, f32[384,128]{1,0:T(8,128)S(1)}, u32[]{:S(2)}, u32[]{:S(2)}) collective-permute-start(f32[384,128]{1,0:T(8,128)S(1)} %get-tuple-element.48), channel_id=1, source_target_pairs={{0,216},{8,192},{16,248},{24,136},{64,48},{72,32},{192,112},{200,9... | collective-permute-start | bytes 589832 | tf_op jit(solution)/shard_map/ppermute | solution.py:98
  61.4 8.9 %collective-permute-start.10 = (f32[384,128]{1,0:T(8,128)S(1)}, f32[384,128]{1,0:T(8,128)S(1)}, u32[]{:S(2)}, u32[]{:S(2)}) collective-permute-start(f32[384,128]{1,0:T(8,128)S(1)} %get-tuple-element.50), channel_id=1, source_target_pairs={{0,200},{8,208},{16,0},{24,8},{64,184},{72,176},{192,80},{200,88},... | collective-permute-start | bytes 589832 | tf_op jit(solution)/shard_map/ppermute | solution.py:98
  62.7 10.1 %collective-permute-start.16 = (f32[384,128]{1,0:T(8,128)S(1)}, f32[384,128]{1,0:T(8,128)S(1)}, u32[]{:S(2)}, u32[]{:S(2)}) collective-permute-start(f32[384,128]{1,0:T(8,128)S(1)} %get-tuple-element.54), channel_id=1, source_target_pairs={{0,144},{8,152},{16,104},{24,56},{64,160},{72,168},{192,176},{200,... | collective-permute-start | bytes 589832 | tf_op jit(solution)/shard_map/ppermute | solution.py:98
  64.0 10.9 %collective-permute-start.18 = (f32[384,128]{1,0:T(8,128)S(1)}, f32[384,128]{1,0:T(8,128)S(1)}, u32[]{:S(2)}, u32[]{:S(2)}) collective-permute-start(f32[384,128]{1,0:T(8,128)S(1)} %get-tuple-element.56), channel_id=1, source_target_pairs={{0,128},{8,24},{16,160},{24,96},{64,232},{72,56},{192,248},{200,18... | collective-permute-start | bytes 589832 | tf_op jit(solution)/shard_map/ppermute | solution.py:98
  66.0 12.4 %collective-permute-start.7 = (f32[384,128]{1,0:T(8,128)S(1)}, f32[384,128]{1,0:T(8,128)S(1)}, u32[]{:S(2)}, u32[]{:S(2)}) collective-permute-start(f32[384,128]{1,0:T(8,128)S(1)} %get-tuple-element.78), channel_id=1, source_target_pairs={{160,162},{161,163},{168,170},{169,171}} | collective-permute-start | bytes 589832 | tf_op jit(solution)/shard_map/ppermute | solution.py:98
  69.6 12.4 %collective-permute-start.9 = (f32[384,128]{1,0:T(8,128)S(1)}, f32[384,128]{1,0:T(8,128)S(1)}, u32[]{:S(2)}, u32[]{:S(2)}) collective-permute-start(f32[384,128]{1,0:T(8,128)S(1)} %get-tuple-element.78), channel_id=1, source_target_pairs={{160,166},{161,167},{168,174},{169,175}} | collective-permute-start | bytes 589832 | tf_op jit(solution)/shard_map/ppermute | solution.py:98
  70.3 11.8 %collective-permute-start.11 = (f32[384,128]{1,0:T(8,128)S(1)}, f32[384,128]{1,0:T(8,128)S(1)}, u32[]{:S(2)}, u32[]{:S(2)}) collective-permute-start(f32[384,128]{1,0:T(8,128)S(1)} %get-tuple-element.78), channel_id=1, source_target_pairs={{160,164},{161,165},{168,172},{169,173}} | collective-permute-start | bytes 589832 | tf_op jit(solution)/shard_map/ppermute | solution.py:98
  75.1 9.3 %collective-permute-start.27 = (f32[2,384,128]{2,1,0:T(8,128)S(1)}, f32[2,384,128]{2,1,0:T(8,128)S(1)}, u32[]{:S(2)}, u32[]{:S(2)}) collective-permute-start(f32[2,384,128]{2,1,0:T(8,128)S(1)} %pad_maximum_fusion.3.refs_0_), channel_id=1, source_target_pairs={{8,0},{16,8},{24,16},{0,24},{40,32},{48,40},{56,48},{32,56},{72,64... | collective-permute-start | bytes 1179656 | tf_op jit(solution)/shard_map/ppermute | solution.py:98
  75.2 9.2 %collective-permute-start.25 = (f32[2,384,128]{2,1,0:T(8,128)S(1)}, f32[2,384,128]{2,1,0:T(8,128)S(1)}, u32[]{:S(2)}, u32[]{:S(2)}) collective-permute-start(f32[2,384,128]{2,1,0:T(8,128)S(1)} %pad_maximum_fusion.3.refs_0_), channel_id=1, source_target_pairs={{24,0},{0,8},{8,16},{16,24},{56,32},{32,40},{40,48},{48,56},{88,64... | collective-permute-start | bytes 1179656 | tf_op jit(solution)/shard_map/ppermute | solution.py:98
  78.4 9.6 %collective-permute-start.21 = (f32[2,384,128]{2,1,0:T(8,128)S(1)}, f32[2,384,128]{2,1,0:T(8,128)S(1)}, u32[]{:S(2)}, u32[]{:S(2)}) collective-permute-start(f32[2,384,128]{2,1,0:T(8,128)S(1)} %pad_maximum_fusion.3.refs_0_), channel_id=1, source_target_pairs={{224,0},{232,8},{240,16},{248,24},{0,32},{8,40},{16,48},{24,56},{3... | collective-permute-start | bytes 1179656 | tf_op jit(solution)/shard_map/ppermute | solution.py:98
  82.1 7.8 %collective-permute-start.19 = (f32[2,384,128]{2,1,0:T(8,128)S(1)}, f32[2,384,128]{2,1,0:T(8,128)S(1)}, u32[]{:S(2)}, u32[]{:S(2)}) collective-permute-start(f32[2,384,128]{2,1,0:T(8,128)S(1)} %pad_maximum_fusion.3.refs_0_), channel_id=1, source_target_pairs={{32,0},{40,8},{48,16},{56,24},{64,32},{72,40},{80,48},{88,56},{96,... | collective-permute-start | bytes 1179656 | tf_op jit(solution)/shard_map/ppermute | solution.py:98
  82.1 7.9 %collective-permute-start.12 = (f32[384,128]{1,0:T(8,128)S(1)}, f32[384,128]{1,0:T(8,128)S(1)}, u32[]{:S(2)}, u32[]{:S(2)}) collective-permute-start(f32[384,128]{1,0:T(8,128)S(1)} %add_add_fusion.2), channel_id=1, source_target_pairs={{160,184},{168,176},{161,185},{169,177},{162,186},{170,178},{163,1... | collective-permute-start | bytes 589832 | tf_op jit(solution)/shard_map/ppermute | solution.py:98
  90.0 25.4 %collective-permute-start.28 = (f32[2,960,128]{2,1,0:T(8,128)S(1)}, f32[2,960,128]{2,1,0:T(8,128)S(1)}, u32[]{:S(2)}, u32[]{:S(2)}) collective-permute-start(f32[2,960,128]{2,1,0:T(8,128)S(1)} %get-tuple-element.69), channel_id=1, source_target_pairs={{8,0},{16,8},{24,16},{0,24},{40,32},{48,40},{56,48},{32,56},{72,64... | collective-permute-start | bytes 2949128 | tf_op jit(solution)/shard_map/ppermute | solution.py:98
  90.1 5.3 %collective-permute-start.14 = (f32[384,128]{1,0:T(8,128)S(1)}, f32[384,128]{1,0:T(8,128)S(1)}, u32[]{:S(2)}, u32[]{:S(2)}) collective-permute-start(f32[384,128]{1,0:T(8,128)S(1)} %add.90), channel_id=1, source_target_pairs={{160,64},{168,72},{176,80},{184,88},{161,65},{169,73},{177,81},{18... | collective-permute-start | bytes 589832 | tf_op jit(solution)/shard_map/ppermute | solution.py:98
  90.8 13.4 %collective-permute-start.13 = (f32[384,128]{1,0:T(8,128)S(1)}, f32[384,128]{1,0:T(8,128)S(1)}, u32[]{:S(2)}, u32[]{:S(2)}) collective-permute-start(f32[384,128]{1,0:T(8,128)S(1)} %add.90), channel_id=1, source_target_pairs={{160,0},{168,8},{176,16},{184,24},{161,1},{169,9},{177,17},{185,25... | collective-permute-start | bytes 589832 | tf_op jit(solution)/shard_map/ppermute | solution.py:98
  92.1 12.2 %collective-permute-start.22 = (f32[2,384,128]{2,1,0:T(8,128)S(1)}, f32[2,384,128]{2,1,0:T(8,128)}, u32[]{:S(2)}, u32[]{:S(2)}) collective-permute-start(f32[2,384,128]{2,1,0:T(8,128)S(1)} %collective-permute-done.21.refs_2_), channel_id=1, source_target_pairs={{224,0},{232,8},{240,16},{248,24},{0,32},{8,40},{16,48},{24,56},{3... | collective-permute-start | bytes 1179656 | tf_op jit(solution)/shard_map/ppermute | solution.py:98
  92.2 12.1 %collective-permute-start.20 = (f32[2,384,128]{2,1,0:T(8,128)S(1)}, f32[2,384,128]{2,1,0:T(8,128)}, u32[]{:S(2)}, u32[]{:S(2)}) collective-permute-start(f32[2,384,128]{2,1,0:T(8,128)S(1)} %collective-permute-done.19.refs_1_), channel_id=1, source_target_pairs={{32,0},{40,8},{48,16},{56,24},{64,32},{72,40},{80,48},{88,56},{96,... | collective-permute-start | bytes 1179656 | tf_op jit(solution)/shard_map/ppermute | solution.py:98
  104.3 8.3 %collective-permute-start.24 = (f32[384,128]{1,0:T(8,128)S(1)}, f32[384,128]{1,0:T(8,128)S(1)}, u32[]{:S(2)}, u32[]{:S(2)}) collective-permute-start(f32[384,128]{1,0:T(8,128)S(1)} %add_add_fusion.1), channel_id=1, source_target_pairs={{160,128},{168,136},{176,144},{184,152},{0,224},{8,232},{16,240},{... | collective-permute-start | bytes 589832 | tf_op jit(solution)/shard_map/ppermute | solution.py:98
  107.5 7.2 %collective-permute-start.23 = (f32[384,128]{1,0:T(8,128)S(1)}, f32[384,128]{1,0:T(8,128)S(1)}, u32[]{:S(2)}, u32[]{:S(2)}) collective-permute-start(f32[384,128]{1,0:T(8,128)S(1)} %add_add_fusion.1), channel_id=1, source_target_pairs={{160,192},{168,200},{176,208},{184,216},{0,32},{8,40},{16,48},{24,... | collective-permute-start | bytes 589832 | tf_op jit(solution)/shard_map/ppermute | solution.py:98
  108.8 22.6 %collective-permute-start.26 = (f32[2,960,128]{2,1,0:T(8,128)S(1)}, f32[2,960,128]{2,1,0:T(8,128)}, u32[]{:S(2)}, u32[]{:S(2)}) collective-permute-start(f32[2,960,128]{2,1,0:T(8,128)S(1)} %get-tuple-element.70), channel_id=1, source_target_pairs={{24,0},{0,8},{8,16},{16,24},{56,32},{32,40},{40,48},{48,56},{88,64... | collective-permute-start | bytes 2949128 | tf_op jit(solution)/shard_map/ppermute | solution.py:98
  112.6 18.8 %collective-permute-start.29 = (f32[2,384,128]{2,1,0:T(8,128)}, f32[2,384,128]{2,1,0:T(8,128)}, u32[]{:S(2)}, u32[]{:S(2)}) collective-permute-start(f32[2,384,128]{2,1,0:T(8,128)} %collective-permute-done.20.refs_5_), channel_id=1, source_target_pairs={{32,0},{40,8},{48,16},{56,24},{64,32},{72,40},{80,48},{88,56},{96,... | collective-permute-start | bytes 1179656 | tf_op jit(solution)/shard_map/ppermute | solution.py:98
  112.6 18.8 %collective-permute-start.30 = (f32[2,384,128]{2,1,0:T(8,128)}, f32[2,384,128]{2,1,0:T(8,128)}, u32[]{:S(2)}, u32[]{:S(2)}) collective-permute-start(f32[2,384,128]{2,1,0:T(8,128)} %collective-permute-done.22.refs_6_), channel_id=1, source_target_pairs={{224,0},{232,8},{240,16},{248,24},{0,32},{8,40},{16,48},{24,56},{3... | collective-permute-start | bytes 1179656 | tf_op jit(solution)/shard_map/ppermute | solution.py:98
  116.5 14.9 %collective-permute-start.32 = (f32[2,384,128]{2,1,0:T(8,128)}, f32[2,384,128]{2,1,0:T(8,128)}, u32[]{:S(2)}, u32[]{:S(2)}) collective-permute-start(f32[2,384,128]{2,1,0:T(8,128)} %get-tuple-element.67), channel_id=1, source_target_pairs={{224,0},{232,8},{240,16},{248,24},{0,32},{8,40},{16,48},{24,56},{3... | collective-permute-start | bytes 1179656 | tf_op jit(solution)/shard_map/ppermute | solution.py:98
  117.0 14.4 %collective-permute-start.31 = (f32[2,384,128]{2,1,0:T(8,128)}, f32[2,384,128]{2,1,0:T(8,128)}, u32[]{:S(2)}, u32[]{:S(2)}) collective-permute-start(f32[2,384,128]{2,1,0:T(8,128)} %get-tuple-element.68), channel_id=1, source_target_pairs={{32,0},{40,8},{48,16},{56,24},{64,32},{72,40},{80,48},{88,56},{96,... | collective-permute-start | bytes 1179656 | tf_op jit(solution)/shard_map/ppermute | solution.py:98
  (11 other events, 206.6 us)
Sparse Core Ops, SparseCore 0:
  66.1 24.9 all-gather.2
